TPU v7x, 32 devices: a whole 2x2x4 slice. The times are simulated.
32 devices in a mesh: blk: 16 (over z, y, x), rep: 2 (over core).
Axes of the slice: x: 2, y: 2, z: 4, core: 2. Of those that a mesh axis runs over, the one named last changes fastest.
Arguments:
- patches: bfloat16 [2, 16384, 768], P('rep', 'blk'), may hold values from -6 to 6
- latents: bfloat16 [2, 512, 768], P('rep', 'blk'), may hold values from -6 to 6
- norm_gain: bfloat16 [5, 768], replicated, may hold values from 0.099609375 to 1.8984375
- norm_bias: bfloat16 [5, 768], replicated, may hold values from -1.75 to 1.75
- read_in: bfloat16 [3, 768, 768], replicated, may hold values from -0.21875 to 0.21875
- read_out: bfloat16 [768, 768], replicated, may hold values from -1.75 to 1.75
- self_in: bfloat16 [3, 768, 768], replicated, may hold values from -0.21875 to 0.21875
- self_out: bfloat16 [768, 768], replicated, may hold values from -2 to 2
- write_in: bfloat16 [3, 768, 768], replicated, may hold values from -0.21875 to 0.21875
- write_out: bfloat16 [768, 768], replicated, may hold values from -0.3125 to 0.3125
- feed_up: bfloat16 [768, 3072], replicated, may hold values from -0.21875 to 0.21875
- feed_down: bfloat16 [3072, 768], replicated, may hold values from -0.109375 to 0.109375
- group_image: int32 [2, 64], P('rep'), may hold values from 0 to 63, as said below
- cot_patches: bfloat16 [2, 16384, 768], P('rep', 'blk'), may hold values from -6 to 6
- cot_latents: bfloat16 [2, 512, 768], P('rep', 'blk'), may hold values from -6 to 6
Outputs:
- out_patches: bfloat16 [2, 16384, 768], P('rep', 'blk')
- out_latents: bfloat16 [2, 512, 768], P('rep', 'blk')
- gradient_patches: bfloat16 [2, 16384, 768], P('rep', 'blk')
- gradient_latents: bfloat16 [2, 512, 768], P('rep', 'blk')
- gradient_gain: float32 [5, 768], P(None, 'blk')
- gradient_bias: float32 [5, 768], P(None, 'blk')
- gradient_read_in: float32 [3, 768, 768], P(None, 'blk')
- gradient_read_out: float32 [768, 768], P('blk')
- gradient_self_in: float32 [3, 768, 768], P(None, 'blk')
- gradient_self_out: float32 [768, 768], P('blk')
- gradient_write_in: float32 [3, 768, 768], P(None, 'blk')
- gradient_write_out: float32 [768, 768], P('blk')
- gradient_up: float32 [768, 3072], P('blk')
- gradient_down: float32 [3072, 768], P('blk')
Inputs may be any that keep to these rules, and one draw needn't show every extreme that they name: `group_image`: along each row ids never fall and the groups of one image are contiguous; an image's id is the index of its last group. Group 0 is an image of its own, and one image runs from one of the first 4 groups to one of the last 4 groups of its row.
All inputs are finite; a program needn't handle non-finite values.
Results may differ from a plain program's by a relative error of at most 0.025.
Values may be sent and summed in bfloat16 or wider, within the bound.
No kernel may reach another device: no remote copies, remote signals or barrier semaphores. Data moves between devices by JAX's collectives and lax.ppermute only.
A program may use at most 192 MiB of HBM per device.

v0:
```python
import jax
import jax.numpy as jnp
from jax import lax
from jax.sharding import PartitionSpec as P

D = 768
HEADS = 12
HEAD = 64
LAT = 8


def narrow(tensor):
    return tensor.astype(jnp.bfloat16)


def multiply(left, right):
    return jnp.dot(left, right, preferred_element_type=jnp.float32)


def left_transposed(left, right):
    return lax.dot_general(
        left, right, (((0,), (0,)), ((), ())), preferred_element_type=jnp.float32
    )


def right_transposed(left, right):
    return lax.dot_general(
        left, right, (((1,), (1,)), ((), ())), preferred_element_type=jnp.float32
    )


def layer_norm(tensor, scale_row, shift_row):
    center = tensor - jnp.mean(tensor, axis=-1, keepdims=True)
    spread = jnp.mean(center * center, axis=-1, keepdims=True)
    return center * lax.rsqrt(spread + 1e-06) * scale_row + shift_row


def gelu_value(tensor):
    return 0.5 * tensor * (1.0 + lax.erf(tensor * 0.7071067811865476))


def norm_backward(tensor, scale_row, shift_row, upstream):
    _, pullback = jax.vjp(layer_norm, tensor, scale_row, shift_row)
    return pullback(upstream)


def to_heads(tensor, blocks):
    return tensor.reshape(blocks, -1, HEADS, HEAD)


def attend_forward(queries, key_rows, values, allowed):
    scores = jnp.einsum(
        "bqhe,bkhe->bhqk", queries, key_rows, preferred_element_type=jnp.float32
    ) * HEAD ** (-0.5)
    if allowed is not None:
        scores = jnp.where(allowed, scores, -1e30)
    highest = jnp.max(scores, axis=-1, keepdims=True)
    powers = jnp.exp(scores - highest)
    totals = jnp.sum(powers, axis=-1, keepdims=True)
    shares = powers / totals
    mixture = jnp.einsum(
        "bhqk,bkhe->bqhe", narrow(shares), values, preferred_element_type=jnp.float32
    )
    return (mixture, highest + jnp.log(totals), shares)


def attend_backward(queries, key_rows, values, allowed, log_total, upstream, inner):
    factor = HEAD ** (-0.5)
    scores = (
        jnp.einsum("bqhe,bkhe->bhqk", queries, key_rows, preferred_element_type=jnp.float32)
        * factor
    )
    if allowed is not None:
        scores = jnp.where(allowed, scores, -1e30)
    shares = jnp.exp(scores - log_total)
    value_grad = jnp.einsum(
        "bhqk,bqhe->bkhe", narrow(shares), upstream, preferred_element_type=jnp.float32
    )
    share_grad = jnp.einsum("bqhe,bkhe->bhqk", upstream, values, preferred_element_type=jnp.float32)
    if inner is None:
        inner = jnp.sum(shares * share_grad, axis=-1, keepdims=True)
    score_grad = narrow(shares * (share_grad - inner))
    query_grad = (
        jnp.einsum("bhqk,bkhe->bqhe", score_grad, key_rows, preferred_element_type=jnp.float32)
        * factor
    )
    key_grad = (
        jnp.einsum("bhqk,bqhe->bkhe", score_grad, queries, preferred_element_type=jnp.float32)
        * factor
    )
    return (query_grad, key_grad, value_grad)


def body(
    patches,
    latents,
    norm_gain,
    norm_bias,
    read_in,
    read_out,
    self_in,
    self_out,
    write_in,
    write_out,
    feed_up,
    feed_down,
    group_image,
    cot_patches,
    cot_latents,
):
    gain = norm_gain.astype(jnp.float32)
    shift = norm_bias.astype(jnp.float32)
    patch_in = patches[0].astype(jnp.float32)
    latent_in = latents[0].astype(jnp.float32)
    tok_count = patch_in.shape[0]
    lat_count = latent_in.shape[0]
    groups = lat_count // LAT
    read_query_src = narrow(layer_norm(latent_in, gain[0], shift[0]))
    read_patch_src = narrow(layer_norm(patch_in, gain[1], shift[1]))
    read_queries = narrow(multiply(read_query_src, read_in[0]))
    read_keys = narrow(multiply(read_patch_src, read_in[1]))
    read_values = narrow(multiply(read_patch_src, read_in[2]))
    read_mix, read_log, _ = attend_forward(
        to_heads(read_queries, groups),
        to_heads(read_keys, groups),
        to_heads(read_values, groups),
        None,
    )
    read_mix = narrow(read_mix.reshape(lat_count, D))
    after_read = latent_in + multiply(read_mix, read_out)
    self_src = narrow(layer_norm(after_read, gain[2], shift[2]))
    self_queries = narrow(multiply(self_src, self_in[0]))
    self_keys = narrow(multiply(self_src, self_in[1]))
    self_values = narrow(multiply(self_src, self_in[2]))
    owners = jnp.repeat(group_image[0], LAT)
    own_owner = lax.dynamic_slice_in_dim(owners, lax.axis_index("blk") * lat_count, lat_count, 0)
    keys_all, values_all = (
        lax.all_gather(self_keys, "blk", axis=0, tiled=True),
        lax.all_gather(self_values, "blk", axis=0, tiled=True),
    )
    allowed_all = (own_owner[:, None] == owners[None, :])[None, None]
    self_mix, self_log, self_shares = attend_forward(
        to_heads(self_queries, 1), to_heads(keys_all, 1), to_heads(values_all, 1), allowed_all
    )
    full_mix = jnp.einsum(
        "bhqk,bkhe->bqhe",
        self_shares,
        to_heads(values_all, 1).astype(jnp.float32),
        precision=lax.Precision.HIGHEST,
    )
    self_mix = narrow(self_mix.reshape(lat_count, D))
    after_self = after_read + multiply(self_mix, self_out)
    write_latent_src = narrow(layer_norm(after_self, gain[3], shift[3]))
    write_queries = narrow(multiply(read_patch_src, write_in[0]))
    write_keys = narrow(multiply(write_latent_src, write_in[1]))
    write_values = narrow(multiply(write_latent_src, write_in[2]))
    write_mix, write_log, _ = attend_forward(
        to_heads(write_queries, groups),
        to_heads(write_keys, groups),
        to_heads(write_values, groups),
        None,
    )
    write_mix = narrow(write_mix.reshape(tok_count, D))
    written = patch_in + multiply(write_mix, write_out)
    hidden_src = narrow(layer_norm(written, gain[4], shift[4]))
    hidden = multiply(hidden_src, feed_up)
    active = narrow(gelu_value(hidden))
    result = written + multiply(active, feed_down)
    upper_grad = cot_patches[0].astype(jnp.float32)
    feed_err = narrow(upper_grad)
    down_grad = left_transposed(active, feed_err)
    active_grad = right_transposed(feed_err, feed_down)
    _, gelu_pull = jax.vjp(gelu_value, hidden)
    hidden_grad = narrow(gelu_pull(active_grad)[0])
    up_grad = left_transposed(hidden_src, hidden_grad)
    norm_part, gain_four, shift_four = norm_backward(
        written, gain[4], shift[4], right_transposed(hidden_grad, feed_up)
    )
    written_grad = upper_grad + norm_part
    write_err = narrow(written_grad)
    write_out_grad = left_transposed(write_mix, write_err)
    write_up = narrow(right_transposed(write_err, write_out))
    query_part, key_part, value_part = attend_backward(
        to_heads(write_queries, groups),
        to_heads(write_keys, groups),
        to_heads(write_values, groups),
        None,
        write_log,
        to_heads(write_up, groups),
        None,
    )
    query_part = narrow(query_part.reshape(tok_count, D))
    key_part = narrow(key_part.reshape(lat_count, D))
    value_part = narrow(value_part.reshape(lat_count, D))
    write_in_grad = jnp.stack(
        [
            left_transposed(read_patch_src, query_part),
            left_transposed(write_latent_src, key_part),
            left_transposed(write_latent_src, value_part),
        ]
    )
    query_back = right_transposed(query_part, write_in[0])
    latent_write, gain_three, shift_three = norm_backward(
        after_self,
        gain[3],
        shift[3],
        right_transposed(key_part, write_in[1]) + right_transposed(value_part, write_in[2]),
    )
    self_grad = cot_latents[0].astype(jnp.float32) + latent_write
    self_err = narrow(self_grad)
    self_out_grad = left_transposed(self_mix, self_err)
    self_up_flat = narrow(right_transposed(self_err, self_out))
    self_up = to_heads(self_up_flat, 1)
    inner = jnp.einsum(
        "bqhe,bqhe->bhq", self_up.astype(jnp.float32), full_mix, precision=lax.Precision.HIGHEST
    )[..., None]
    key_piece = lax.all_gather(self_keys, "blk", axis=0, tiled=True)
    value_piece = lax.all_gather(self_values, "blk", axis=0, tiled=True)
    width = key_piece.shape[0]
    allowed = (own_owner[:, None] == owners[None, :])[None, None]
    query_step, key_step, value_step = attend_backward(
        to_heads(self_queries, 1),
        to_heads(key_piece, 1),
        to_heads(value_piece, 1),
        allowed,
        self_log,
        self_up,
        inner,
    )
    key_total = key_step.reshape(width, D)
    value_total = value_step.reshape(width, D)
    self_query_grad, key_total, value_total = (query_step, key_total, value_total)
    key_local, value_local = (
        lax.psum_scatter(
            key_total.astype(jnp.bfloat16), "blk", scatter_dimension=0, tiled=True
        ).astype(jnp.float32),
        lax.psum_scatter(
            value_total.astype(jnp.bfloat16), "blk", scatter_dimension=0, tiled=True
        ).astype(jnp.float32),
    )
    self_query_grad = narrow(self_query_grad.reshape(lat_count, D))
    key_local = narrow(key_local)
    value_local = narrow(value_local)
    self_in_grad = jnp.stack(
        [
            left_transposed(self_src, self_query_grad),
            left_transposed(self_src, key_local),
            left_transposed(self_src, value_local),
        ]
    )
    self_back = (
        right_transposed(self_query_grad, self_in[0])
        + right_transposed(key_local, self_in[1])
        + right_transposed(value_local, self_in[2])
    )
    latent_self, gain_two, shift_two = norm_backward(after_read, gain[2], shift[2], self_back)
    read_grad = self_grad + latent_self
    read_err = narrow(read_grad)
    read_out_grad = left_transposed(read_mix, read_err)
    read_up = narrow(right_transposed(read_err, read_out))
    query_part, key_part, value_part = attend_backward(
        to_heads(read_queries, groups),
        to_heads(read_keys, groups),
        to_heads(read_values, groups),
        None,
        read_log,
        to_heads(read_up, groups),
        None,
    )
    query_part = narrow(query_part.reshape(lat_count, D))
    key_part = narrow(key_part.reshape(tok_count, D))
    value_part = narrow(value_part.reshape(tok_count, D))
    read_in_grad = jnp.stack(
        [
            left_transposed(read_query_src, query_part),
            left_transposed(read_patch_src, key_part),
            left_transposed(read_patch_src, value_part),
        ]
    )
    latent_read, gain_zero, shift_zero = norm_backward(
        latent_in, gain[0], shift[0], right_transposed(query_part, read_in[0])
    )
    patch_read, gain_one, shift_one = norm_backward(
        patch_in,
        gain[1],
        shift[1],
        query_back
        + right_transposed(key_part, read_in[1])
        + right_transposed(value_part, read_in[2]),
    )
    latent_grad = read_grad + latent_read
    patch_grad = written_grad + patch_read
    gain_grad = jnp.stack([gain_zero, gain_one, gain_two, gain_three, gain_four])
    shift_grad = jnp.stack([shift_zero, shift_one, shift_two, shift_three, shift_four])
    (
        part_ri,
        part_ro,
        part_si,
        part_so,
        part_wi,
        part_wo,
        part_up,
        part_down,
        gain_part,
        shift_part,
    ) = (
        lax.psum_scatter(
            read_in_grad.astype(jnp.bfloat16), "blk", scatter_dimension=1, tiled=True
        ).astype(jnp.float32),
        lax.psum_scatter(
            read_out_grad.astype(jnp.bfloat16), "blk", scatter_dimension=0, tiled=True
        ).astype(jnp.float32),
        lax.psum_scatter(
            self_in_grad.astype(jnp.bfloat16), "blk", scatter_dimension=1, tiled=True
        ).astype(jnp.float32),
        lax.psum_scatter(
            self_out_grad.astype(jnp.bfloat16), "blk", scatter_dimension=0, tiled=True
        ).astype(jnp.float32),
        lax.psum_scatter(
            write_in_grad.astype(jnp.bfloat16), "blk", scatter_dimension=1, tiled=True
        ).astype(jnp.float32),
        lax.psum_scatter(
            write_out_grad.astype(jnp.bfloat16), "blk", scatter_dimension=0, tiled=True
        ).astype(jnp.float32),
        lax.psum_scatter(
            up_grad.astype(jnp.bfloat16), "blk", scatter_dimension=0, tiled=True
        ).astype(jnp.float32),
        lax.psum_scatter(
            down_grad.astype(jnp.bfloat16), "blk", scatter_dimension=0, tiled=True
        ).astype(jnp.float32),
        lax.psum_scatter(
            gain_grad.astype(jnp.bfloat16), "blk", scatter_dimension=1, tiled=True
        ).astype(jnp.float32),
        lax.psum_scatter(
            shift_grad.astype(jnp.bfloat16), "blk", scatter_dimension=1, tiled=True
        ).astype(jnp.float32),
    )
    sum_ri, sum_ro, sum_si, sum_so, sum_wi, sum_wo, sum_up, sum_down, gain_sum, shift_sum = (
        lax.psum(part_ri.astype(jnp.bfloat16), "rep").astype(jnp.float32),
        lax.psum(part_ro.astype(jnp.bfloat16), "rep").astype(jnp.float32),
        lax.psum(part_si.astype(jnp.bfloat16), "rep").astype(jnp.float32),
        lax.psum(part_so.astype(jnp.bfloat16), "rep").astype(jnp.float32),
        lax.psum(part_wi.astype(jnp.bfloat16), "rep").astype(jnp.float32),
        lax.psum(part_wo.astype(jnp.bfloat16), "rep").astype(jnp.float32),
        lax.psum(part_up.astype(jnp.bfloat16), "rep").astype(jnp.float32),
        lax.psum(part_down.astype(jnp.bfloat16), "rep").astype(jnp.float32),
        lax.psum(gain_part.astype(jnp.bfloat16), "rep").astype(jnp.float32),
        lax.psum(shift_part.astype(jnp.bfloat16), "rep").astype(jnp.float32),
    )
    return (
        narrow(result)[None],
        narrow(after_self)[None],
        narrow(patch_grad)[None],
        narrow(latent_grad)[None],
        gain_sum,
        shift_sum,
        sum_ri,
        sum_ro,
        sum_si,
        sum_so,
        sum_wi,
        sum_wo,
        sum_up,
        sum_down,
    )


def solution(mesh):
    return jax.shard_map(
        body,
        mesh=mesh,
        in_specs=(
            P("rep", "blk", None),
            P("rep", "blk", None),
            P(),
            P(),
            P(),
            P(),
            P(),
            P(),
            P(),
            P(),
            P(),
            P(),
            P("rep", None),
            P("rep", "blk", None),
            P("rep", "blk", None),
        ),
        out_specs=(
            P("rep", "blk", None),
            P("rep", "blk", None),
            P("rep", "blk", None),
            P("rep", "blk", None),
            P(None, "blk"),
            P(None, "blk"),
            P(None, "blk", None),
            P("blk", None),
            P(None, "blk", None),
            P("blk", None),
            P(None, "blk", None),
            P("blk", None),
            P("blk", None),
            P("blk", None),
        ),
        check_vma=False,
    )
```

profile of v0, /device:TPU:0, one launch (start us, length us, event | category | flops | bytes accessed | tf_op | source)
XLA Modules:
  0.0 1877.1 jit_solution(13775575857966226409)
XLA Ops:
  10.6 4.1 convolution_convert_fusion.6
  14.7 4.1 convolution_convert_fusion.7
  18.8 2.6 copy.112
  21.4 3.9 reshape.644
  27.5 2.6 copy.111
  30.1 3.9 reshape.642
  42.8 2.2 fusion.140
  45.1 2.2 fusion.137
  47.3 47.1 %all_gather.9 = bf16[512,768]{1,0:T(8,128)(2,1)S(1)} all-gather(bf16[32,768]{1,0:T(8,128)(2,1)S(1)} %fusion.143), channel_id=1, replica_groups=mesh['blk'=16,'rep'=2] {'blk'}, dimensions={0}, use_global_device_ids=true | all-gather | bytes 835584 | tf_op jit(solution)/shard_map/all_gather | solution.py:138
  98.1 40.5 %all_gather.8 = bf16[512,768]{1,0:T(8,128)(2,1)S(1)} all-gather(bf16[32,768]{1,0:T(8,128)(2,1)} %fusion.137), channel_id=1, replica_groups=mesh['blk'=16,'rep'=2] {'blk'}, dimensions={0}, use_global_device_ids=true | all-gather | bytes 835584 | tf_op jit(solution)/shard_map/all_gather | solution.py:139
  148.5 4.3 convolution_convert_fusion.5
  156.4 2.6 copy.121
  159.0 3.9 reshape.650
  174.3 2.6 copy.127
  176.9 11.4 multiply_convert_fusion
  188.3 11.5 add_convert_fusion
  199.8 9.3 fusion.247
  209.1 3.6 copy.128
  212.7 4.5 multiply_reduce_fusion
  221.0 2.6 convolution_convert_fusion.4
  223.6 2.7 copy.129
  226.3 3.9 reshape.652
  242.2 2.4 multiply_reduce_fusion.5
  250.5 2.1 fusion.110
  258.5 4.3 convolution_convert_fusion.8
  265.1 110.9 %reduce-scatter.37.cloned.1.call-done = bf16[32,768]{1,0:T(8,128)(2,1)} async-done(((bf16[512,768]{1,0:T(8,128)(2,1)}), bf16[32,768]{1,0:T(8,128)(2,1)}) %reduce-scatter.37.cloned.1.call-update) | async-done | bytes 49168
  379.6 122.6 %reduce-scatter.39.cloned.1.call-done = bf16[32,768]{1,0:T(8,128)(2,1)} async-done(((bf16[512,768]{1,0:T(8,128)(2,1)}), bf16[32,768]{1,0:T(8,128)(2,1)}) %reduce-scatter.39.cloned.1.call-update) | async-done | bytes 49168
  535.5 9.8 convolution_convert_fusion.1
  545.7 9.2 convolution_convert_fusion
  555.7 3.3 fusion.62
  560.5 3.4 fusion.236
  565.5 3.2 fusion.9
  570.1 60.2 %reduce-scatter.31.cloned.1.call-done = bf16[48,768]{1,0:T(8,128)(2,1)} async-done(((bf16[768,768]{1,0:T(8,128)(2,1)}), bf16[48,768]{1,0:T(8,128)(2,1)}) %reduce-scatter.31.cloned.1.call-update) | async-done | bytes 73744 | tf_op jit(solution)/shard_map/reduce_scatter | solution.py:322
  630.3 127.9 %reduce-scatter.27.cloned.1.call-done = bf16[48,768]{1,0:T(8,128)(2,1)} async-done(((bf16[768,768]{1,0:T(8,128)(2,1)}), bf16[48,768]{1,0:T(8,128)(2,1)}) %reduce-scatter.27.cloned.1.call-update) | async-done | bytes 73744 | tf_op jit(solution)/shard_map/reduce_scatter | solution.py:316
  758.2 127.9 %reduce-scatter.23.cloned.1.call-done = bf16[48,768]{1,0:T(8,128)(2,1)} async-done(((bf16[768,768]{1,0:T(8,128)(2,1)}), bf16[48,768]{1,0:T(8,128)(2,1)}) %reduce-scatter.23.cloned.1.call-update) | async-done | bytes 73744 | tf_op jit(solution)/shard_map/reduce_scatter | solution.py:310
  886.2 138.4 %reduce-scatter.29.cloned.1.call-done = bf16[3,48,768]{2,1,0:T(8,128)(2,1)} async-done(((bf16[3,768,768]{2,1,0:T(8,128)(2,1)}), bf16[3,48,768]{2,1,0:T(8,128)(2,1)}) %reduce-scatter.29.cloned.1.call-update) | async-done | bytes 221200 | tf_op jit(solution)/shard_map/reduce_scatter | solution.py:319
  1024.6 138.5 %reduce-scatter.25.cloned.1.call-done = bf16[3,48,768]{2,1,0:T(8,128)(2,1)} async-done(((bf16[3,768,768]{2,1,0:T(8,128)(2,1)}), bf16[3,48,768]{2,1,0:T(8,128)(2,1)}) %reduce-scatter.25.cloned.1.call-update) | async-done | bytes 221200 | tf_op jit(solution)/shard_map/reduce_scatter | solution.py:313
  1163.1 138.8 %reduce-scatter.21.cloned.1.call-done = bf16[3,48,768]{2,1,0:T(8,128)(2,1)} async-done(((bf16[3,768,768]{2,1,0:T(8,128)(2,1)}), bf16[3,48,768]{2,1,0:T(8,128)(2,1)}) %reduce-scatter.21.cloned.1.call-update) | async-done | bytes 221200 | tf_op jit(solution)/shard_map/reduce_scatter | solution.py:307
  1301.9 141.7 %reduce-scatter.33.cloned.1.call-done = bf16[48,3072]{1,0:T(8,128)(2,1)} async-done(((bf16[768,3072]{1,0:T(8,128)(2,1)}), bf16[48,3072]{1,0:T(8,128)(2,1)}) %reduce-scatter.33.cloned.1.call-update) | async-done | bytes 294928 | tf_op jit(solution)/shard_map/reduce_scatter | solution.py:325
  1443.6 142.3 %reduce-scatter.35.cloned.1.call-done = bf16[192,768]{1,0:T(8,128)(2,1)} async-done(((bf16[3072,768]{1,0:T(8,128)(2,1)}), bf16[192,768]{1,0:T(8,128)(2,1)}) %reduce-scatter.35.cloned.1.call-update) | async-done | bytes 294928 | tf_op jit(solution)/shard_map/reduce_scatter | solution.py:328
  1585.9 10.0 fusion.23
  1595.9 2.6 copy.154
  1598.5 5.9 fusion.15
  1604.4 2.7 copy.155
  1607.8 104.0 %reduce-scatter.43.cloned.1.call-done = bf16[48,5]{1,0:T(8,128)(2,1)} async-done(((bf16[768,5]{1,0:T(8,128)(2,1)}), bf16[48,5]{1,0:T(8,128)(2,1)}) %reduce-scatter.43.cloned.1.call-update) | async-done | bytes 496
  1712.6 124.9 %reduce-scatter.41.cloned.1.call-done = bf16[48,5]{1,0:T(8,128)(2,1)} async-done(((bf16[768,5]{1,0:T(8,128)(2,1)}), bf16[48,5]{1,0:T(8,128)(2,1)}) %reduce-scatter.41.cloned.1.call-update) | async-done | bytes 496
  1838.3 2.5 all-reduce
  1841.9 18.2 all-reduce.4.cloned.1.call-done
  (424 shorter events, 127.7 us)
Async XLA Ops:
  7.2 162.2 %copy-start = (bf16[768,768]{1,0:T(8,128)(2,1)S(1)}, bf16[768,768]{1,0:T(8,128)(2,1)}, u32[]{:S(2)}) copy-start(bf16[768,768]{1,0:T(8,128)(2,1)} %param.24) | copy-start | bytes 3538948
  7.2 368.8 %reduce-scatter.37.cloned.1.call-start = ((), (), s32[]{:S(2)}) async-start(), calls=%async_computation.20 | async-start | bytes 835584
  10.6 15.1 copy-start.66
  10.6 15.1 copy-start.88
  10.6 30.1 %copy-start.68 = (f32[768]{0:T(1024)}, f32[768]{0:T(1024)S(1)}, u32[]{:S(2)}) copy-start(f32[768]{0:T(1024)S(1)} %get-tuple-element.125) | copy-start | bytes 9220
  18.8 6.5 copy-start.20
  25.4 8.5 copy-start.96
  25.6 8.3 copy-start.113
  25.6 8.3 copy-start.104
  27.4 6.5 copy-start.32
  40.5 55.1 %copy-start.93 = (f32[32]{0:T(128)}, f32[32]{0:T(128)S(1)}, u32[]{:S(2)}) copy-start(f32[32]{0:T(128)S(1)} %broadcast_multiply_fusion.3) | copy-start | bytes 388
  41.2 56.0 %copy-start.112 = (s32[1,64]{1,0:T(1,128)S(1)}, s32[1,64]{1,0:T(1,128)}, u32[]{:S(2)}) copy-start(s32[1,64]{1,0:T(1,128)} %param.27) | copy-start | bytes 772
  176.9 11.4 copy-start.23
  176.9 23.0 %slice-start = ((s8[4718592]{0:T(1024)(128)(4,1)}), s8[4194304]{0:T(1024)(128)(4,1)S(1)}, s32[]{:S(2)}) async-start(s8[4718592]{0:T(1024)(128)(4,1)} %bitcast.350), calls=%async_computation.25 | async-start | bytes 8388608
  188.3 11.5 slice-start.1
  223.6 6.5 copy-start.14
  223.6 6.5 copy-start.50
  223.6 6.5 copy-start.54
  236.1 12.3 copy-start.12
  240.5 7.2 copy-start.58
  255.7 246.5 %reduce-scatter.39.cloned.1.call-start = ((), (), s32[]{:S(2)}) async-start(), calls=%async_computation.21 | async-start | bytes 835584
  258.5 371.8 %reduce-scatter.31.cloned.1.call-start = ((), (), s32[]{:S(2)}) async-start(), calls=%async_computation.17 | async-start | bytes 1253376 | tf_op jit(solution)/shard_map/reduce_scatter | solution.py:322
  262.8 239.3 %copy-start.16 = (f32[32,768]{1,0:T(8,128)S(1)}, f32[32,768]{1,0:T(8,128)}, u32[]{:S(2)}) copy-start(f32[32,768]{1,0:T(8,128)} %copy-done.15) | copy-start | bytes 294916
  262.8 239.3 %copy-start.69 = (f32[768]{0:T(1024)S(1)}, f32[768]{0:T(1024)}, u32[]{:S(2)}) copy-start(f32[768]{0:T(1024)} %copy-done.68) | copy-start | bytes 9220
  262.9 239.3 %copy-start.94 = (f32[32]{0:T(128)S(1)}, f32[32]{0:T(128)}, u32[]{:S(2)}) copy-start(f32[32]{0:T(128)} %copy-done.93) | copy-start | bytes 388
  262.9 239.3 %copy-start.102 = (f32[32]{0:T(128)S(1)}, f32[32]{0:T(128)}, u32[]{:S(2)}) copy-start(f32[32]{0:T(128)} %copy-done.101) | copy-start | bytes 388
  262.9 495.4 %reduce-scatter.27.cloned.1.call-start = ((), (), s32[]{:S(2)}) async-start(), calls=%async_computation.15 | async-start | bytes 1253376 | tf_op jit(solution)/shard_map/reduce_scatter | solution.py:316
  264.5 239.6 %copy-start.116 = (f32[32]{0:T(128)S(1)}, f32[32]{0:T(128)}, u32[]{:S(2)}) copy-start(f32[32]{0:T(128)} %copy-done.115) | copy-start | bytes 388
  264.5 239.8 %copy-start.31 = (f32[32,768]{1,0:T(8,128)S(1)}, f32[32,768]{1,0:T(8,128)}, u32[]{:S(2)}) copy-start(f32[32,768]{1,0:T(8,128)} %copy-done.30) | copy-start | bytes 294916
  264.5 239.8 %copy-start.59 = (bf16[1,32,768]{2,1,0:T(8,128)(2,1)S(1)}, bf16[1,32,768]{2,1,0:T(8,128)(2,1)}, u32[]{:S(2)}) copy-start(bf16[1,32,768]{2,1,0:T(8,128)(2,1)} %param.29) | copy-start | bytes 147460
  264.5 239.8 %copy-start.110 = (f32[32]{0:T(128)S(1)}, f32[32]{0:T(128)}, u32[]{:S(2)}) copy-start(f32[32]{0:T(128)} %copy-done.109) | copy-start | bytes 388
  264.5 239.9 %copy-start.45 = (bf16[32,768]{1,0:T(8,128)(2,1)S(1)}, bf16[32,768]{1,0:T(8,128)(2,1)}, u32[]{:S(2)}) copy-start(bf16[32,768]{1,0:T(8,128)(2,1)} %copy-done.44) | copy-start | bytes 147460
  264.5 621.6 %reduce-scatter.23.cloned.1.call-start = ((), (), s32[]{:S(2)}) async-start(), calls=%async_computation.13 | async-start | bytes 1253376 | tf_op jit(solution)/shard_map/reduce_scatter | solution.py:310
  377.8 128.4 %copy-start.38 = (bf16[4,12,256,8]{2,3,1,0:T(8,128)(2,1)S(1)}, bf16[4,12,256,8]{2,3,1,0:T(8,128)(2,1)}, u32[]{:S(2)}) copy-start(bf16[4,12,256,8]{2,3,1,0:T(8,128)(2,1)} %copy-done.37) | copy-start | bytes 589828
  377.8 128.4 %copy-start.48 = (bf16[4,8,12,64]{3,2,1,0:T(8,128)(2,1)S(1)}, bf16[4,8,12,64]{3,2,1,0:T(8,128)(2,1)}, u32[]{:S(2)}) copy-start(bf16[4,8,12,64]{3,2,1,0:T(8,128)(2,1)} %reshape.651) | copy-start | bytes 147460
  506.1 518.6 %reduce-scatter.29.cloned.1.call-start = ((), (), s32[]{:S(2)}) async-start(), calls=%async_computation.16 | async-start | bytes 3760128 | tf_op jit(solution)/shard_map/reduce_scatter | solution.py:319
  513.1 650.0 %reduce-scatter.25.cloned.1.call-start = ((), (), s32[]{:S(2)}) async-start(), calls=%async_computation.14 | async-start | bytes 3760128 | tf_op jit(solution)/shard_map/reduce_scatter | solution.py:313
  517.4 784.5 %reduce-scatter.21.cloned.1.call-start = ((), (), s32[]{:S(2)}) async-start(), calls=%async_computation.12 | async-start | bytes 3760128 | tf_op jit(solution)/shard_map/reduce_scatter | solution.py:307
  534.9 908.7 %reduce-scatter.33.cloned.1.call-start = ((), (), s32[]{:S(2)}) async-start(), calls=%async_computation.18 | async-start | bytes 5013504 | tf_op jit(solution)/shard_map/reduce_scatter | solution.py:325
  545.4 1040.5 %reduce-scatter.35.cloned.1.call-start = ((), (), s32[]{:S(2)}) async-start(), calls=%async_computation.19 | async-start | bytes 5013504 | tf_op jit(solution)/shard_map/reduce_scatter | solution.py:328
  555.0 1156.8 %reduce-scatter.43.cloned.1.call-start = ((), (), s32[]{:S(2)}) async-start(), calls=%async_computation.23 | async-start | bytes 208896
  565.4 1272.1 %reduce-scatter.41.cloned.1.call-start = ((), (), s32[]{:S(2)}) async-start(), calls=%async_computation.22 | async-start | bytes 208896
  569.8 1290.3 %all-reduce.4.cloned.1.call-start = ((), (), s32[]{:S(2)}) async-start(), calls=%async_computation.24 | async-start | bytes 2949120 | tf_op jit(solution)/shard_map/psum | solution.py:339
  1604.4 265.7 %copy-start.1 = (bf16[768,768]{1,0:T(8,128)(2,1)S(1)}, bf16[768,768]{1,0:T(8,128)(2,1)}, u32[]{:S(2)}) copy-start(bf16[768,768]{1,0:T(8,128)(2,1)} %param.24) | copy-start | bytes 3538948
  1860.1 7.2 copy-start.55
  1860.1 7.9 copy-start.65
  1860.1 8.6 copy-start.64
  1860.1 9.3 copy-start.63
  (85 other events, 208.1 us)
Sparse Core Ops, SparseCore 0:
  255.8 120.1 reduce-scatter.36
  380.7 121.4 reduce-scatter.38
  506.9 123.3 reduce-scatter.30
  634.9 123.2 reduce-scatter.26
  762.9 123.2 reduce-scatter.22
  891.1 133.4 reduce-scatter.28
  1029.7 133.3 reduce-scatter.24
  1168.2 133.6 reduce-scatter.20
  1307.1 136.4 reduce-scatter.32
  1449.4 136.4 reduce-scatter.34
  1591.1 120.5 reduce-scatter.42
  1716.9 120.5 reduce-scatter.40
  1840.3 19.7 all-reduce.3
where the time goes:
time: 1890 us; the launch traced here: 1880 us
  waiting for transfers between devices  1500 us (79%)
  matrix products  154 us (8%)
  blocking collectives  90 us (5%)
  local copies, waits for them, and re-layouts  77.8 us (4%)
  other arithmetic  41.5 us (2%)
    unnamed x17, waiting for transfers between devices  463 us
    reduce_scatter x1, waiting for transfers between devices, body(): lax.psum_scatter(down_grad.astype(jnp.bfloat16), 'blk', scatter_dimension...  142 us
    reduce_scatter x1, waiting for transfers between devices, body(): lax.psum_scatter(up_grad.astype(jnp.bfloat16), 'blk', scatter_dimension=0...  142 us
    reduce_scatter x1, waiting for transfers between devices, body(): lax.psum_scatter(read_in_grad.astype(jnp.bfloat16), 'blk', scatter_dimens...  139 us
    reduce_scatter x1, waiting for transfers between devices, body(): lax.psum_scatter(self_in_grad.astype(jnp.bfloat16), 'blk', scatter_dimens...  138 us
    reduce_scatter x1, waiting for transfers between devices, body(): lax.psum_scatter(write_in_grad.astype(jnp.bfloat16), 'blk', scatter_dimen...  138 us
    reduce_scatter x1, waiting for transfers between devices, body(): lax.psum_scatter(self_out_grad.astype(jnp.bfloat16), 'blk', scatter_dimen...  128 us
    reduce_scatter x1, waiting for transfers between devices, body(): lax.psum_scatter(read_out_grad.astype(jnp.bfloat16), 'blk', scatter_dimen...  128 us
  transfers between devices with their start and end apart: 13, of which 13 were waited for; matrix products, arithmetic and copies ran while one was open for 5% of the time, Pallas kernels for 0%

commit v1 on v0

v1 whole, which is shorter than its diff:
```python
import functools

import jax
import jax.numpy as jnp
from jax import lax
from jax.experimental import pallas as pl
from jax.experimental.pallas import tpu as pltpu
from jax.sharding import PartitionSpec as P

D = 768
HEADS = 12
HEAD = 64
LAT = 8
FACTOR = HEAD ** (-0.5)
HL = HEADS * LAT
BF = jnp.bfloat16
F32 = jnp.float32
VMEM_LIMIT = 60 * 1024 * 1024


def narrow(tensor):
    return tensor.astype(BF)


def mm(left, right):
    return lax.dot_general(left, right, (((1,), (0,)), ((), ())), preferred_element_type=F32)


def mm_tn(left, right):
    return lax.dot_general(left, right, (((0,), (0,)), ((), ())), preferred_element_type=F32)


def mm_nt(left, right):
    return lax.dot_general(left, right, (((1,), (1,)), ((), ())), preferred_element_type=F32)


def norm_parts(tensor):
    center = tensor - jnp.mean(tensor, axis=-1, keepdims=True)
    spread = jnp.mean(center * center, axis=-1, keepdims=True)
    inverse = lax.rsqrt(spread + 1e-06)
    return center * inverse, inverse


def norm_forward(tensor, gain, shift):
    unit, _ = norm_parts(tensor)
    return unit * gain + shift


def norm_back(unit, inverse, gain, upstream):
    scaled = upstream * gain
    return inverse * (
        scaled
        - jnp.mean(scaled, axis=-1, keepdims=True)
        - unit * jnp.mean(scaled * unit, axis=-1, keepdims=True)
    )


def fold_rows(tensor):
    rows, cols = tensor.shape
    return jnp.sum(tensor.reshape(rows // 8, 8, cols), axis=0)


def head_mask():
    head = lax.broadcasted_iota(jnp.int32, (HEADS, 1, D), 0)
    feature = lax.broadcasted_iota(jnp.int32, (HEADS, 1, D), 2)
    return (feature >= head * HEAD) & (feature < head * HEAD + HEAD)


def expand(rows):
    count = rows.shape[0]
    return narrow(jnp.where(head_mask(), rows[None], 0.0).reshape(HEADS * count, D))


def collapse(rows):
    count = rows.shape[0] // HEADS
    return jnp.sum(jnp.where(head_mask(), rows.reshape(HEADS, count, D), 0.0), axis=0)


def whole(shape):
    return pl.BlockSpec(shape, lambda *_: (0,) * len(shape), pipeline_mode=pl.Buffered(1))


def rows_of(shape):
    return pl.BlockSpec(shape, lambda g: (g,) + (0,) * (len(shape) - 1))


def one_of(index):
    return pl.BlockSpec(
        (None, D, D), lambda *_: (index, 0, 0), pipeline_mode=pl.Buffered(1)
    )


def shaped(shape, dtype):
    return jax.ShapeDtypeStruct(shape, dtype)


def call(body, grid, in_specs, out_specs, out_shape, flops, moved, scratch=()):
    return pl.pallas_call(
        body,
        grid=grid,
        in_specs=in_specs,
        out_specs=out_specs,
        out_shape=out_shape,
        scratch_shapes=scratch,
        compiler_params=pltpu.CompilerParams(
            vmem_limit_bytes=VMEM_LIMIT, dimension_semantics=("arbitrary",) * len(grid)
        ),
        cost_estimate=pl.CostEstimate(
            flops=int(flops), bytes_accessed=int(moved), transcendentals=0
        ),
    )


def read_forward_kernel(
    x_ref, z_ref, norm_ref, in_ref, out_w_ref,
    a1_ref, q1_ref, b1_ref, k1_ref, v1_ref, p1_ref, o1_ref, z1_ref, a2_ref,
    mix_ref,
):
    step = pl.program_id(0)
    last = pl.num_programs(0) - 1

    @pl.when(step == 0)
    def _():
        a1 = narrow(norm_forward(z_ref[...].astype(F32), norm_ref[0:1], norm_ref[5:6]))
        a1_ref[...] = a1
        q1_ref[...] = narrow(mm(a1, in_ref[0])).astype(F32)

    b1 = narrow(norm_forward(x_ref[...].astype(F32), norm_ref[1:2], norm_ref[6:7]))
    b1_ref[...] = b1
    k1 = narrow(mm(b1, in_ref[1]))
    v1 = narrow(mm(b1, in_ref[2]))
    k1_ref[...] = k1
    v1_ref[...] = v1
    own = pl.ds(pl.multiple_of(step * LAT, LAT), LAT)
    scores = mm_nt(expand(q1_ref[own, :]), k1) * FACTOR
    powers = jnp.exp(scores - jnp.max(scores, axis=-1, keepdims=True))
    shares = powers / jnp.sum(powers, axis=-1, keepdims=True)
    p1_ref[...] = shares
    mix_ref[own, :] = collapse(mm(narrow(shares), v1))

    @pl.when(step == last)
    def _():
        o1 = narrow(mix_ref[...])
        o1_ref[...] = o1
        z1 = z_ref[...].astype(F32) + mm(o1, out_w_ref[...])
        z1_ref[...] = z1
        a2_ref[...] = narrow(norm_forward(z1, norm_ref[2:3], norm_ref[7:8]))


def self_forward_kernel(
    all_ref, a2_ref, z1_ref, key_own_ref, query_own_ref, norm_ref, in_ref, out_w_ref, wk_ref, wv_ref,
    k2_ref, v2_ref, p2_ref, l2_ref, o2_ref, z2_ref, out_ref, b3_ref, k3_ref, v3_ref,
):
    k2 = narrow(mm(all_ref[...], in_ref[1]))
    v2 = narrow(mm(all_ref[...], in_ref[2]))
    k2_ref[...] = k2
    v2_ref[...] = v2
    q2 = narrow(mm(a2_ref[...], in_ref[0])).astype(F32)
    scores = mm_nt(k2, expand(q2)) * FACTOR
    allowed = key_own_ref[...] == query_own_ref[...]
    scores = jnp.where(allowed, scores, -1e30)
    highest = jnp.max(scores, axis=0, keepdims=True)
    powers = jnp.exp(scores - highest)
    totals = jnp.sum(powers, axis=0, keepdims=True)
    shares = powers / totals
    p2_ref[...] = shares
    l2_ref[...] = highest + jnp.log(totals)
    o2 = narrow(collapse(mm_tn(narrow(shares), v2)))
    o2_ref[...] = o2
    z2 = z1_ref[...] + mm(o2, out_w_ref[...])
    z2_ref[...] = z2
    out_ref[...] = narrow(z2)
    b3 = narrow(norm_forward(z2, norm_ref[3:4], norm_ref[8:9]))
    b3_ref[...] = b3
    k3_ref[...] = narrow(mm(b3, wk_ref[...])).astype(F32)
    v3_ref[...] = narrow(mm(b3, wv_ref[...])).astype(F32)


ROOT_HALF = 0.7071067811865476
DENSITY = 0.3989422804014327


def patch_kernel(
    chunk, x_ref, q3_ref, cot_ref, k3_ref, v3_ref, norm_ref, wo_ref, up_ref, down_ref,
    out_ref, h_ref, g_ref, du_ref, o3_ref, e3_ref, dq3_ref, dx1_ref, dk3_ref, dv3_ref,
    gain_ref, shift_ref,
):
    step = pl.program_id(0)
    own = pl.ds(pl.multiple_of(step * LAT, LAT), LAT)
    kx = expand(k3_ref[own, :])
    vx = expand(v3_ref[own, :])
    q3 = q3_ref[...]
    tokens = q3.shape[0]
    scores = (mm_nt(kx, q3) * FACTOR).reshape(HEADS, LAT, tokens)
    powers = jnp.exp(scores - jnp.max(scores, axis=1, keepdims=True))
    shares = powers / jnp.sum(powers, axis=1, keepdims=True)
    shares_low = narrow(shares.reshape(HL, tokens))
    o3 = narrow(mm_tn(shares_low, vx))
    o3_ref[...] = o3
    x1 = x_ref[...].astype(F32) + mm(o3, wo_ref[...])
    unit, inverse = norm_parts(x1)
    gain = norm_ref[4:5]
    h = narrow(unit * gain + norm_ref[9:10])
    h_ref[...] = h
    e4 = cot_ref[...]
    x2 = x1
    dh = jnp.zeros((tokens, D), F32)
    hidden = up_ref.shape[1]
    for start in range(0, hidden, chunk):
        part = slice(start, start + chunk)
        u = mm(h, up_ref[:, part])
        cdf = 0.5 + 0.5 * lax.erf(u * ROOT_HALF)
        g = narrow(u * cdf)
        g_ref[:, part] = g
        x2 = x2 + mm(g, down_ref[part, :])
        slope = cdf + u * (jnp.exp(-0.5 * u * u) * DENSITY)
        du = narrow(mm_nt(e4, down_ref[part, :]) * slope)
        du_ref[:, part] = du
        dh = dh + mm_nt(du, up_ref[:, part])
    out_ref[...] = narrow(x2)

    @pl.when(step == 0)
    def _():
        gain_ref[...] = jnp.zeros_like(gain_ref)
        shift_ref[...] = jnp.zeros_like(shift_ref)

    gain_ref[...] += fold_rows(dh * unit)
    shift_ref[...] += fold_rows(dh)
    dx1 = e4.astype(F32) + norm_back(unit, inverse, gain, dh)
    dx1_ref[...] = dx1
    e3 = narrow(dx1)
    e3_ref[...] = e3
    do3 = narrow(mm_nt(e3, wo_ref[...]))
    dshares = mm_nt(vx, do3).reshape(HEADS, LAT, tokens)
    inner = jnp.sum(shares * dshares, axis=1, keepdims=True)
    dscores = narrow((shares * (dshares - inner)).reshape(HL, tokens))
    dq3_ref[...] = narrow(mm_tn(dscores, kx) * FACTOR)
    dv3_ref[...] = collapse(mm(shares_low, do3))
    dk3_ref[...] = collapse(mm(dscores, q3)) * FACTOR


def latent_back_kernel(
    dk3_ref, dv3_ref, z2_ref, cot_ref, k2_ref, v2_ref, p2_ref, norm_ref, wk_ref, wv_ref, out_w_ref,
    dk3_low_ref, dv3_low_ref, dz2_ref, e2_ref, do2_ref, inner_ref, dq2_ref, gain_ref, shift_ref,
):
    dk3 = narrow(dk3_ref[...])
    dv3 = narrow(dv3_ref[...])
    dk3_low_ref[...] = dk3
    dv3_low_ref[...] = dv3
    upstream = mm_nt(dk3, wk_ref[...]) + mm_nt(dv3, wv_ref[...])
    unit, inverse = norm_parts(z2_ref[...])
    gain_ref[...] = fold_rows(upstream * unit)
    shift_ref[...] = fold_rows(upstream)
    dz2 = cot_ref[...].astype(F32) + norm_back(unit, inverse, norm_ref[3:4], upstream)
    dz2_ref[...] = dz2
    e2 = narrow(dz2)
    e2_ref[...] = e2
    do2 = narrow(mm_nt(e2, out_w_ref[...]))
    do2_ref[...] = do2
    shares = p2_ref[...]
    dshares = mm_nt(v2_ref[...], expand(do2.astype(F32)))
    inner = jnp.sum(shares * dshares, axis=0, keepdims=True)
    inner_ref[...] = inner
    dscores = narrow(shares * (dshares - inner))
    dq2_ref[...] = narrow(collapse(mm_tn(dscores, k2_ref[...])) * FACTOR)


def self_back_kernel(
    q_all_ref, do_all_ref, l_ref, inner_ref, key_own_ref, query_own_ref, k2_ref, v2_ref,
    dq2_ref, z1_ref, dz2_ref, norm_ref, in_ref, out_w_ref,
    dk2_ref, dv2_ref, dz1_ref, e1_ref, do1_ref, gain_ref, shift_ref,
):
    count = k2_ref.shape[0]
    total = q_all_ref.shape[0]
    q_all = q_all_ref[...]
    do_all = do_all_ref[...]
    scores = mm_nt(expand(k2_ref[...].astype(F32)), q_all) * FACTOR
    allowed = key_own_ref[...] == query_own_ref[...]
    log_total = jnp.broadcast_to(l_ref[...], (HEADS, count, total)).reshape(HEADS * count, total)
    shares = jnp.where(allowed, jnp.exp(jnp.where(allowed, scores - log_total, 0.0)), 0.0)
    dv2 = narrow(collapse(mm(narrow(shares), do_all)))
    dshares = mm_nt(expand(v2_ref[...].astype(F32)), do_all)
    inner = jnp.broadcast_to(inner_ref[...], (HEADS, count, total)).reshape(HEADS * count, total)
    dscores = narrow(shares * (dshares - inner))
    dk2 = narrow(collapse(mm(dscores, q_all)) * FACTOR)
    dk2_ref[...] = dk2
    dv2_ref[...] = dv2
    upstream = mm_nt(dq2_ref[...], in_ref[0]) + mm_nt(dk2, in_ref[1]) + mm_nt(dv2, in_ref[2])
    unit, inverse = norm_parts(z1_ref[...])
    gain_ref[...] = fold_rows(upstream * unit)
    shift_ref[...] = fold_rows(upstream)
    dz1 = dz2_ref[...] + norm_back(unit, inverse, norm_ref[2:3], upstream)
    dz1_ref[...] = dz1
    e1 = narrow(dz1)
    e1_ref[...] = e1
    do1_ref[...] = narrow(mm_nt(e1, out_w_ref[...])).astype(F32)


def read_back_kernel(
    do1_ref, q1_ref, p1_ref, k1_ref, v1_ref,
    dq1_ref, dk1_ref, dv1_ref,
):
    step = pl.program_id(0)
    own = pl.ds(pl.multiple_of(step * LAT, LAT), LAT)
    qx = expand(q1_ref[own, :])
    dox = expand(do1_ref[own, :])
    shares = p1_ref[...]
    dshares = mm_nt(dox, v1_ref[...])
    inner = jnp.sum(shares * dshares, axis=-1, keepdims=True)
    dscores = narrow(shares * (dshares - inner))
    dv1_ref[...] = narrow(mm_tn(narrow(shares), dox))
    dk1_ref[...] = narrow(mm_tn(dscores, qx) * FACTOR)
    dq1_ref[...] = collapse(mm(dscores, k1_ref[...])) * FACTOR


def input_back_kernel(
    x_ref, dx1_ref, dq3_ref, dk1_ref, dv1_ref, z_ref, dz1_ref, dq1_ref, norm_ref, in_ref, wq_ref,
    dx_ref, dz_ref, gain_ref, shift_ref, gain_zero_ref, shift_zero_ref,
):
    step = pl.program_id(0)

    @pl.when(step == 0)
    def _():
        gain_ref[...] = jnp.zeros_like(gain_ref)
        shift_ref[...] = jnp.zeros_like(shift_ref)
        upstream = mm_nt(dq1_ref[...], in_ref[0])
        unit, inverse = norm_parts(z_ref[...].astype(F32))
        gain_zero_ref[...] = fold_rows(upstream * unit)
        shift_zero_ref[...] = fold_rows(upstream)
        dz_ref[...] = narrow(dz1_ref[...] + norm_back(unit, inverse, norm_ref[0:1], upstream))

    upstream = (
        mm_nt(dq3_ref[...], wq_ref[...])
        + mm_nt(dk1_ref[...], in_ref[1])
        + mm_nt(dv1_ref[...], in_ref[2])
    )
    unit, inverse = norm_parts(x_ref[...].astype(F32))
    gain_ref[...] += fold_rows(upstream * unit)
    shift_ref[...] += fold_rows(upstream)
    dx_ref[...] = narrow(dx1_ref[...] + norm_back(unit, inverse, norm_ref[1:2], upstream))


def bits_of(count):
    bits = count.bit_length() - 1
    if 1 << bits != count:
        raise ValueError("axis size")
    return bits


def swap(tensor, axis, bit, count):
    return lax.ppermute(tensor, axis, [(i, i ^ (1 << bit)) for i in range(count)])


def own_bit(bit, axis="blk"):
    return (lax.axis_index(axis) >> bit) & 1


def doubled(tensor, bit, place, count):
    other = swap(tensor, "blk", bit, count)
    mine_first = own_bit(bit) == 0
    return jnp.stack(
        [jnp.where(mine_first, tensor, other), jnp.where(mine_first, other, tensor)], place
    )


def gather_rows(tensor, count):
    bits = bits_of(count)
    rows, cols = tensor.shape
    for place, bit in enumerate(range(bits - 1, 1, -1)):
        tensor = doubled(tensor, bit, place, count)
    lead = max(bits - 2, 0)
    if bits < 2:
        for bit in range(bits - 1, -1, -1):
            tensor = doubled(tensor, bit, 0, count)
        return tensor.reshape(count, rows, cols)
    left, right = tensor[..., : cols // 2], tensor[..., cols // 2 :]
    left = doubled(left, 1, lead, count)
    right = doubled(right, 0, lead, count)
    left = doubled(left, 0, lead + 1, count)
    right = doubled(right, 1, lead, count)
    return jnp.concatenate([left, right], -1).reshape(count, rows, cols)


def scatter_orders(bits):
    high = list(range(2, bits))
    if bits < 3:
        base = list(range(bits))
        return [base, base[::-1], base]
    return [[0, 1] + high, [1] + high[:1] + [0] + high[1:], high[:1] + [0, 1] + high[1:]]


def scatter_sum(tensor, order, count):
    bits = bits_of(count)
    rows, cols = tensor.shape[1:]
    tensor = tensor.reshape((2,) * bits + (rows, cols))
    left = list(range(bits - 1, -1, -1))
    for bit in order:
        place = left.index(bit)
        left.pop(place)
        mine = own_bit(bit)
        send = lax.dynamic_index_in_dim(tensor, 1 - mine, place, keepdims=False)
        keep = lax.dynamic_index_in_dim(tensor, mine, place, keepdims=False)
        got = swap(send, "blk", bit, count)
        tensor = narrow(keep.astype(F32) + got.astype(F32))
    return tensor


def half_columns(tensor, which):
    width = tensor.shape[1] // 2
    return lax.dynamic_slice_in_dim(tensor, which * width, width, 1)


def weight_halves(left, right, core, count):
    def half(which):
        grad = narrow(mm_tn(left, half_columns(right, which)))
        return grad.reshape(count, -1, grad.shape[1])

    return half(1 - core), half(core)


def make_body(n_blk, n_rep):
    rep_bits = bits_of(n_rep)
    orders = scatter_orders(bits_of(n_blk))

    def merge_core(pairs):
        other = jnp.concatenate([pair[0] for pair in pairs], 1) if len(pairs) > 1 else pairs[0][0]
        mine = jnp.concatenate([pair[1] for pair in pairs], 1) if len(pairs) > 1 else pairs[0][1]
        got = swap(other, "rep", 0, n_rep)
        return narrow(mine.astype(F32) + got.astype(F32))

    def finish(tensor, core):
        for bit in range(1, rep_bits):
            tensor = narrow(tensor.astype(F32) + swap(tensor, "rep", bit, n_rep).astype(F32))
        return tensor

    def body(
        patches, latents, norm_gain, norm_bias, read_in, read_out, self_in, self_out,
        write_in, write_out, feed_up, feed_down, group_image, cot_patches, cot_latents,
    ):
        x, z, cot, cot_z = patches[0], latents[0], cot_patches[0], cot_latents[0]
        tokens, lat = x.shape[0], z.shape[0]
        groups = lat // LAT
        size = tokens // groups
        total = lat * n_blk
        hidden = feed_up.shape[1]
        core = lax.axis_index("rep") & 1
        norms = jnp.concatenate(
            [norm_gain, norm_bias, jnp.zeros((6, D), BF)], 0
        ).astype(F32)
        norm_spec = whole((16, D))
        square = whole((D, D))
        three = whole((3, D, D))
        lat_spec = whole((lat, D))
        patch_spec = rows_of((size, D))
        grid = (groups,)
        unit_flops = 2 * tokens * D * D

        a1, q1, b1, k1, v1, p1, o1, z1, a2 = call(
            read_forward_kernel, grid,
            [patch_spec, lat_spec, norm_spec, three, square],
            [lat_spec, lat_spec, patch_spec, patch_spec, patch_spec,
             pl.BlockSpec((None, HL, size), lambda g: (g, 0, 0)), lat_spec, lat_spec, lat_spec],
            [shaped((lat, D), BF), shaped((lat, D), F32)] + [shaped((tokens, D), BF)] * 3
            + [shaped((groups, HL, size), F32), shaped((lat, D), BF), shaped((lat, D), F32), shaped((lat, D), BF)],
            2 * unit_flops, 12 * tokens * D,
            [pltpu.VMEM((lat, D), F32)],
        )(x, z, norms, read_in, read_out)

        a2_all = gather_rows(a2, n_blk).reshape(total, D)
        q3 = narrow(mm(b1, write_in[0]))

        owners = jnp.repeat(group_image[0], LAT)
        own = lax.dynamic_slice_in_dim(owners, lax.axis_index("blk") * lat, lat, 0)
        own_heads = jnp.tile(own, HEADS)
        hl2 = HEADS * lat
        k2, v2, p2, l2, o2, z2, out_latents, b3, k3, v3 = call(
            self_forward_kernel, (1,),
            [whole((total, D)), lat_spec, lat_spec, whole((total, 1)), whole((1, hl2)), norm_spec, three, square,
             one_of(1), one_of(2)],
            [whole((total, D)), whole((total, D)), whole((total, hl2)), whole((1, hl2))] + [lat_spec] * 6,
            [shaped((total, D), BF), shaped((total, D), BF), shaped((total, hl2), F32), shaped((1, hl2), F32),
             shaped((lat, D), BF), shaped((lat, D), F32), shaped((lat, D), BF), shaped((lat, D), BF),
             shaped((lat, D), F32), shaped((lat, D), F32)],
            unit_flops * 2, 10 * D * D * 2,
        )(a2_all, a2, z1, owners[:, None], own_heads[None, :], norms, self_in, self_out, write_in, write_in)

        out_patches, h, g, du, o3, e3, dq3, dx1, dk3, dv3, gain4, shift4 = call(
            functools.partial(patch_kernel, D), grid,
            [patch_spec, patch_spec, patch_spec, lat_spec, lat_spec, norm_spec, square,
             whole((D, hidden)), whole((hidden, D))],
            [patch_spec, patch_spec, rows_of((size, hidden)), rows_of((size, hidden)), patch_spec, patch_spec,
             patch_spec, patch_spec, rows_of((LAT, D)), rows_of((LAT, D)), whole((8, D)), whole((8, D))],
            [shaped((tokens, D), BF), shaped((tokens, D), BF), shaped((tokens, hidden), BF), shaped((tokens, hidden), BF),
             shaped((tokens, D), BF), shaped((tokens, D), BF), shaped((tokens, D), BF), shaped((tokens, D), F32),
             shaped((lat, D), F32), shaped((lat, D), F32), shaped((8, D), F32), shaped((8, D), F32)],
            unit_flops * 20, 40 * tokens * D,
        )(x, q3, cot, k3, v3, norms, write_out, feed_up, feed_down)

        dk3, dv3, dz2, e2, do2, inner2, dq2, gain3, shift3 = call(
            latent_back_kernel, (1,),
            [lat_spec] * 4 + [whole((total, D))] * 2 + [whole((total, hl2)), norm_spec, one_of(1), one_of(2), square],
            [lat_spec] * 5 + [whole((1, hl2)), lat_spec, whole((8, D)), whole((8, D))],
            [shaped((lat, D), BF), shaped((lat, D), BF), shaped((lat, D), F32), shaped((lat, D), BF), shaped((lat, D), BF),
             shaped((1, hl2), F32), shaped((lat, D), BF), shaped((8, D), F32), shaped((8, D), F32)],
            unit_flops, 10 * D * D,
        )(dk3, dv3, z2, cot_z, k2, v2, p2, norms, write_in, write_in, self_out)

        stats = jnp.concatenate([l2, inner2], 0)
        stats_top = narrow(stats)
        rest = stats - stats_top.astype(F32)
        stats_mid = narrow(rest)
        stats_low = narrow(rest - stats_mid.astype(F32))
        extra = jnp.concatenate([stats_top, stats_mid, stats_low], 0).reshape(-1, D)
        extra_rows = extra.shape[0]
        pad = -(lat + extra_rows) % 16
        payload = jnp.concatenate([do2, extra, jnp.zeros((pad, D), BF)], 0)
        spread = gather_rows(payload, n_blk)
        do_all = spread[:, :lat].reshape(total, D)
        stats_all = spread[:, lat : lat + extra_rows].reshape(n_blk, 3, 2, HEADS, lat).astype(F32)
        stats_all = jnp.sum(stats_all, axis=1).transpose(1, 2, 0, 3).reshape(2, HEADS, 1, total)
        q2_all = narrow(mm(a2_all, self_in[0]))

        up_part = merge_core([weight_halves(h, du, core, n_blk)])
        up_sum = scatter_sum(up_part, orders[0], n_blk)
        down_part = merge_core([weight_halves(g, cot, core, n_blk)])
        down_sum = scatter_sum(down_part, orders[1], n_blk)
        mid_part = merge_core(
            [weight_halves(o3, e3, core, n_blk), weight_halves(b1, dq3, core, n_blk),
             weight_halves(b3, dk3, core, n_blk), weight_halves(b3, dv3, core, n_blk),
             weight_halves(o2, e2, core, n_blk)]
        )
        mid_sum = scatter_sum(mid_part, orders[2], n_blk)

        place = lax.axis_index("blk") * lat
        k2_own = lax.dynamic_slice_in_dim(k2, place, lat, 0)
        v2_own = lax.dynamic_slice_in_dim(v2, place, lat, 0)
        dk2, dv2, dz1, e1, do1, gain2, shift2 = call(
            self_back_kernel, (1,),
            [whole((total, D))] * 2 + [whole((HEADS, 1, total))] * 2 + [whole((hl2, 1)), whole((1, total))]
            + [lat_spec] * 5 + [norm_spec, three, square],
            [lat_spec] * 5 + [whole((8, D)), whole((8, D))],
            [shaped((lat, D), BF), shaped((lat, D), BF), shaped((lat, D), F32), shaped((lat, D), BF), shaped((lat, D), F32),
             shaped((8, D), F32), shaped((8, D), F32)],
            unit_flops, 10 * D * D,
        )(q2_all, do_all, stats_all[0], stats_all[1], own_heads[:, None], owners[None, :], k2_own, v2_own,
          dq2, z1, dz2, norms, self_in, read_out)

        dq1, dk1, dv1 = call(
            read_back_kernel, grid,
            [lat_spec, lat_spec, pl.BlockSpec((None, HL, size), lambda g: (g, 0, 0)), patch_spec, patch_spec],
            [rows_of((LAT, D)), patch_spec, patch_spec],
            [shaped((lat, D), F32), shaped((tokens, D), BF), shaped((tokens, D), BF)],
            unit_flops / 2, 10 * tokens * D,
        )(do1, q1, p1, k1, v1)
        dq1 = narrow(dq1)

        dx, dz, gain1, shift1, gain0, shift0 = call(
            input_back_kernel, grid,
            [patch_spec] * 5 + [lat_spec] * 3 + [norm_spec, three, one_of(0)],
            [patch_spec, lat_spec] + [whole((8, D))] * 4,
            [shaped((tokens, D), BF), shaped((lat, D), BF)] + [shaped((8, D), F32)] * 4,
            unit_flops * 3, 14 * tokens * D,
        )(x, dx1, dq3, dk1, dv1, z, dz1, dq1, norms, read_in, write_in)

        late_self = scatter_sum(
            merge_core([weight_halves(a2, dq2, core, n_blk), weight_halves(a2, dk2, core, n_blk),
                        weight_halves(a2, dv2, core, n_blk)]),
            orders[0], n_blk)
        late_read = scatter_sum(
            merge_core([weight_halves(b1, dk1, core, n_blk), weight_halves(b1, dv1, core, n_blk)]),
            orders[1], n_blk)
        gains = jnp.sum(jnp.stack([gain0, gain1, gain2, gain3, gain4]), 1)
        shifts = jnp.sum(jnp.stack([shift0, shift1, shift2, shift3, shift4]), 1)
        norm_rows = D // n_blk

        def norm_block(which):
            block = narrow(jnp.where(which == 0, gains, shifts)).reshape(5, n_blk, norm_rows)
            block = block.transpose(1, 0, 2).reshape(n_blk, 5 * norm_rows)
            block = jnp.pad(block, ((0, 0), (0, 16 * (D // 2) - 5 * norm_rows)))
            return block.reshape(n_blk, 16, D // 2)

        late_mix = scatter_sum(
            merge_core([weight_halves(a1, dq1, core, n_blk), weight_halves(o1, e1, core, n_blk),
                        (norm_block(1 - core), norm_block(core))]),
            orders[2], n_blk)

        rows = D // n_blk
        up_rows = up_sum.reshape(rows, 2, -1, D // 2) if False else up_sum
        flat = jnp.concatenate([mid_sum, late_self, late_read, late_mix, down_sum], 0)
        up_flat = jnp.concatenate(
            [up_rows[:, i * (D // 2) : (i + 1) * (D // 2)] for i in range(hidden // D)], 0
        )
        flat = finish(jnp.concatenate([flat, up_flat], 0), core)
        partner = swap(flat, "rep", 0, n_rep)
        low = jnp.where(core == 0, flat, partner).astype(F32)
        high = jnp.where(core == 0, partner, flat).astype(F32)
        pieces = []
        start = 0
        for index in range(12):
            part = slice(start, start + rows)
            pieces.append(jnp.concatenate([low[part], high[part]], 1))
            start += rows
            if index == 11:
                norm_low, norm_high = low[start : start + 16], high[start : start + 16]
                start += 16
        wo_g, wq_g, wk_g, wv_g, so_g, sq_g, sk_g, sv_g, rk_g, rv_g, rq_g, ro_g = pieces
        down_g = jnp.concatenate(
            [low[start : start + hidden // n_blk], high[start : start + hidden // n_blk]], 1
        )
        start += hidden // n_blk
        up_low, up_high = [], []
        for _ in range(hidden // D):
            up_low.append(low[start : start + rows])
            up_high.append(high[start : start + rows])
            start += rows
        up_g = jnp.concatenate(up_low + up_high, 1)
        gain_g = norm_low.reshape(-1)[: 5 * norm_rows].reshape(5, norm_rows)
        shift_g = norm_high.reshape(-1)[: 5 * norm_rows].reshape(5, norm_rows)
        return (
            out_patches[None], out_latents[None], dx[None], dz[None], gain_g, shift_g,
            jnp.stack([rq_g, rk_g, rv_g]), ro_g,
            jnp.stack([sq_g, sk_g, sv_g]), so_g,
            jnp.stack([wq_g, wk_g, wv_g]), wo_g,
            up_g, down_g,
        )

    return body


def solution(mesh):
    return jax.shard_map(
        make_body(mesh.shape["blk"], mesh.shape["rep"]),
        mesh=mesh,
        in_specs=(
            P("rep", "blk", None), P("rep", "blk", None), P(), P(), P(), P(), P(), P(), P(), P(), P(), P(),
            P("rep", None), P("rep", "blk", None), P("rep", "blk", None),
        ),
        out_specs=(
            P("rep", "blk", None), P("rep", "blk", None), P("rep", "blk", None), P("rep", "blk", None),
            P(None, "blk"), P(None, "blk"), P(None, "blk", None), P("blk", None), P(None, "blk", None),
            P("blk", None), P(None, "blk", None), P("blk", None), P("blk", None), P("blk", None),
        ),
        check_vma=False,
    )
```

time: 1890 us -> 426 us (0.23)
  waiting for transfers between devices: 1500 us -> 169 us
  matrix products: 154 us -> 54.1 us
  blocking collectives: 90 us -> 0 us
  Pallas kernels: 0 us -> 88.5 us
  local copies, waits for them, and re-layouts: 77.8 us -> 29.1 us
  starting transfers between devices: 1.47 us -> 47.5 us
    reduce_scatter x8 -> x0, waiting for transfers between devices: 1020 us -> none  [the longest x1 142 us: body(): lax.psum_scatter(down_grad.astype(jnp.bfloat16), 'blk', scatter_dimension...]
    unnamed x17 -> x0, waiting for transfers between devices: 463 us -> none
    ppermute x0 -> x43, waiting for transfers between devices: none -> 169 us  [swap(): return lax.ppermute(tensor, axis, [(i, i ^ 1 << bit) for i in range(count)])]
    dot_general x61 -> x30, matrix products: 154 us -> 54.1 us  [the longest x28 46.5 us: mm_tn(): lax.dot_general(left, right, (((0,), (0,)), ((), ())), preferred_element_...]
    pallas_call x0 -> x7, Pallas kernels: none -> 88.5 us  [the longest x1 39.6 us: body(): call(functools.partial(patch_kernel, D), grid, [patch_spec, patch_spec, p...]
    all_gather x2 -> x0, blocking collectives: 87.5 us -> none  [the longest x1 47.1 us: body(): lax.all_gather(self_keys, 'blk', axis=0, tiled=True)]
    ppermute x0 -> x43, starting transfers between devices: none -> 47.5 us  [swap(): return lax.ppermute(tensor, axis, [(i, i ^ 1 << bit) for i in range(count)])]
    convert_element_type x20 -> x2, local copies, waits for them, and re-layouts: 21.3 us -> 0.19 us  [narrow(): return tensor.astype(BF)]
  transfers between devices with their start and end apart: 13 -> 43, of which waited for: 13 -> 22; matrix products, arithmetic and copies ran while one was open for 5% -> 16% of each run, Pallas kernels for 0% -> 6%
where the time goes in v1:
time: 426 us; the launch traced here: 419 us
  waiting for transfers between devices  169 us (40%)
  Pallas kernels  88.5 us (21%)
  matrix products  54.1 us (13%)
  starting transfers between devices  47.5 us (11%)
  local copies, waits for them, and re-layouts  29.1 us (7%)
  other arithmetic  28.8 us (7%)
    ppermute x43, waiting for transfers between devices, swap(): return lax.ppermute(tensor, axis, [(i, i ^ 1 << bit) for i in range(count)])  169 us
    ppermute x43, starting transfers between devices, swap(): return lax.ppermute(tensor, axis, [(i, i ^ 1 << bit) for i in range(count)])  47.5 us
    dot_general x28, matrix products, mm_tn(): lax.dot_general(left, right, (((0,), (0,)), ((), ())), preferred_element_...  46.5 us
    pallas_call x1, Pallas kernels, body(): call(functools.partial(patch_kernel, D), grid, [patch_spec, patch_spec, p...  39.6 us
    convert_element_type x29, other arithmetic, narrow(): return tensor.astype(BF)  17 us
    unnamed x126, local copies, waits for them, and re-layouts  15 us
    pallas_call x1, Pallas kernels, body(): call(input_back_kernel, grid, [patch_spec] * 5 + [lat_spec] * 3 + [norm_s...  11 us
    pallas_call x1, Pallas kernels, body(): call(read_forward_kernel, grid, [patch_spec, lat_spec, norm_spec, three,...  10.8 us
  transfers between devices with their start and end apart: 43, of which 22 were waited for; matrix products, arithmetic and copies ran while one was open for 16% of the time, Pallas kernels for 6%

profile of v1, /device:TPU:0, one launch (start us, length us, event | category | flops | bytes accessed | tf_op | source)
XLA Modules:
  0.0 419.2 jit_solution(11811812864425454818)
XLA Ops:
  2.2 10.8 %shard_map.254 = (bf16[32,768]{1,0:T(8,128)(2,1)}, f32[32,768]{1,0:T(8,128)}, bf16[1024,768]{1,0:T(8,128)(2,1)}, bf16[1024,768]{1,0:T(8,128)(2,1)}, bf16[1024,76...) custom-call(bf16[1024,768]{1,0:T(8,128)(2,1)} %bitcast.356, ...), custom_call_target="tpu_custom_call" | custom-call | flops 2415919104 | bytes 9437184 | tf_op jit(solution)/shard_map/pallas_call | solution.py:458
  12.9 4.1 collective-permute-start
  17.0 2.8 collective-permute-done
  22.1 3.2 collective-permute-done.1
  27.2 4.3 %convolution_convert_fusion.4.q3_ref = bf16[1024,768]{1,0:T(8,128)(2,1)} fusion(bf16[1024,768]{1,0:T(8,128)(2,1)} %get-tuple-element.70, bf16[3,768,768]{2,1,0:T(8,128)(2,1)} %wq_ref.1), kind=kOutput, calls=%fused_computation.23 | convolution fusion | flops 1208745984 | bytes 4325376 | tf_op jit(solution)/shard_map/dot_general | solution.py:26
  37.0 2.5 collective-permute-done.2
  39.9 2.2 collective-permute-done.5
  42.2 3.0 collective-permute-done.3
  45.5 3.2 convolution_convert_fusion.5.q_all_ref
  48.7 7.7 %shard_map.255 = (bf16[512,768]{1,0:T(8,128)(2,1)}, bf16[512,768]{1,0:T(8,128)(2,1)}, f32[512,384]{1,0:T(8,128)}, f32[1,384]{1,0:T(1,128)}, bf16[32,768]{1,0:T(8...) custom-call(bf16[512,768]{1,0:T(8,128)(2,1)} %bitcast.337, ...), custom_call_target="tpu_custom_call" | custom-call | flops 2415919104 | bytes 11796480 | tf_op jit(solution)/shard_map/pallas_call | solution.py:476
  56.5 39.6 %shard_map.256 = (bf16[1024,768]{1,0:T(8,128)(2,1)}, bf16[1024,768]{1,0:T(8,128)(2,1)}, bf16[1024,3072]{1,0:T(8,128)(2,1)}, bf16[1024,3072]{1,0:T(8,128)(2,1)}, ...) custom-call(bf16[1024,768]{1,0:T(8,128)(2,1)} %bitcast.357, ...), custom_call_target="tpu_custom_call" | custom-call | flops 24159191040 | bytes 31457280 | tf_op jit(solution)/shard_map/pallas_call | solution.py:487
  96.1 6.2 %shard_map.257 = (bf16[32,768]{1,0:T(8,128)(2,1)}, bf16[32,768]{1,0:T(8,128)(2,1)}, f32[32,768]{1,0:T(8,128)}, bf16[32,768]{1,0:T(8,128)(2,1)}, bf16[32,768]{1,0...) custom-call(f32[32,768]{1,0:T(8,128)} %get-tuple-element.79.dk3_ref, ...), custom_call_target="tpu_custom_call" | custom-call | flops 1207959552 | bytes 5898240 | tf_op jit(solution)/shard_map/pallas_call | solution.py:499
  103.7 2.6 convolution_convert_fusion.23
  118.1 4.8 %convolution_convert_fusion.1 = bf16[3072,384]{1,0:T(8,128)(2,1)} fusion(bf16[1024,3072]{1,0:T(8,128)(2,1)S(1)} %bitcast.389, bf16[1,1024,768]{2,1,0:T(8,128)(2,1)S(1)} %copy-done.38, s32[]{:T(128)S(6)} %select_n.333), kind=kOutput, calls=%fused_computation.6 | convolution fusion | flops 2417098752 | bytes 9437188 | tf_op jit(solution)/shard_map/dot_general | solution.py:30
  122.9 4.8 %convolution_convert_fusion = bf16[3072,384]{1,0:T(8,128)(2,1)} fusion(bf16[1024,3072]{1,0:T(8,128)(2,1)S(1)} %bitcast.389, bf16[1,1024,768]{2,1,0:T(8,128)(2,1)S(1)} %copy-done.38, s32[]{:T(128)S(6)} %select_n.334), kind=kOutput, calls=%fused_computation.5 | convolution fusion | flops 2417098752 | bytes 9437188 | tf_op jit(solution)/shard_map/dot_general | solution.py:30
  127.8 2.3 collective-permute-start.6
  135.2 5.9 %convolution_convert_fusion.3 = bf16[768,1536]{1,0:T(8,128)(2,1)} fusion(bf16[1024,768]{1,0:T(8,128)(2,1)S(1)} %copy-done.44, bf16[1024,3072]{1,0:T(8,128)(2,1)} %get-tuple-element.125, s32[]{:T(128)S(6)} %select_n.347), kind=kOutput, calls=%fused_computation.9 | convolution fusion | flops 2417098752 | bytes 7077892 | tf_op jit(solution)/shard_map/dot_general | solution.py:30
  141.1 4.3 %convolution_convert_fusion.2 = bf16[768,1536]{1,0:T(8,128)(2,1)} fusion(bf16[1024,768]{1,0:T(8,128)(2,1)S(1)} %copy-done.44, bf16[1024,3072]{1,0:T(8,128)(2,1)S(1)} %bitcast.391, s32[]{:T(128)S(6)} %select_n.348), kind=kOutput, calls=%fused_computation.8 | convolution fusion | flops 2417098752 | bytes 7077892 | tf_op jit(solution)/shard_map/dot_general | solution.py:30
  145.6 2.0 collective-permute-start.7
  147.8 4.3 %collective-permute-done.7 = bf16[2,48,768]{2,1,0:T(8,128)(2,1)S(1)} collective-permute-done((bf16[2,48,768]{2,1,0:T(8,128)(2,1)S(1)}, bf16[2,48,768]{2,1,0:T(8,128)(2,1)S(1)}, u32[]{:S(2)}, u32[]{:S(2)}) %collective-permute-start.7) | collective-permute-done | bytes 147488 | tf_op jit(solution)/shard_map/ppermute | solution.py:351
  154.6 3.3 collective-permute-done.10
  161.7 4.2 %collective-permute-done.11 = bf16[2,2,2,48,384]{4,3,0,1,2:T(8,128)(2,1)S(1)} collective-permute-done((bf16[2,2,2,48,384]{4,3,0,1,2:T(8,128)(2,1)S(1)}, bf16[2,2,2,48,384]{4,3,0,1,2:T(8,128)(2,1)S(1)}, u32[]{:S(2)}, u32[]{:S(2)}) %collective-permute-start.11) | collective-permute-done | bytes 294944 | tf_op jit(solution)/shard_map/ppermute | solution.py:351
  170.3 7.2 %shard_map.258 = (bf16[32,768]{1,0:T(8,128)(2,1)}, bf16[32,768]{1,0:T(8,128)(2,1)}, f32[32,768]{1,0:T(8,128)}, bf16[32,768]{1,0:T(8,128)(2,1)}, f32[32,768]{1,0:...) custom-call(bf16[512,768]{1,0:T(8,128)(2,1)} %convolution_convert_fusion.5.q_all_ref, bf16[512,768]{1,0:T(8,128)(2,1)} %bitcast.335, ...), custom_call_target="tpu_custom_call" | custom-call | flops 1207959552 | bytes 5898240 | tf_op jit(solution)/shard_map/pallas_call | solution.py:537
  177.5 1.9 convolution_convert_fusion.14
  179.4 1.9 convolution_convert_fusion.17
  181.3 6.0 %shard_map.259 = (f32[32,768]{1,0:T(8,128)}, bf16[1024,768]{1,0:T(8,128)(2,1)}, bf16[1024,768]{1,0:T(8,128)(2,1)}) custom-call(f32[32,768]{1,0:T(8,128)} %get-tuple-element.90.do1_ref, f32[32,768]{1,0:T(8,128)} %get-tuple-element.91.q1_ref, f32[4,96,256]{2,1,0:T(8,128)} %get-tuple-element.92.p1_ref, bf16[1024,768]{1,0:T(8,128)(2,1)} %get-tuple-element.93.k1_ref, ...), custom_call_target="tpu_custom_call" | custom-call | flops 603979776 | bytes 7864320 | tf_op jit(solution)/shard_map/pallas_call | solution.py:548
  190.1 2.8 convolution_convert_fusion.10
  195.0 11.0 %shard_map.260 = (bf16[1024,768]{1,0:T(8,128)(2,1)}, bf16[32,768]{1,0:T(8,128)(2,1)}, f32[8,768]{1,0:T(8,128)}, f32[8,768]{1,0:T(8,128)}, f32[8,768]{1,0:T(8,128)}, /*index=5*/f32[8,768]{1,0:T(8,128)}) custom-call(bf16[1024,768]{1,0:T(8,128)(2,1)} %bitcast.358, f32[1024,768]{1,0:T(8,128)} %get-tuple-element.77.dx1_ref, ...), custom_call_target="tpu_custom_call" | custom-call | flops 3623878656 | bytes 11010048 | tf_op jit(solution)/shard_map/pallas_call | solution.py:557
  224.8 2.4 fusion.1
  229.1 2.4 fusion
  231.8 5.0 %collective-permute-done.23 = bf16[2,2,2,96,384]{4,3,0,2,1:T(8,128)(2,1)S(1)} collective-permute-done((bf16[2,2,2,96,384]{4,3,0,2,1:T(8,128)(2,1)S(1)}, bf16[2,2,2,96,384]{4,3,0,2,1:T(8,128)(2,1)S(1)}, u32[]{:S(2)}, u32[]{:S(2)}) %collective-permute-start.23) | collective-permute-done | bytes 589856 | tf_op jit(solution)/shard_map/ppermute | solution.py:351
  239.9 7.3 %collective-permute-done.24 = bf16[2,2,96,384]{3,2,0,1:T(8,128)(2,1)S(1)} collective-permute-done((bf16[2,2,96,384]{3,2,0,1:T(8,128)(2,1)S(1)}, bf16[2,2,96,384]{3,2,0,1:T(8,128)(2,1)S(1)}, u32[]{:S(2)}, u32[]{:S(2)}) %collective-permute-start.24) | collective-permute-done | bytes 294944 | tf_op jit(solution)/shard_map/ppermute | solution.py:351
  249.7 36.5 %collective-permute-done.25 = bf16[2,96,384]{2,1,0:T(8,128)(2,1)S(1)} collective-permute-done((bf16[2,96,384]{2,1,0:T(8,128)(2,1)S(1)}, bf16[2,96,384]{2,1,0:T(8,128)(2,1)S(1)}, u32[]{:S(2)}, u32[]{:S(2)}) %collective-permute-start.25) | collective-permute-done | bytes 147488 | tf_op jit(solution)/shard_map/ppermute | solution.py:351
  286.8 7.7 %collective-permute-done.29 = bf16[2,2,112,384]{3,2,0,1:T(8,128)(2,1)S(1)} collective-permute-done((bf16[2,2,112,384]{3,2,0,1:T(8,128)(2,1)S(1)}, bf16[2,2,112,384]{3,2,0,1:T(8,128)(2,1)S(1)}, u32[]{:S(2)}, u32[]{:S(2)}) %collective-permute-start.29) | collective-permute-done | bytes 344096 | tf_op jit(solution)/shard_map/ppermute | solution.py:351
  295.5 2.6 add_convert_fusion
  298.2 2.1 collective-permute-done.30
  301.7 3.2 collective-permute-start.31
  306.9 6.6 %collective-permute-done.19 = bf16[2,2,144,384]{3,2,0,1:T(8,128)(2,1)S(1)} collective-permute-done((bf16[2,2,144,384]{3,2,0,1:T(8,128)(2,1)S(1)}, bf16[2,2,144,384]{3,2,0,1:T(8,128)(2,1)S(1)}, u32[]{:S(2)}, u32[]{:S(2)}) %collective-permute-start.19) | collective-permute-done | bytes 442400 | tf_op jit(solution)/shard_map/ppermute | solution.py:351
  314.2 36.4 %collective-permute-done.20 = bf16[2,144,384]{2,1,0:T(8,128)(2,1)S(1)} collective-permute-done((bf16[2,144,384]{2,1,0:T(8,128)(2,1)S(1)}, bf16[2,144,384]{2,1,0:T(8,128)(2,1)S(1)}, u32[]{:S(2)}, u32[]{:S(2)}) %collective-permute-start.20) | collective-permute-done | bytes 221216 | tf_op jit(solution)/shard_map/ppermute | solution.py:351
  351.3 2.7 collective-permute-start.21
  356.6 6.0 %collective-permute-done.39 = bf16[2,2,48,1536]{3,2,0,1:T(8,128)(2,1)S(1)} collective-permute-done((bf16[2,2,48,1536]{3,2,0,1:T(8,128)(2,1)S(1)}, bf16[2,2,48,1536]{3,2,0,1:T(8,128)(2,1)S(1)}, u32[]{:S(2)}, u32[]{:S(2)}) %collective-permute-start.39) | collective-permute-done | bytes 589856 | tf_op jit(solution)/shard_map/ppermute | solution.py:351
  365.3 11.8 %collective-permute-done.14 = bf16[2,2,240,384]{3,2,1,0:T(8,128)(2,1)S(1)} collective-permute-done((bf16[2,2,240,384]{3,2,1,0:T(8,128)(2,1)S(1)}, bf16[2,2,240,384]{3,2,1,0:T(8,128)(2,1)S(1)}, u32[]{:S(2)}, u32[]{:S(2)}) %collective-permute-start.14) | collective-permute-done | bytes 737312 | tf_op jit(solution)/shard_map/ppermute | solution.py:351
  377.6 1.9 collective-permute-start.15
  379.5 5.6 %collective-permute-done.15 = bf16[2,240,384]{2,1,0:T(8,128)(2,1)S(1)} collective-permute-done((bf16[2,240,384]{2,1,0:T(8,128)(2,1)S(1)}, bf16[2,240,384]{2,1,0:T(8,128)(2,1)S(1)}, u32[]{:S(2)}, u32[]{:S(2)}) %collective-permute-start.15) | collective-permute-done | bytes 368672 | tf_op jit(solution)/shard_map/ppermute | solution.py:351
  385.1 2.7 collective-permute-start.41
  388.0 6.8 %collective-permute-done.41 = bf16[48,1536]{1,0:T(8,128)(2,1)S(1)} collective-permute-done((bf16[48,1536]{1,0:T(8,128)(2,1)S(1)}, bf16[48,1536]{1,0:T(8,128)(2,1)S(1)}, u32[]{:S(2)}, u32[]{:S(2)}) %collective-permute-start.41) | collective-permute-done | bytes 147488 | tf_op jit(solution)/shard_map/ppermute | solution.py:351
  395.6 7.6 %collective-permute-done.16 = bf16[240,384]{1,0:T(8,128)(2,1)S(1)} collective-permute-done((bf16[240,384]{1,0:T(8,128)(2,1)S(1)}, bf16[240,384]{1,0:T(8,128)(2,1)S(1)}, u32[]{:S(2)}, u32[]{:S(2)}) %collective-permute-start.16) | collective-permute-done | bytes 184352 | tf_op jit(solution)/shard_map/ppermute | solution.py:351
  403.6 2.2 collective-permute-done.42
  (359 shorter events, 98.3 us)
Async XLA Ops:
  12.9 6.9 %collective-permute-start = (bf16[32,768]{1,0:T(8,128)(2,1)}, bf16[32,768]{1,0:T(8,128)(2,1)S(1)}, u32[]{:S(2)}, u32[]{:S(2)}) collective-permute-start(bf16[32,768]{1,0:T(8,128)(2,1)} %get-tuple-element.71.a2_ref), channel_id=1, source_target_pairs={{0,16},{2,18},{4,20},{6,22},{8,24},{10,26},{12,28},{14,30},{16,0},... | collective-permute-start | bytes 147464 | tf_op jit(solution)/shard_map/ppermute | solution.py:351
  20.7 4.7 %collective-permute-start.1 = (bf16[2,32,768]{2,1,0:T(8,128)(2,1)S(1)}, bf16[2,32,768]{2,1,0:T(8,128)(2,1)S(1)}, u32[]{:S(2)}, u32[]{:S(2)}) collective-permute-start(bf16[2,32,768]{2,1,0:T(8,128)(2,1)S(1)} %pad_maximum_fusion.17), channel_id=1, source_target_pairs={{0,8},{2,10},{4,12},{6,14},{8,0},{10,2},{12,4},{14,6},{16,24},{18,... | collective-permute-start | bytes 294920 | tf_op jit(solution)/shard_map/ppermute | solution.py:351
  25.4 11.0 %collective-permute-start.4 = (bf16[2,2,32,384]{3,2,0,1:T(8,128)(2,1)S(1)}, bf16[2,2,32,384]{3,2,0,1:T(8,128)(2,1)S(1)}, u32[]{:S(2)}, u32[]{:S(2)}) collective-permute-start(bf16[2,2,32,384]{3,2,0,1:T(8,128)(2,1)S(1)} %get-tuple-element.185), channel_id=1, source_target_pairs={{0,2},{2,0},{4,6},{6,4},{8,10},{10,8},{12,14},{14,12},{16,18},{18,... | collective-permute-start | bytes 294920 | tf_op jit(solution)/shard_map/ppermute | solution.py:351
  34.9 4.6 %collective-permute-start.2 = (bf16[2,2,32,384]{3,2,0,1:T(8,128)(2,1)S(1)}, bf16[2,2,32,384]{3,2,0,1:T(8,128)(2,1)S(1)}, u32[]{:S(2)}, u32[]{:S(2)}) collective-permute-start(bf16[2,2,32,384]{3,2,0,1:T(8,128)(2,1)S(1)} %get-tuple-element.184), channel_id=1, source_target_pairs={{0,4},{2,6},{4,0},{6,2},{8,12},{10,14},{12,8},{14,10},{16,20},{18,... | collective-permute-start | bytes 294920 | tf_op jit(solution)/shard_map/ppermute | solution.py:351
  36.4 5.7 %collective-permute-start.5 = (bf16[2,2,2,32,384]{4,3,0,1,2:T(8,128)(2,1)S(1)}, bf16[2,2,2,32,384]{4,3,0,1,2:T(8,128)(2,1)S(1)}, u32[]{:S(2)}, u32[]{:S(2)}) collective-permute-start(bf16[2,2,2,32,384]{4,3,0,1,2:T(8,128)(2,1)S(1)} %pad_maximum_fusion.10), channel_id=1, source_target_pairs={{0,4},{2,6},{4,0},{6,2},{8,12},{10,14},{12,8},{14,10},{16,20},{18,... | collective-permute-start | bytes 589832 | tf_op jit(solution)/shard_map/ppermute | solution.py:351
  39.5 5.7 %collective-permute-start.3 = (bf16[2,2,2,32,384]{4,3,0,1,2:T(8,128)(2,1)S(1)}, bf16[2,2,2,32,384]{4,3,0,1,2:T(8,128)(2,1)S(1)}, u32[]{:S(2)}, u32[]{:S(2)}) collective-permute-start(bf16[2,2,2,32,384]{4,3,0,1,2:T(8,128)(2,1)S(1)} %pad_maximum_fusion.9), channel_id=1, source_target_pairs={{0,2},{2,0},{4,6},{6,4},{8,10},{10,8},{12,14},{14,12},{16,18},{18,... | collective-permute-start | bytes 589832 | tf_op jit(solution)/shard_map/ppermute | solution.py:351
  127.8 17.6 %collective-permute-start.6 = (bf16[48,768]{1,0:T(8,128)(2,1)S(1)}, bf16[48,768]{1,0:T(8,128)(2,1)S(1)}, u32[]{:S(2)}, u32[]{:S(2)}) collective-permute-start(bf16[48,768]{1,0:T(8,128)(2,1)S(1)} %maximum_maximum_fusion.2), channel_id=1, source_target_pairs={{0,16},{2,18},{4,20},{6,22},{8,24},{10,26},{12,28},{14,30},{16,0},... | collective-permute-start | bytes 221192 | tf_op jit(solution)/shard_map/ppermute | solution.py:351
  134.7 160.2 %collective-permute-start.12 = (bf16[16,240,384]{2,1,0:T(8,128)(2,1)}, bf16[16,240,384]{2,1,0:T(8,128)(2,1)}, u32[]{:S(2)}, u32[]{:S(2)}) collective-permute-start(bf16[16,240,384]{2,1,0:T(8,128)(2,1)} %constant_dynamic-update-slice_fusion.5), channel_id=1, source_target_pairs={{0,1},{1,0},{2,3},{3,2},{4,5},{5,4},{6,7},{7,6},{8,9},{9,8},{10,11... | collective-permute-start | bytes 8847368 | tf_op jit(solution)/shard_map/ppermute | solution.py:351
  134.7 88.6 %collective-permute-start.32 = (bf16[16,192,384]{2,1,0:T(8,128)(2,1)}, bf16[16,192,384]{2,1,0:T(8,128)(2,1)}, u32[]{:S(2)}, u32[]{:S(2)}) collective-permute-start(bf16[16,192,384]{2,1,0:T(8,128)(2,1)} %bitcast.116), channel_id=1, source_target_pairs={{0,1},{1,0},{2,3},{3,2},{4,5},{5,4},{6,7},{7,6},{8,9},{9,8},{10,11... | collective-permute-start | bytes 7077896 | tf_op jit(solution)/shard_map/ppermute | solution.py:351
  145.4 82.2 %collective-permute-start.37 = (bf16[16,48,1536]{2,1,0:T(8,128)(2,1)}, bf16[16,48,1536]{2,1,0:T(8,128)(2,1)}, u32[]{:S(2)}, u32[]{:S(2)}) collective-permute-start(bf16[16,48,1536]{2,1,0:T(8,128)(2,1)} %bitcast.127), channel_id=1, source_target_pairs={{0,1},{1,0},{2,3},{3,2},{4,5},{5,4},{6,7},{7,6},{8,9},{9,8},{10,11... | collective-permute-start | bytes 7077896 | tf_op jit(solution)/shard_map/ppermute | solution.py:351
  145.6 6.5 %collective-permute-start.7 = (bf16[2,48,768]{2,1,0:T(8,128)(2,1)S(1)}, bf16[2,48,768]{2,1,0:T(8,128)(2,1)S(1)}, u32[]{:S(2)}, u32[]{:S(2)}) collective-permute-start(bf16[2,48,768]{2,1,0:T(8,128)(2,1)S(1)} %pad_maximum_fusion.12), channel_id=1, source_target_pairs={{0,8},{2,10},{4,12},{6,14},{8,0},{10,2},{12,4},{14,6},{16,24},{18,... | collective-permute-start | bytes 442376 | tf_op jit(solution)/shard_map/ppermute | solution.py:351
  152.2 5.7 %collective-permute-start.10 = (bf16[2,2,48,384]{3,2,0,1:T(8,128)(2,1)S(1)}, bf16[2,2,48,384]{3,2,0,1:T(8,128)(2,1)S(1)}, u32[]{:S(2)}, u32[]{:S(2)}) collective-permute-start(bf16[2,2,48,384]{3,2,0,1:T(8,128)(2,1)S(1)} %get-tuple-element.175), channel_id=1, source_target_pairs={{0,2},{2,0},{4,6},{6,4},{8,10},{10,8},{12,14},{14,12},{16,18},{18,... | collective-permute-start | bytes 442376 | tf_op jit(solution)/shard_map/ppermute | solution.py:351
  153.0 6.5 %collective-permute-start.8 = (bf16[2,2,48,384]{3,2,0,1:T(8,128)(2,1)S(1)}, bf16[2,2,48,384]{3,2,0,1:T(8,128)(2,1)S(1)}, u32[]{:S(2)}, u32[]{:S(2)}) collective-permute-start(bf16[2,2,48,384]{3,2,0,1:T(8,128)(2,1)S(1)} %get-tuple-element.174), channel_id=1, source_target_pairs={{0,4},{2,6},{4,0},{6,2},{8,12},{10,14},{12,8},{14,10},{16,20},{18,... | collective-permute-start | bytes 442376 | tf_op jit(solution)/shard_map/ppermute | solution.py:351
  157.9 8.0 %collective-permute-start.11 = (bf16[2,2,2,48,384]{4,3,0,1,2:T(8,128)(2,1)S(1)}, bf16[2,2,2,48,384]{4,3,0,1,2:T(8,128)(2,1)S(1)}, u32[]{:S(2)}, u32[]{:S(2)}) collective-permute-start(bf16[2,2,2,48,384]{4,3,0,1,2:T(8,128)(2,1)S(1)} %pad_maximum_fusion.8), channel_id=1, source_target_pairs={{0,4},{2,6},{4,0},{6,2},{8,12},{10,14},{12,8},{14,10},{16,20},{18,... | collective-permute-start | bytes 884744 | tf_op jit(solution)/shard_map/ppermute | solution.py:351
  159.6 7.7 %collective-permute-start.9 = (bf16[2,2,2,48,384]{4,3,0,1,2:T(8,128)(2,1)S(1)}, bf16[2,2,2,48,384]{4,3,0,1,2:T(8,128)(2,1)S(1)}, u32[]{:S(2)}, u32[]{:S(2)}) collective-permute-start(bf16[2,2,2,48,384]{4,3,0,1,2:T(8,128)(2,1)S(1)} %pad_maximum_fusion.7), channel_id=1, source_target_pairs={{0,2},{2,0},{4,6},{6,4},{8,10},{10,8},{12,14},{14,12},{16,18},{18,... | collective-permute-start | bytes 884744 | tf_op jit(solution)/shard_map/ppermute | solution.py:351
  195.0 23.8 %collective-permute-start.22 = (bf16[16,96,384]{2,1,0:T(8,128)(2,1)}, bf16[16,96,384]{2,1,0:T(8,128)(2,1)}, u32[]{:S(2)}, u32[]{:S(2)}) collective-permute-start(bf16[16,96,384]{2,1,0:T(8,128)(2,1)} %pad_maximum_fusion.2), channel_id=1, source_target_pairs={{0,1},{1,0},{2,3},{3,2},{4,5},{5,4},{6,7},{7,6},{8,9},{9,8},{10,11... | collective-permute-start | bytes 3538952 | tf_op jit(solution)/shard_map/ppermute | solution.py:351
  195.0 13.4 %copy-start.35 = (f32[8,768]{1,0:T(8,128)S(1)}, f32[8,768]{1,0:T(8,128)}, u32[]{:S(2)}) copy-start(f32[8,768]{1,0:T(8,128)} %get-tuple-element.115) | copy-start | bytes 73732
  195.0 13.4 %copy-start.34 = (f32[8,768]{1,0:T(8,128)S(1)}, f32[8,768]{1,0:T(8,128)}, u32[]{:S(2)}) copy-start(f32[8,768]{1,0:T(8,128)} %get-tuple-element.116) | copy-start | bytes 73732
  195.0 13.4 %copy-start.32 = (f32[8,768]{1,0:T(8,128)S(1)}, f32[8,768]{1,0:T(8,128)}, u32[]{:S(2)}) copy-start(f32[8,768]{1,0:T(8,128)} %get-tuple-element.117) | copy-start | bytes 73732
  195.0 14.9 %copy-start.33 = (f32[8,768]{1,0:T(8,128)S(1)}, f32[8,768]{1,0:T(8,128)}, u32[]{:S(2)}) copy-start(f32[8,768]{1,0:T(8,128)} %get-tuple-element.121) | copy-start | bytes 73732
  195.0 14.9 %copy-start.31 = (f32[8,768]{1,0:T(8,128)S(1)}, f32[8,768]{1,0:T(8,128)}, u32[]{:S(2)}) copy-start(f32[8,768]{1,0:T(8,128)} %get-tuple-element.122) | copy-start | bytes 73732
  212.3 8.3 %collective-permute-start.27 = (bf16[16,112,384]{2,1,0:T(8,128)(2,1)}, bf16[16,112,384]{2,1,0:T(8,128)(2,1)}, u32[]{:S(2)}, u32[]{:S(2)}) collective-permute-start(bf16[16,112,384]{2,1,0:T(8,128)(2,1)} %pad_maximum_fusion.1), channel_id=1, source_target_pairs={{0,1},{1,0},{2,3},{3,2},{4,5},{5,4},{6,7},{7,6},{8,9},{9,8},{10,11... | collective-permute-start | bytes 4128776 | tf_op jit(solution)/shard_map/ppermute | solution.py:351
  218.8 18.8 %collective-permute-start.17 = (bf16[16,144,384]{2,1,0:T(8,128)(2,1)S(1)}, bf16[16,144,384]{2,1,0:T(8,128)(2,1)S(1)}, u32[]{:S(2)}, u32[]{:S(2)}) collective-permute-start(bf16[16,144,384]{2,1,0:T(8,128)(2,1)S(1)} %pad_maximum_fusion), channel_id=1, source_target_pairs={{0,1},{1,0},{2,3},{3,2},{4,5},{5,4},{6,7},{7,6},{8,9},{9,8},{10,11... | collective-permute-start | bytes 5308424 | tf_op jit(solution)/shard_map/ppermute | solution.py:351
  220.7 16.2 %collective-permute-start.23 = (bf16[2,2,2,96,384]{4,3,0,2,1:T(8,128)(2,1)S(1)}, bf16[2,2,2,96,384]{4,3,0,2,1:T(8,128)(2,1)S(1)}, u32[]{:S(2)}, u32[]{:S(2)}) collective-permute-start(bf16[2,2,2,96,384]{4,3,0,2,1:T(8,128)(2,1)S(1)} %bitcast.372), channel_id=1, source_target_pairs={{0,4},{2,6},{4,0},{6,2},{8,12},{10,14},{12,8},{14,10},{16,20},{18,... | collective-permute-start | bytes 1769480 | tf_op jit(solution)/shard_map/ppermute | solution.py:351
  223.3 25.4 %collective-permute-start.28 = (bf16[2,2,2,112,384]{4,3,0,1,2:T(8,128)(2,1)S(1)}, bf16[2,2,2,112,384]{4,3,0,1,2:T(8,128)(2,1)S(1)}, u32[]{:S(2)}, u32[]{:S(2)}) collective-permute-start(bf16[2,2,2,112,384]{4,3,0,1,2:T(8,128)(2,1)S(1)} %bitcast.367), channel_id=1, source_target_pairs={{0,8},{2,10},{4,12},{6,14},{8,0},{10,2},{12,4},{14,6},{16,24},{18,... | collective-permute-start | bytes 2064392 | tf_op jit(solution)/shard_map/ppermute | solution.py:351
  227.6 77.6 %collective-permute-start.33 = (bf16[2,2,2,192,384]{4,3,0,2,1:T(8,128)(2,1)S(1)}, bf16[2,2,2,192,384]{4,3,0,2,1:T(8,128)(2,1)S(1)}, u32[]{:S(2)}, u32[]{:S(2)}) collective-permute-start(bf16[2,2,2,192,384]{4,3,0,2,1:T(8,128)(2,1)S(1)} %bitcast.359), channel_id=1, source_target_pairs={{0,4},{2,6},{4,0},{6,2},{8,12},{10,14},{12,8},{14,10},{16,20},{18,... | collective-permute-start | bytes 3538952 | tf_op jit(solution)/shard_map/ppermute | solution.py:351
  236.9 69.3 %collective-permute-start.38 = (bf16[2,2,2,48,1536]{4,3,0,1,2:T(8,128)(2,1)S(1)}, bf16[2,2,2,48,1536]{4,3,0,1,2:T(8,128)(2,1)S(1)}, u32[]{:S(2)}, u32[]{:S(2)}) collective-permute-start(bf16[2,2,2,48,1536]{4,3,0,1,2:T(8,128)(2,1)S(1)} %bitcast.360), channel_id=1, source_target_pairs={{0,2},{2,0},{4,6},{6,4},{8,10},{10,8},{12,14},{14,12},{16,18},{18,... | collective-permute-start | bytes 3538952 | tf_op jit(solution)/shard_map/ppermute | solution.py:351
  237.6 9.6 %collective-permute-start.24 = (bf16[2,2,96,384]{3,2,0,1:T(8,128)(2,1)S(1)}, bf16[2,2,96,384]{3,2,0,1:T(8,128)(2,1)S(1)}, u32[]{:S(2)}, u32[]{:S(2)}) collective-permute-start(bf16[2,2,96,384]{3,2,0,1:T(8,128)(2,1)S(1)} %dynamic-slice_bitcast_fusion.9), channel_id=1, source_target_pairs={{0,8},{2,10},{4,12},{6,14},{8,0},{10,2},{12,4},{14,6},{16,24},{18,... | collective-permute-start | bytes 884744 | tf_op jit(solution)/shard_map/ppermute | solution.py:351
  247.2 54.5 %collective-permute-start.18 = (bf16[2,2,2,144,384]{4,3,0,1,2:T(8,128)(2,1)S(1)}, bf16[2,2,2,144,384]{4,3,0,1,2:T(8,128)(2,1)S(1)}, u32[]{:S(2)}, u32[]{:S(2)}) collective-permute-start(bf16[2,2,2,144,384]{4,3,0,1,2:T(8,128)(2,1)S(1)} %bitcast.362), channel_id=1, source_target_pairs={{0,2},{2,0},{4,6},{6,4},{8,10},{10,8},{12,14},{14,12},{16,18},{18,... | collective-permute-start | bytes 2654216 | tf_op jit(solution)/shard_map/ppermute | solution.py:351
  248.6 37.5 %collective-permute-start.25 = (bf16[2,96,384]{2,1,0:T(8,128)(2,1)S(1)}, bf16[2,96,384]{2,1,0:T(8,128)(2,1)S(1)}, u32[]{:S(2)}, u32[]{:S(2)}) collective-permute-start(bf16[2,96,384]{2,1,0:T(8,128)(2,1)S(1)} %dynamic-slice_bitcast_fusion.15), channel_id=1, source_target_pairs={{0,2},{2,0},{4,6},{6,4},{8,10},{10,8},{12,14},{14,12},{16,18},{18,... | collective-permute-start | bytes 442376 | tf_op jit(solution)/shard_map/ppermute | solution.py:351
  286.2 8.4 %collective-permute-start.29 = (bf16[2,2,112,384]{3,2,0,1:T(8,128)(2,1)S(1)}, bf16[2,2,112,384]{3,2,0,1:T(8,128)(2,1)S(1)}, u32[]{:S(2)}, u32[]{:S(2)}) collective-permute-start(bf16[2,2,112,384]{3,2,0,1:T(8,128)(2,1)S(1)} %dynamic-slice_bitcast_fusion.6), channel_id=1, source_target_pairs={{0,2},{2,0},{4,6},{6,4},{8,10},{10,8},{12,14},{14,12},{16,18},{18,... | collective-permute-start | bytes 1032200 | tf_op jit(solution)/shard_map/ppermute | solution.py:351
  294.5 108.8 %collective-permute-start.26 = (bf16[96,384]{1,0:T(8,128)(2,1)S(1)}, bf16[96,384]{1,0:T(8,128)(2,1)S(1)}, u32[]{:S(2)}, u32[]{:S(2)}) collective-permute-start(bf16[96,384]{1,0:T(8,128)(2,1)S(1)} %dynamic-slice_bitcast_fusion.18), channel_id=1, source_target_pairs={{0,16},{2,18},{4,20},{6,22},{8,24},{10,26},{12,28},{14,30},{16,0},... | collective-permute-start | bytes 221192 | tf_op jit(solution)/shard_map/ppermute | solution.py:351
  294.9 5.5 %collective-permute-start.30 = (bf16[2,112,384]{2,1,0:T(8,128)(2,1)S(1)}, bf16[2,112,384]{2,1,0:T(8,128)(2,1)S(1)}, u32[]{:S(2)}, u32[]{:S(2)}) collective-permute-start(bf16[2,112,384]{2,1,0:T(8,128)(2,1)S(1)} %dynamic-slice_bitcast_fusion.12), channel_id=1, source_target_pairs={{0,4},{2,6},{4,0},{6,2},{8,12},{10,14},{12,8},{14,10},{16,20},{18,... | collective-permute-start | bytes 516104 | tf_op jit(solution)/shard_map/ppermute | solution.py:351
  300.4 54.1 %collective-permute-start.13 = (bf16[2,2,2,240,384]{4,3,2,1,0:T(8,128)(2,1)S(1)}, bf16[2,2,2,240,384]{4,3,2,1,0:T(8,128)(2,1)S(1)}, u32[]{:S(2)}, u32[]{:S(2)}) collective-permute-start(bf16[2,2,2,240,384]{4,3,2,1,0:T(8,128)(2,1)S(1)} %dynamic-slice_bitcast_fusion), channel_id=1, source_target_pairs={{0,8},{2,10},{4,12},{6,14},{8,0},{10,2},{12,4},{14,6},{16,24},{18,... | collective-permute-start | bytes 4423688 | tf_op jit(solution)/shard_map/ppermute | solution.py:351
  301.7 101.7 %collective-permute-start.31 = (bf16[112,384]{1,0:T(8,128)(2,1)S(1)}, bf16[112,384]{1,0:T(8,128)(2,1)S(1)}, u32[]{:S(2)}, u32[]{:S(2)}) collective-permute-start(bf16[112,384]{1,0:T(8,128)(2,1)S(1)} %dynamic-slice_bitcast_fusion.17), channel_id=1, source_target_pairs={{0,16},{2,18},{4,20},{6,22},{8,24},{10,26},{12,28},{14,30},{16,0},... | collective-permute-start | bytes 258056 | tf_op jit(solution)/shard_map/ppermute | solution.py:351
  305.2 8.4 %collective-permute-start.19 = (bf16[2,2,144,384]{3,2,0,1:T(8,128)(2,1)S(1)}, bf16[2,2,144,384]{3,2,0,1:T(8,128)(2,1)S(1)}, u32[]{:S(2)}, u32[]{:S(2)}) collective-permute-start(bf16[2,2,144,384]{3,2,0,1:T(8,128)(2,1)S(1)} %dynamic-slice_bitcast_fusion.4), channel_id=1, source_target_pairs={{0,4},{2,6},{4,0},{6,2},{8,12},{10,14},{12,8},{14,10},{16,20},{18,... | collective-permute-start | bytes 1327112 | tf_op jit(solution)/shard_map/ppermute | solution.py:351
  306.1 45.1 %collective-permute-start.34 = (bf16[2,2,192,384]{3,2,0,1:T(8,128)(2,1)S(1)}, bf16[2,2,192,384]{3,2,0,1:T(8,128)(2,1)S(1)}, u32[]{:S(2)}, u32[]{:S(2)}) collective-permute-start(bf16[2,2,192,384]{3,2,0,1:T(8,128)(2,1)S(1)} %dynamic-slice_bitcast_fusion.3), channel_id=1, source_target_pairs={{0,8},{2,10},{4,12},{6,14},{8,0},{10,2},{12,4},{14,6},{16,24},{18,... | collective-permute-start | bytes 1769480 | tf_op jit(solution)/shard_map/ppermute | solution.py:351
  313.7 36.9 %collective-permute-start.20 = (bf16[2,144,384]{2,1,0:T(8,128)(2,1)S(1)}, bf16[2,144,384]{2,1,0:T(8,128)(2,1)S(1)}, u32[]{:S(2)}, u32[]{:S(2)}) collective-permute-start(bf16[2,144,384]{2,1,0:T(8,128)(2,1)S(1)} %dynamic-slice_bitcast_fusion.10), channel_id=1, source_target_pairs={{0,8},{2,10},{4,12},{6,14},{8,0},{10,2},{12,4},{14,6},{16,24},{18,... | collective-permute-start | bytes 663560 | tf_op jit(solution)/shard_map/ppermute | solution.py:351
  350.6 12.0 %collective-permute-start.39 = (bf16[2,2,48,1536]{3,2,0,1:T(8,128)(2,1)S(1)}, bf16[2,2,48,1536]{3,2,0,1:T(8,128)(2,1)S(1)}, u32[]{:S(2)}, u32[]{:S(2)}) collective-permute-start(bf16[2,2,48,1536]{3,2,0,1:T(8,128)(2,1)S(1)} %dynamic-slice_bitcast_fusion.2), channel_id=1, source_target_pairs={{0,4},{2,6},{4,0},{6,2},{8,12},{10,14},{12,8},{14,10},{16,20},{18,... | collective-permute-start | bytes 1769480 | tf_op jit(solution)/shard_map/ppermute | solution.py:351
  351.3 52.0 %collective-permute-start.21 = (bf16[144,384]{1,0:T(8,128)(2,1)S(1)}, bf16[144,384]{1,0:T(8,128)(2,1)S(1)}, u32[]{:S(2)}, u32[]{:S(2)}) collective-permute-start(bf16[144,384]{1,0:T(8,128)(2,1)S(1)} %dynamic-slice_bitcast_fusion.16), channel_id=1, source_target_pairs={{0,16},{2,18},{4,20},{6,22},{8,24},{10,26},{12,28},{14,30},{16,0},... | collective-permute-start | bytes 331784 | tf_op jit(solution)/shard_map/ppermute | solution.py:351
  354.5 9.0 %collective-permute-start.35 = (bf16[2,192,384]{2,1,0:T(8,128)(2,1)S(1)}, bf16[2,192,384]{2,1,0:T(8,128)(2,1)S(1)}, u32[]{:S(2)}, u32[]{:S(2)}) collective-permute-start(bf16[2,192,384]{2,1,0:T(8,128)(2,1)S(1)} %dynamic-slice_bitcast_fusion.8), channel_id=1, source_target_pairs={{0,2},{2,0},{4,6},{6,4},{8,10},{10,8},{12,14},{14,12},{16,18},{18,... | collective-permute-start | bytes 884744 | tf_op jit(solution)/shard_map/ppermute | solution.py:351
  362.7 14.4 %collective-permute-start.14 = (bf16[2,2,240,384]{3,2,1,0:T(8,128)(2,1)S(1)}, bf16[2,2,240,384]{3,2,1,0:T(8,128)(2,1)S(1)}, u32[]{:S(2)}, u32[]{:S(2)}) collective-permute-start(bf16[2,2,240,384]{3,2,1,0:T(8,128)(2,1)S(1)} %dynamic-slice_bitcast_fusion.1), channel_id=1, source_target_pairs={{0,2},{2,0},{4,6},{6,4},{8,10},{10,8},{12,14},{14,12},{16,18},{18,... | collective-permute-start | bytes 2211848 | tf_op jit(solution)/shard_map/ppermute | solution.py:351
  363.5 14.1 %collective-permute-start.40 = (bf16[2,48,1536]{2,1,0:T(8,128)(2,1)S(1)}, bf16[2,48,1536]{2,1,0:T(8,128)(2,1)S(1)}, u32[]{:S(2)}, u32[]{:S(2)}) collective-permute-start(bf16[2,48,1536]{2,1,0:T(8,128)(2,1)S(1)} %dynamic-slice_bitcast_fusion.7), channel_id=1, source_target_pairs={{0,8},{2,10},{4,12},{6,14},{8,0},{10,2},{12,4},{14,6},{16,24},{18,... | collective-permute-start | bytes 884744 | tf_op jit(solution)/shard_map/ppermute | solution.py:351
  377.1 26.4 %collective-permute-start.36 = (bf16[192,384]{1,0:T(8,128)(2,1)S(1)}, bf16[192,384]{1,0:T(8,128)(2,1)S(1)}, u32[]{:S(2)}, u32[]{:S(2)}) collective-permute-start(bf16[192,384]{1,0:T(8,128)(2,1)S(1)} %dynamic-slice_bitcast_fusion.14), channel_id=1, source_target_pairs={{0,16},{2,18},{4,20},{6,22},{8,24},{10,26},{12,28},{14,30},{16,0},... | collective-permute-start | bytes 442376 | tf_op jit(solution)/shard_map/ppermute | solution.py:351
  377.6 7.6 %collective-permute-start.15 = (bf16[2,240,384]{2,1,0:T(8,128)(2,1)S(1)}, bf16[2,240,384]{2,1,0:T(8,128)(2,1)S(1)}, u32[]{:S(2)}, u32[]{:S(2)}) collective-permute-start(bf16[2,240,384]{2,1,0:T(8,128)(2,1)S(1)} %dynamic-slice_bitcast_fusion.5), channel_id=1, source_target_pairs={{0,4},{2,6},{4,0},{6,2},{8,12},{10,14},{12,8},{14,10},{16,20},{18,... | collective-permute-start | bytes 1105928 | tf_op jit(solution)/shard_map/ppermute | solution.py:351
  385.1 9.7 %collective-permute-start.41 = (bf16[48,1536]{1,0:T(8,128)(2,1)S(1)}, bf16[48,1536]{1,0:T(8,128)(2,1)S(1)}, u32[]{:S(2)}, u32[]{:S(2)}) collective-permute-start(bf16[48,1536]{1,0:T(8,128)(2,1)S(1)} %dynamic-slice_bitcast_fusion.13), channel_id=1, source_target_pairs={{0,16},{2,18},{4,20},{6,22},{8,24},{10,26},{12,28},{14,30},{16,0},... | collective-permute-start | bytes 442376 | tf_op jit(solution)/shard_map/ppermute | solution.py:351
  394.8 8.4 %collective-permute-start.16 = (bf16[240,384]{1,0:T(8,128)(2,1)S(1)}, bf16[240,384]{1,0:T(8,128)(2,1)S(1)}, u32[]{:S(2)}, u32[]{:S(2)}) collective-permute-start(bf16[240,384]{1,0:T(8,128)(2,1)S(1)} %dynamic-slice_bitcast_fusion.11), channel_id=1, source_target_pairs={{0,16},{2,18},{4,20},{6,22},{8,24},{10,26},{12,28},{14,30},{16,0},... | collective-permute-start | bytes 552968 | tf_op jit(solution)/shard_map/ppermute | solution.py:351
  403.6 2.3 collective-permute-start.42
  (44 other events, 175.6 us)

commit v2 on v1

v2 whole, which is shorter than its diff:
```python
import functools

import jax
import jax.numpy as jnp
from jax import lax
from jax.experimental import pallas as pl
from jax.experimental.pallas import tpu as pltpu
from jax.sharding import PartitionSpec as P

D = 768
HEADS = 12
HEAD = 64
LAT = 8
FACTOR = HEAD ** (-0.5)
HL = HEADS * LAT
BF = jnp.bfloat16
F32 = jnp.float32


def narrow(tensor):
    return tensor.astype(BF)


def mm(left, right):
    return lax.dot_general(left, right, (((1,), (0,)), ((), ())), preferred_element_type=F32)


def mm_tn(left, right):
    return lax.dot_general(left, right, (((0,), (0,)), ((), ())), preferred_element_type=F32)


def mm_nt(left, right):
    return lax.dot_general(left, right, (((1,), (1,)), ((), ())), preferred_element_type=F32)


def norm_parts(tensor):
    center = tensor - jnp.mean(tensor, axis=-1, keepdims=True)
    spread = jnp.mean(center * center, axis=-1, keepdims=True)
    inverse = lax.rsqrt(spread + 1e-06)
    return center * inverse, inverse


def norm_forward(tensor, gain, shift):
    unit, _ = norm_parts(tensor)
    return unit * gain + shift


def norm_back(unit, inverse, gain, upstream):
    scaled = upstream * gain
    return inverse * (
        scaled
        - jnp.mean(scaled, axis=-1, keepdims=True)
        - unit * jnp.mean(scaled * unit, axis=-1, keepdims=True)
    )


def fold_rows(tensor):
    rows, cols = tensor.shape
    return jnp.sum(tensor.reshape(rows // 8, 8, cols), axis=0)


def head_mask():
    head = lax.broadcasted_iota(jnp.int32, (HEADS, 1, D), 0)
    feature = lax.broadcasted_iota(jnp.int32, (HEADS, 1, D), 2)
    return (feature >= head * HEAD) & (feature < head * HEAD + HEAD)


def expand(rows):
    count = rows.shape[0]
    return narrow(jnp.where(head_mask(), rows[None], 0.0).reshape(HEADS * count, D))


def collapse(rows):
    count = rows.shape[0] // HEADS
    return jnp.sum(jnp.where(head_mask(), rows.reshape(HEADS, count, D), 0.0), axis=0)


def whole(shape):
    return pl.BlockSpec(shape, lambda *_: (0,) * len(shape), pipeline_mode=pl.Buffered(1))


def rows_of(shape):
    return pl.BlockSpec(shape, lambda g: (g,) + (0,) * (len(shape) - 1))


def one_of(index):
    return pl.BlockSpec(
        (None, D, D), lambda *_: (index, 0, 0), pipeline_mode=pl.Buffered(1)
    )


def shaped(shape, dtype):
    return jax.ShapeDtypeStruct(shape, dtype)


def in_hbm(tensor):
    return pltpu.with_memory_space_constraint(tensor, pltpu.HBM)


def image_marks(image_ref, places_ref, shape, axis, rows):
    index = lax.broadcasted_iota(jnp.int32, shape, axis)
    marks = jnp.zeros(shape, jnp.int32)
    for group in range(shape[axis] // rows):
        inside = (index >= group * rows) & (index < (group + 1) * rows)
        marks = jnp.where(inside, image_ref[0, places_ref[group]], marks)
    return marks


def gathered(refs):
    pieces = [ref[...] for ref in refs]
    return jnp.concatenate([piece.reshape(-1, piece.shape[-1]) for piece in pieces], 0)


def call(body, grid, in_specs, out_specs, out_shape, flops, moved, scratch=(), vmem=20):
    return pl.pallas_call(
        body,
        grid=grid,
        in_specs=in_specs,
        out_specs=out_specs,
        out_shape=out_shape,
        scratch_shapes=scratch,
        compiler_params=pltpu.CompilerParams(
            vmem_limit_bytes=vmem << 20, dimension_semantics=("arbitrary",) * len(grid)
        ),
        cost_estimate=pl.CostEstimate(
            flops=int(flops), bytes_accessed=int(moved), transcendentals=0
        ),
    )


def read_forward_kernel(
    x_ref, z_ref, norm_ref, in_ref, out_w_ref,
    a1_ref, q1_ref, b1_ref, k1_ref, v1_ref, p1_ref, o1_ref, z1_ref, a2_ref,
    mix_ref,
):
    step = pl.program_id(0)
    last = pl.num_programs(0) - 1

    @pl.when(step == 0)
    def _():
        a1 = narrow(norm_forward(z_ref[...].astype(F32), norm_ref[0:1], norm_ref[5:6]))
        a1_ref[...] = a1
        q1_ref[...] = narrow(mm(a1, in_ref[0])).astype(F32)

    b1 = narrow(norm_forward(x_ref[...].astype(F32), norm_ref[1:2], norm_ref[6:7]))
    b1_ref[...] = b1
    k1 = narrow(mm(b1, in_ref[1]))
    v1 = narrow(mm(b1, in_ref[2]))
    k1_ref[...] = k1
    v1_ref[...] = v1
    own = pl.ds(pl.multiple_of(step * LAT, LAT), LAT)
    scores = mm_nt(expand(q1_ref[own, :]), k1) * FACTOR
    powers = jnp.exp(scores - jnp.max(scores, axis=-1, keepdims=True))
    shares = powers / jnp.sum(powers, axis=-1, keepdims=True)
    p1_ref[...] = shares
    mix_ref[own, :] = collapse(mm(narrow(shares), v1))

    @pl.when(step == last)
    def _():
        o1 = narrow(mix_ref[...])
        o1_ref[...] = o1
        z1 = z_ref[...].astype(F32) + mm(o1, out_w_ref[...])
        z1_ref[...] = z1
        a2_ref[...] = narrow(norm_forward(z1, norm_ref[2:3], norm_ref[7:8]))


def self_forward_kernel(
    image_ref, places_ref, own_at_ref, piece0_ref, piece1_ref, piece2_ref, piece3_ref,
    a2_ref, z1_ref, norm_ref, in_ref, out_w_ref, wk_ref, wv_ref,
    all_ref, allowed_ref, k2_ref, v2_ref, p2_ref, l2_ref, o2_ref, z2_ref, out_ref, b3_ref, k3_ref, v3_ref,
):
    everyone = gathered((piece0_ref, piece1_ref, piece2_ref, piece3_ref))
    all_ref[...] = everyone
    k2 = narrow(mm(everyone, in_ref[1]))
    v2 = narrow(mm(everyone, in_ref[2]))
    k2_ref[...] = k2
    v2_ref[...] = v2
    q2 = narrow(mm(a2_ref[...], in_ref[0])).astype(F32)
    scores = mm_nt(expand(q2), k2) * FACTOR
    total, count = everyone.shape[0], q2.shape[0]
    owners = image_marks(image_ref, places_ref, (1, total), 1, LAT)
    own = jnp.concatenate([image_marks(image_ref, own_at_ref, (count, 1), 0, LAT)] * HEADS, 0)
    allowed = own == owners
    allowed_ref[...] = jnp.where(allowed, 1.0, 0.0)
    scores = jnp.where(allowed, scores, -1e30)
    highest = jnp.max(scores, axis=-1, keepdims=True)
    powers = jnp.exp(scores - highest)
    totals = jnp.sum(powers, axis=-1, keepdims=True)
    shares = powers / totals
    p2_ref[...] = shares
    l2_ref[...] = highest + jnp.log(totals)
    o2 = narrow(collapse(mm(narrow(shares), v2)))
    o2_ref[...] = o2
    z2 = z1_ref[...] + mm(o2, out_w_ref[...])
    z2_ref[...] = z2
    out_ref[...] = narrow(z2)
    b3 = narrow(norm_forward(z2, norm_ref[3:4], norm_ref[8:9]))
    b3_ref[...] = b3
    k3_ref[...] = narrow(mm(b3, wk_ref[...])).astype(F32)
    v3_ref[...] = narrow(mm(b3, wv_ref[...])).astype(F32)


ROOT_HALF = 0.7071067811865476
DENSITY = 0.3989422804014327


def patch_kernel(
    chunk, x_ref, q3_ref, cot_ref, k3_ref, v3_ref, norm_ref, wo_ref, up_ref, down_ref,
    out_ref, he_ref, gd_ref, o3_ref, e3_ref, dq3_ref, dx1_ref, dk3_ref, dv3_ref,
    gain_ref, shift_ref,
):
    step = pl.program_id(0)
    own = pl.ds(pl.multiple_of(step * LAT, LAT), LAT)
    kx = expand(k3_ref[own, :])
    vx = expand(v3_ref[own, :])
    q3 = q3_ref[...]
    tokens = q3.shape[0]
    scores = (mm_nt(kx, q3) * FACTOR).reshape(HEADS, LAT, tokens)
    powers = jnp.exp(scores - jnp.max(scores, axis=1, keepdims=True))
    shares = powers / jnp.sum(powers, axis=1, keepdims=True)
    shares_low = narrow(shares.reshape(HL, tokens))
    o3 = narrow(mm_tn(shares_low, vx))
    o3_ref[...] = o3
    x1 = x_ref[...].astype(F32) + mm(o3, wo_ref[...])
    unit, inverse = norm_parts(x1)
    gain = norm_ref[4:5]
    h = narrow(unit * gain + norm_ref[9:10])
    e4 = cot_ref[...]
    he_ref[0] = h
    he_ref[1] = e4
    x2 = x1
    dh = jnp.zeros((tokens, D), F32)
    hidden = up_ref.shape[1]
    for start in range(0, hidden, chunk):
        part = slice(start, start + chunk)
        u = mm(h, up_ref[:, part])
        cdf = 0.5 + 0.5 * lax.erf(u * ROOT_HALF)
        g = narrow(u * cdf)
        gd_ref[1, :, part] = g
        x2 = x2 + mm(g, down_ref[part, :])
        slope = cdf + u * (jnp.exp(-0.5 * u * u) * DENSITY)
        du = narrow(mm_nt(e4, down_ref[part, :]) * slope)
        gd_ref[0, :, part] = du
        dh = dh + mm_nt(du, up_ref[:, part])
    out_ref[...] = narrow(x2)

    @pl.when(step == 0)
    def _():
        gain_ref[...] = jnp.zeros_like(gain_ref)
        shift_ref[...] = jnp.zeros_like(shift_ref)

    gain_ref[...] += fold_rows(dh * unit)
    shift_ref[...] += fold_rows(dh)
    dx1 = e4.astype(F32) + norm_back(unit, inverse, gain, dh)
    dx1_ref[...] = dx1
    e3 = narrow(dx1)
    e3_ref[...] = e3
    do3 = narrow(mm_nt(e3, wo_ref[...]))
    dshares = mm_nt(vx, do3).reshape(HEADS, LAT, tokens)
    inner = jnp.sum(shares * dshares, axis=1, keepdims=True)
    dscores = narrow((shares * (dshares - inner)).reshape(HL, tokens))
    dq3_ref[...] = narrow(mm_tn(dscores, kx) * FACTOR)
    dv3_ref[...] = collapse(mm(shares_low, do3))
    dk3_ref[...] = collapse(mm(dscores, q3)) * FACTOR


STAT = 2 * HEADS


def latent_back_kernel(
    dk3_ref, dv3_ref, z2_ref, cot_ref, k2_ref, v2_ref, p2_ref, l2_ref, norm_ref, wk_ref, wv_ref, out_w_ref,
    dk3_low_ref, dv3_low_ref, dz2_ref, e2_ref, send_ref, dq2_ref, gain_ref, shift_ref,
):
    dk3 = narrow(dk3_ref[...])
    dv3 = narrow(dv3_ref[...])
    dk3_low_ref[...] = dk3
    dv3_low_ref[...] = dv3
    upstream = mm_nt(dk3, wk_ref[...]) + mm_nt(dv3, wv_ref[...])
    unit, inverse = norm_parts(z2_ref[...])
    gain_ref[...] = fold_rows(upstream * unit)
    shift_ref[...] = fold_rows(upstream)
    dz2 = cot_ref[...].astype(F32) + norm_back(unit, inverse, norm_ref[3:4], upstream)
    dz2_ref[...] = dz2
    e2 = narrow(dz2)
    e2_ref[...] = e2
    do2 = narrow(mm_nt(e2, out_w_ref[...]))
    send_ref[:, :D] = do2
    shares = p2_ref[...]
    dshares = mm_nt(expand(do2.astype(F32)), v2_ref[...])
    inner = jnp.sum(shares * dshares, axis=-1, keepdims=True)
    count = do2.shape[0]
    lane = lax.broadcasted_iota(jnp.int32, (count, 128), 1)
    stats = jnp.zeros((count, 128), F32)
    for slot, columns in ((0, l2_ref[...]), (HEADS, inner)):
        for head in range(HEADS):
            place = slot + head
            chosen = (lane == place) | (lane == place + STAT) | (lane == place + 2 * STAT)
            stats = jnp.where(chosen, columns[head * count : (head + 1) * count], stats)
    top = narrow(stats)
    rest = stats - top.astype(F32)
    middle = narrow(rest)
    bottom = narrow(rest - middle.astype(F32))
    send_ref[:, D:] = narrow(
        jnp.where(lane < STAT, top.astype(F32), jnp.where(lane < 2 * STAT, middle.astype(F32), bottom.astype(F32)))
    )
    dscores = narrow(shares * (dshares - inner))
    dq2_ref[...] = narrow(collapse(mm(dscores, k2_ref[...])) * FACTOR)


def spread_stat(stats, slot, count):
    shape = (HEADS * count, 128)
    place = lax.broadcasted_iota(jnp.int32, shape, 1)
    column = lax.broadcasted_iota(jnp.int32, shape, 0)
    chosen = jnp.zeros(shape, jnp.bool_)
    for term in range(3):
        head = place - (slot + term * STAT)
        chosen |= (head >= 0) & (head < HEADS) & (column >= head * count) & (column < (head + 1) * count)
    return mm_nt(narrow(jnp.where(chosen, 1.0, 0.0)), stats)


def put_units(core_ref, other_ref, mine_ref, units):
    count = mine_ref.shape[0]
    rows = D // count
    for core in range(2):
        @pl.when(core_ref[0] == core)
        def _():
            for ref, pairs in ((other_ref, units[1 - core]), (mine_ref, units[core])):
                for index, (left, right) in enumerate(pairs):
                    grad = narrow(mm_tn(left[...], right[...]).reshape(count, rows, D))
                    ref[:, index * rows : (index + 1) * rows, :] = grad


def early_kernel(
    core_ref, o3_ref, e3_ref, b1_ref, dq3_ref, b3_ref, dk3_ref, dv3_ref, other_ref, mine_ref
):
    put_units(core_ref, other_ref, mine_ref,
              [[(o3_ref, e3_ref), (b3_ref, dk3_ref)], [(b1_ref, dq3_ref), (b3_ref, dv3_ref)]])


def late_kernel(
    core_ref, b1_ref, dk1_ref, dv1_ref, a1_ref, dq1_ref, o1_ref, e1_ref, a2_ref, dq2_ref, o2_ref, e2_ref,
    dk2_ref, dv2_ref, other_ref, mine_ref,
):
    put_units(core_ref, other_ref, mine_ref,
              [[(b1_ref, dk1_ref), (a1_ref, dq1_ref), (a2_ref, dq2_ref), (o2_ref, e2_ref)],
               [(b1_ref, dv1_ref), (o1_ref, e1_ref), (a2_ref, dk2_ref), (a2_ref, dv2_ref)]])


def stage_kernel(parts, pick_ref, *refs):
    for index in range(parts):
        keep_ref, got_ref = refs[2 * index : 2 * index + 2]
        send_ref, stay_ref = refs[2 * parts + 2 * index : 2 * parts + 2 * index + 2]
        mine = pick_ref[index]
        send_ref[...] = narrow(keep_ref[1 - mine].astype(F32) + got_ref[1 - mine].astype(F32))
        stay_ref[...] = narrow(keep_ref[mine].astype(F32) + got_ref[mine].astype(F32))


def last_stage_kernel(parts, pick_ref, *refs):
    send_ref, stay_ref = refs[2 * parts :]
    mine = pick_ref[0]
    start = 0
    for index in range(parts):
        keep_ref, got_ref = refs[2 * index : 2 * index + 2]
        rows = keep_ref.shape[1]
        span = slice(start, start + rows)
        send_ref[span] = narrow(keep_ref[1 - mine].astype(F32) + got_ref[1 - mine].astype(F32))
        stay_ref[span] = narrow(keep_ref[mine].astype(F32) + got_ref[mine].astype(F32))
        start += rows


def sum_kernel(keep_ref, got_ref, out_ref):
    out_ref[...] = narrow(keep_ref[...].astype(F32) + got_ref[...].astype(F32))


def early_out_kernel(core_ref, mine_ref, partner_ref, up_ref, down_ref, wo_ref, in_ref):
    rows = wo_ref.shape[0]
    feed_rows = down_ref.shape[0]
    for core in range(2):
        @pl.when(core_ref[0] == core)
        def _():
            zero, one = (mine_ref, partner_ref) if core == 0 else (partner_ref, mine_ref)
            for index in range(feed_rows // rows):
                up_ref[:, index * D : (index + 1) * D] = zero[index * rows : (index + 1) * rows].astype(F32)
            down_ref[...] = one[:feed_rows].astype(F32)
            wo_ref[...] = zero[feed_rows : feed_rows + rows].astype(F32)
            in_ref[0] = one[feed_rows : feed_rows + rows].astype(F32)
            in_ref[1] = zero[feed_rows + rows :].astype(F32)
            in_ref[2] = one[feed_rows + rows :].astype(F32)


def late_out_kernel(core_ref, mine_ref, partner_ref, read_in_ref, read_out_ref, self_in_ref, self_out_ref):
    rows = read_out_ref.shape[0]
    for core in range(2):
        @pl.when(core_ref[0] == core)
        def _():
            zero, one = (mine_ref, partner_ref) if core == 0 else (partner_ref, mine_ref)

            def unit(ref, index):
                return ref[index * rows : (index + 1) * rows].astype(F32)

            read_in_ref[0] = unit(zero, 1)
            read_in_ref[1] = unit(zero, 0)
            read_in_ref[2] = unit(one, 0)
            read_out_ref[...] = unit(one, 1)
            self_in_ref[0] = unit(zero, 2)
            self_in_ref[1] = unit(one, 2)
            self_in_ref[2] = unit(one, 3)
            self_out_ref[...] = unit(zero, 3)


def feed_kernel(which_ref, gd_ref, he_ref, out_ref):
    part = pl.program_id(0)
    count, rows, _ = out_ref.shape
    slab = D // count

    @pl.when(which_ref[0] == 0)
    def _():
        grad = narrow(mm_tn(he_ref[...], gd_ref[...]).reshape(count, slab, D))
        out_ref[:, pl.ds(pl.multiple_of(part * slab, 8), slab), :] = grad

    @pl.when(which_ref[0] == 1)
    def _():
        grad = narrow(mm_tn(gd_ref[...], he_ref[...]).reshape(D // rows, rows, D))
        out_ref[pl.ds(part * (D // rows), D // rows)] = grad


def inner_back_kernel(
    piece0_ref, piece1_ref, piece2_ref, piece3_ref, q_all_ref, allowed_ref, k2_ref, v2_ref,
    dq2_ref, z1_ref, dz2_ref, norm_ref, in_ref, out_w_ref, q1_ref, p1_ref, k1_ref, v1_ref,
    dk2_ref, dv2_ref, dz1_ref, e1_ref, gain_ref, shift_ref, dq1_ref, dk1_ref, dv1_ref,
    do1_ref,
):
    step = pl.program_id(0)

    @pl.when(step == 0)
    def _():
        count = dq2_ref.shape[0]
        half, total = count // 2, q_all_ref.shape[0]

        def own_rows(ref):
            return jnp.concatenate([ref[:half], ref[total // 2 : total // 2 + half]], 0).astype(F32)

        q_all = q_all_ref[...]
        spread = gathered((piece0_ref, piece1_ref, piece2_ref, piece3_ref))
        do_all = spread[:, :D]
        stats = spread[:, D:]
        scores = mm_nt(expand(own_rows(k2_ref)), q_all) * FACTOR
        allowed = allowed_ref[...] > 0.5
        log_total = spread_stat(stats, 0, count)
        shares = jnp.where(allowed, jnp.exp(jnp.where(allowed, scores - log_total, 0.0)), 0.0)
        dv2 = narrow(collapse(mm(narrow(shares), do_all)))
        dshares = mm_nt(expand(own_rows(v2_ref)), do_all)
        dscores = narrow(shares * (dshares - spread_stat(stats, HEADS, count)))
        dk2 = narrow(collapse(mm(dscores, q_all)) * FACTOR)
        dk2_ref[...] = dk2
        dv2_ref[...] = dv2
        upstream = mm_nt(dq2_ref[...], in_ref[0]) + mm_nt(dk2, in_ref[1]) + mm_nt(dv2, in_ref[2])
        unit, inverse = norm_parts(z1_ref[...])
        gain_ref[...] = fold_rows(upstream * unit)
        shift_ref[...] = fold_rows(upstream)
        dz1 = dz2_ref[...] + norm_back(unit, inverse, norm_ref[2:3], upstream)
        dz1_ref[...] = dz1
        e1 = narrow(dz1)
        e1_ref[...] = e1
        do1_ref[...] = narrow(mm_nt(e1, out_w_ref[...])).astype(F32)

    own = pl.ds(pl.multiple_of(step * LAT, LAT), LAT)
    qx = expand(q1_ref[own, :])
    dox = expand(do1_ref[own, :])
    shares = p1_ref[...]
    dshares = mm_nt(dox, v1_ref[...])
    inner = jnp.sum(shares * dshares, axis=-1, keepdims=True)
    dscores = narrow(shares * (dshares - inner))
    dv1_ref[...] = narrow(mm_tn(narrow(shares), dox))
    dk1_ref[...] = narrow(mm_tn(dscores, qx) * FACTOR)
    dq1_ref[own, :] = collapse(mm(dscores, k1_ref[...])) * FACTOR


def input_back_kernel(
    x_ref, dx1_ref, dq3_ref, dk1_ref, dv1_ref, z_ref, dz1_ref, dq1_ref, norm_ref, in_ref, wq_ref,
    gain2_ref, shift2_ref, gain3_ref, shift3_ref, gain4_ref, shift4_ref,
    dx_ref, dz_ref, sums_ref, gain_ref, shift_ref,
):
    step = pl.program_id(0)

    def total(tensor):
        return jnp.sum(tensor, axis=0, keepdims=True)

    @pl.when(step == 0)
    def _():
        gain_ref[...] = jnp.zeros_like(gain_ref)
        shift_ref[...] = jnp.zeros_like(shift_ref)
        upstream = mm_nt(narrow(dq1_ref[...]), in_ref[0])
        unit, inverse = norm_parts(z_ref[...].astype(F32))
        sums_ref[...] = jnp.zeros_like(sums_ref)
        sums_ref[0:1] = total(upstream * unit)
        sums_ref[5:6] = total(upstream)
        for index, ref in enumerate((gain2_ref, gain3_ref, gain4_ref)):
            sums_ref[2 + index : 3 + index] = total(ref[...])
        for index, ref in enumerate((shift2_ref, shift3_ref, shift4_ref)):
            sums_ref[7 + index : 8 + index] = total(ref[...])
        dz_ref[...] = narrow(dz1_ref[...] + norm_back(unit, inverse, norm_ref[0:1], upstream))

    upstream = (
        mm_nt(dq3_ref[...], wq_ref[...])
        + mm_nt(dk1_ref[...], in_ref[1])
        + mm_nt(dv1_ref[...], in_ref[2])
    )
    unit, inverse = norm_parts(x_ref[...].astype(F32))
    gain_ref[...] += fold_rows(upstream * unit)
    shift_ref[...] += fold_rows(upstream)
    dx_ref[...] = narrow(dx1_ref[...] + norm_back(unit, inverse, norm_ref[1:2], upstream))

    @pl.when(step == pl.num_programs(0) - 1)
    def _():
        sums_ref[1:2] = total(gain_ref[...])
        sums_ref[6:7] = total(shift_ref[...])


def bits_of(count):
    bits = count.bit_length() - 1
    if 1 << bits != count:
        raise ValueError("axis size")
    return bits


def swap(tensor, axis, bit, count):
    return lax.ppermute(tensor, axis, [(i, i ^ (1 << bit)) for i in range(count)])


def own_bit(bit, axis="blk"):
    return (lax.axis_index(axis) >> bit) & 1


def gather_rows(tensor, count, line, fill):
    bits = bits_of(count)
    step = 0
    for bit in range(bits - 1, 1, -1):
        other = swap(line.gate(tensor), "blk", bit, count)
        beside = fill(step)
        line.note((other, beside) if beside is not None else other)
        tensor = jnp.stack([tensor, other], step)
        step += 1
    rows = tensor.shape[-2]
    left, right = tensor[..., : rows // 2, :], tensor[..., rows // 2 :, :]
    for bit_left, bit_right in ((1, 0), (0, 1)):
        got_left = swap(line.gate(left), "blk", bit_left, count)
        got_right = swap(line.gate(right), "blk", bit_right, count)
        beside = fill(step)
        line.note((got_left, got_right) + (() if beside is None else (beside,)))
        if bit_left == 1:
            left = jnp.stack([left, got_left], step)
            right = jnp.stack([right, got_right], step)
        step += 1
    return [piece.reshape(count // 2, -1, piece.shape[-1]) for piece in (left, got_left, right, got_right)]


def gather_places(count, groups):
    bits = bits_of(count)

    def spans(order):
        distances = [0]
        for bit in order:
            distances = [d | (on << bit) for d in distances for on in (0, 1)]
        return distances

    high = list(range(bits - 1, 1, -1))
    distance, place = [], []
    half = groups // 2
    for order, last, first in ((high + [1], 0, 0), (high + [0], 1, half)):
        for on in (0, 1):
            for d in spans(order):
                for group in range(first, first + half):
                    distance.append(d | (on << last))
                    place.append(group)
    return distance, place


def scatter_orders(bits):
    if bits < 3:
        return [list(range(bits))] * 3
    low, high = [0, 1], list(range(2, bits))
    return [
        low + high,
        [1] + high[:1] + [0] + high[1:],
        high[:1] + low + high[1:],
    ]


class Line:
    def __init__(self):
        self.last = None

    def gate(self, tensors):
        if self.last is None:
            return tensors
        tensors, _ = lax.optimization_barrier((tensors, self.last))
        return tensors

    def note(self, tensor):
        self.last = tensor


class Scatter:
    def __init__(self, line, count, orders):
        self.line, self.count, self.orders = line, count, orders
        self.left = [list(range(bits_of(count) - 1, -1, -1)) for _ in orders]
        self.step = 0

    def begin(self, parts):
        self.parts = parts
        self.send()

    def send(self):
        if self.step == len(self.orders[0]) - 1 and len({order[-1] for order in self.orders}) == 1:
            self.send_last()
            return
        lead = (self.count >> self.step) // 2
        picks, in_specs, operands, out_specs, out_shape, bits = [], [], [], [], [], []
        for (kept, got, rows, block), left, order in zip(self.parts, self.left, self.orders):
            bit = order[self.step]
            place = left.index(bit)
            left.pop(place)
            inner = lead >> place
            picks.append(own_bit(bit))
            bits.append(bit)
            spec = pl.BlockSpec(
                (None, 2, None, rows, D),
                lambda i, inner=inner, block=block: (i // inner, 0, i % inner, block, 0),
            )
            in_specs += [spec, spec]
            operands += [t.reshape(lead // inner, 2, inner, -1, D) for t in (kept, got)]
            out_specs += [pl.BlockSpec((None, rows, D), lambda i: (i, 0, 0))] * 2
            out_shape += [shaped((lead, rows, D), BF)] * 2
        moved = sum(3 * 4 * lead * part[2] * D for part in self.parts)
        out = call(
            functools.partial(stage_kernel, len(self.parts)), (lead,),
            [pl.BlockSpec(memory_space=pltpu.SMEM)] + in_specs, out_specs, out_shape, 0, moved, vmem=10,
        )(*self.line.gate((jnp.stack(picks).astype(jnp.int32), *operands)))
        self.line.note(out)
        got = [swap(sent, "blk", bit, self.count) for sent, bit in zip(out[::2], bits)]
        self.parts = [
            (stay, arrived, part[2], 0) for stay, arrived, part in zip(out[1::2], got, self.parts)
        ]
        self.step += 1

    def send_last(self):
        bit = self.orders[0][-1]
        rows = [part[2] for part in self.parts]
        operands = [t for kept, got, _, _ in self.parts for t in (kept, got)]
        shape = (sum(rows), D)
        send, stay = call(
            functools.partial(last_stage_kernel, len(rows)), (1,),
            [pl.BlockSpec(memory_space=pltpu.SMEM)] + [whole(t.shape) for t in operands], [whole(shape)] * 2,
            [shaped(shape, BF)] * 2, 0, 12 * shape[0] * D,
        )(*self.line.gate((own_bit(bit).reshape(1).astype(jnp.int32), *operands)))
        self.line.note(stay)
        self.parts = [(stay, swap(send, "blk", bit, self.count), shape[0], 0)]
        self.step += 1

    def flying(self):
        return [part[1] for part in self.parts]

    def result(self):
        ((stay, got, rows, _),) = self.parts
        return call(
            sum_kernel, (1,), [whole((rows, D))] * 2, whole((rows, D)), shaped((rows, D), BF), 0, 6 * rows * D,
        )(*self.line.gate((stay, got)))


def make_body(n_blk, n_rep):
    rep_bits = bits_of(n_rep)
    orders = scatter_orders(bits_of(n_blk))
    rows = D // n_blk

    def body(
        patches, latents, norm_gain, norm_bias, read_in, read_out, self_in, self_out,
        write_in, write_out, feed_up, feed_down, group_image, cot_patches, cot_latents,
    ):
        x, z, cot, cot_z = patches[0], latents[0], cot_patches[0], cot_latents[0]
        tokens, lat = x.shape[0], z.shape[0]
        groups = lat // LAT
        size = tokens // groups
        total = lat * n_blk
        hidden = feed_up.shape[1]
        feed_rows = hidden // n_blk
        core = lax.axis_index("rep") & 1
        core_at = core.reshape(1).astype(jnp.int32)
        other_at = 1 - core_at
        norms = jnp.concatenate([norm_gain, norm_bias, jnp.zeros((6, D), BF)], 0).astype(F32)
        norm_spec = whole((16, D))
        square = whole((D, D))
        three = whole((3, D, D))
        lat_spec = whole((lat, D))
        fold_spec = whole((8, D))
        patch_spec = rows_of((size, D))
        smem = pl.BlockSpec(memory_space=pltpu.SMEM)
        share_spec = pl.BlockSpec((None, HL, size), lambda g: (g, 0, 0))
        grid = (groups,)
        unit_flops = 2 * tokens * D * D
        low_lat, full_lat, fold = shaped((lat, D), BF), shaped((lat, D), F32), shaped((8, D), F32)
        low_patch = shaped((tokens, D), BF)
        line = Line()

        a1, q1, b1, k1, v1, p1, o1, z1, a2 = call(
            read_forward_kernel, grid,
            [patch_spec, lat_spec, norm_spec, three, square],
            [lat_spec, lat_spec, patch_spec, patch_spec, patch_spec, share_spec, lat_spec, lat_spec, lat_spec],
            [low_lat, full_lat, low_patch, low_patch, low_patch, shaped((groups, HL, size), F32),
             low_lat, full_lat, low_lat],
            2 * unit_flops, 12 * tokens * D,
            [pltpu.VMEM((lat, D), F32)],
        )(in_hbm(x), z, norms, in_hbm(read_in), in_hbm(read_out))

        q3 = []

        def fill_first(step):
            if step == 0:
                q3.append(narrow(mm(b1, write_in[0])))
                return q3[0]
            return None

        pieces = gather_rows(a2, n_blk, line, fill_first)
        q3 = q3[0]

        me = lax.axis_index("blk")
        distance, place = gather_places(n_blk, groups)
        places = (me ^ jnp.array(distance, jnp.int32)) * groups + jnp.array(place, jnp.int32)
        own_at = me * groups + jnp.arange(groups, dtype=jnp.int32)
        piece_shape = (n_blk // 2, lat // 2)
        hl2 = HEADS * lat
        a2_all, allowed, k2, v2, p2, l2, o2, z2, out_latents, b3, k3, v3 = call(
            self_forward_kernel, (1,),
            [smem] * 3 + [whole(piece_shape + (D,))] * 4 + [lat_spec, lat_spec, norm_spec, three, square,
             one_of(1), one_of(2)],
            [whole((total, D)), whole((hl2, total)), whole((total, D)), whole((total, D)), whole((hl2, total)),
             whole((hl2, 1))] + [lat_spec] * 6,
            [shaped((total, D), BF), shaped((hl2, total), F32), shaped((total, D), BF), shaped((total, D), BF),
             shaped((hl2, total), F32), shaped((hl2, 1), F32),
             low_lat, full_lat, low_lat, low_lat, full_lat, full_lat],
            unit_flops * 2, 10 * D * D * 2,
        )(group_image, places, own_at, *pieces, a2, z1, norms, self_in, self_out, write_in, write_in)

        pair_spec = pl.BlockSpec((2, size, D), lambda g: (0, g, 0))
        out_patches, he, gd, o3, e3, dq3, dx1, dk3, dv3, gain4, shift4 = call(
            functools.partial(patch_kernel, D), grid,
            [patch_spec, patch_spec, patch_spec, lat_spec, lat_spec, norm_spec, square,
             whole((D, hidden)), whole((hidden, D))],
            [patch_spec, pair_spec, pl.BlockSpec((2, size, hidden), lambda g: (0, g, 0)), patch_spec, patch_spec,
             patch_spec, patch_spec, rows_of((LAT, D)), rows_of((LAT, D)), fold_spec, fold_spec],
            [low_patch, shaped((2, tokens, D), BF), shaped((2, tokens, hidden), BF),
             low_patch, low_patch, low_patch, shaped((tokens, D), F32), full_lat, full_lat, fold, fold],
            unit_flops * 20, 40 * tokens * D, vmem=40,
        )(in_hbm(x), in_hbm(q3), in_hbm(cot), k3, v3, norms, write_out, feed_up, feed_down)

        width = D + 128
        dk3, dv3, dz2, e2, payload, dq2, gain3, shift3 = call(
            latent_back_kernel, (1,),
            [lat_spec] * 4 + [whole((total, D))] * 2
            + [whole((hl2, total)), whole((hl2, 1)), norm_spec, one_of(1), one_of(2), square],
            [lat_spec] * 4 + [whole((lat, width)), lat_spec, fold_spec, fold_spec],
            [low_lat, low_lat, full_lat, low_lat, shaped((lat, width), BF), low_lat, fold, fold],
            unit_flops, 10 * D * D,
        )(dk3, dv3, z2, cot_z, k2, v2, p2, l2, norms, write_in, write_in, self_out)
        line.note(payload)

        def feed_grad(which):
            return pl.pallas_call(
                feed_kernel,
                grid_spec=pltpu.PrefetchScalarGridSpec(
                    num_scalar_prefetch=1,
                    grid=(hidden // D,),
                    in_specs=[
                        pl.BlockSpec((None, tokens, D), lambda j, w: (w[0], 0, j)),
                        pl.BlockSpec((None, tokens, D), lambda j, w: (w[0], 0, 0), pipeline_mode=pl.Buffered(1)),
                    ],
                    out_specs=pl.BlockSpec((n_blk, feed_rows, D), lambda j, w: (0, 0, 0), pipeline_mode=pl.Buffered(1)),
                ),
                out_shape=shaped((n_blk, feed_rows, D), BF),
                compiler_params=pltpu.CompilerParams(
                    vmem_limit_bytes=20 << 20, dimension_semantics=("arbitrary",)
                ),
                cost_estimate=pl.CostEstimate(
                    flops=unit_flops * 4, bytes_accessed=20 * tokens * D, transcendentals=0
                ),
            )(*line.gate((which, in_hbm(gd), in_hbm(he))))

        whole_patch = whole((tokens, D))

        def unit_grads(kernel, patch_sized, lat_sized, count):
            return call(
                kernel, (1,),
                [smem] + [whole_patch] * len(patch_sized) + [lat_spec] * len(lat_sized),
                [whole((n_blk, count * rows, D))] * 2, [shaped((n_blk, count * rows, D), BF)] * 2,
                unit_flops, 8 * tokens * D,
            )(*line.gate((core_at, *patch_sized, *lat_sized)))

        def core_swap(tensor):
            return swap(line.gate(tensor), "rep", 0, n_rep)

        early = {}
        first = Scatter(line, n_blk, orders)

        def fill_second(step):
            if step == 0:
                early["feed_other"] = feed_grad(other_at)
                return early["feed_other"]
            if step == 1:
                early["feed_got"] = core_swap(early["feed_other"])
                early["feed_mine"] = feed_grad(core_at)
                return early["feed_mine"], early["feed_got"]
            if step == 2:
                early["other"], early["mine"] = unit_grads(early_kernel, (o3, e3, b1, dq3), (b3, dk3, dv3), 2)
                return early["mine"]
            early["got"] = core_swap(early["other"])
            early["q2_all"] = narrow(mm(line.gate(a2_all), self_in[0]))
            return early["q2_all"], early["got"]

        spread_pieces = gather_rows(payload, n_blk, line, fill_second)
        half = feed_rows // 2
        first.begin([
            (early["feed_mine"], early["feed_got"], half, 0),
            (early["feed_mine"], early["feed_got"], half, 1),
            (early["mine"], early["got"], 2 * rows, 0),
        ])

        dk2, dv2, dz1, e1, gain2, shift2, dq1, dk1, dv1 = call(
            inner_back_kernel, grid,
            [whole(piece_shape + (width,))] * 4 + [whole((total, D)), whole((hl2, total))]
            + [whole((total, D))] * 2 + [lat_spec] * 3 + [norm_spec, three, square, lat_spec, share_spec]
            + [patch_spec] * 2,
            [lat_spec] * 4 + [fold_spec] * 2 + [lat_spec] + [patch_spec] * 2,
            [low_lat, low_lat, full_lat, low_lat, fold, fold, full_lat, low_patch, low_patch],
            2 * unit_flops, 10 * tokens * D,
            [pltpu.VMEM((lat, D), F32)],
        )(*line.gate((*spread_pieces, early["q2_all"], allowed, k2, v2,
                      dq2, z1, dz2, norms, self_in, read_out, q1, in_hbm(p1), in_hbm(k1), in_hbm(v1))))
        line.note((dk1, first.flying()))
        first.send()

        late_other, late_mine = unit_grads(
            late_kernel, (b1, dk1, dv1), (a1, narrow(dq1), o1, e1, a2, dq2, o2, e2, dk2, dv2), 4
        )
        line.note((late_mine, first.flying()))
        late_got = core_swap(late_other)
        first.send()

        dx, dz, norm_grads = call(
            input_back_kernel, grid,
            [patch_spec] * 5 + [lat_spec] * 3 + [norm_spec, three, one_of(0)] + [fold_spec] * 6,
            [patch_spec, lat_spec, norm_spec],
            [low_patch, low_lat, shaped((16, D), F32)],
            unit_flops * 3, 14 * tokens * D,
            [pltpu.VMEM((8, D), F32)] * 2,
        )(*line.gate((in_hbm(x), in_hbm(dx1), in_hbm(dq3), dk1, dv1, z, dz1, dq1, norms, read_in, write_in,
                      gain2, shift2, gain3, shift3, gain4, shift4)))
        norm_got = swap(norm_grads, "rep", 0, n_rep)
        line.note((dx, late_got, first.flying()))
        last = Scatter(line, n_blk, orders)
        last_rows = 4 * rows // 3
        last.begin([(late_mine, late_got, last_rows, i) for i in range(3)])
        first.send()
        norm_grads = norm_grads + norm_got
        for bit in range(1, rep_bits):
            norm_grads = norm_grads + swap(line.gate(norm_grads), "rep", bit, n_rep)
        bits = bits_of(n_blk)

        def finish(flat):
            for bit in range(1, rep_bits):
                flat = narrow(flat.astype(F32) + swap(flat, "rep", bit, n_rep).astype(F32))
            return flat, swap(flat, "rep", 0, n_rep)

        def outputs(kernel, flat, partner, shapes):
            return call(
                kernel, (1,), [smem, whole(flat.shape), whole(flat.shape)], [whole(t) for t in shapes],
                [shaped(t, F32) for t in shapes], 0, 12 * flat.shape[0] * D,
            )(*line.gate((core_at, flat, partner)))

        for step in range(bits):
            got = swap(line.gate(norm_grads), "blk", step, n_blk)
            if step == 0:
                line.note((last.flying(), first.flying(), got))
            elif step == 1:
                last.send()
                while first.step < bits:
                    line.note(first.flying())
                    first.send()
                flat, partner = finish(first.result())
                up, down, wo, write_in_grad = outputs(
                    early_out_kernel, flat, partner, [(rows, hidden), (feed_rows, D), (rows, D), (3, rows, D)]
                )
                line.note((last.flying(), got, up))
            else:
                if last.step < bits:
                    last.send()
                line.note((last.flying(), got))
            norm_grads = norm_grads + got
        while last.step < bits:
            last.send()
            line.note(last.flying())
        flat, partner = finish(last.result())
        read_in_grad, read_out_grad, self_in_grad, self_out_grad = outputs(
            late_out_kernel, flat, partner, [(3, rows, D), (rows, D), (3, rows, D), (rows, D)]
        )
        norm_own = lax.dynamic_slice_in_dim(norm_grads, lax.axis_index("blk") * rows, rows, 1)
        return (
            out_patches[None], out_latents[None], dx[None], dz[None], norm_own[:5], norm_own[5:10],
            read_in_grad, read_out_grad, self_in_grad, self_out_grad, write_in_grad, wo, up, down,
        )

    return body


def solution(mesh):
    return jax.shard_map(
        make_body(mesh.shape["blk"], mesh.shape["rep"]),
        mesh=mesh,
        in_specs=(
            P("rep", "blk", None), P("rep", "blk", None), P(), P(), P(), P(), P(), P(), P(), P(), P(), P(),
            P("rep", None), P("rep", "blk", None), P("rep", "blk", None),
        ),
        out_specs=(
            P("rep", "blk", None), P("rep", "blk", None), P("rep", "blk", None), P("rep", "blk", None),
            P(None, "blk"), P(None, "blk"), P(None, "blk", None), P("blk", None), P(None, "blk", None),
            P("blk", None), P(None, "blk", None), P("blk", None), P("blk", None), P("blk", None),
        ),
        check_vma=False,
    )
```

time: 426 us -> 297 us (0.70)
  waiting for transfers between devices: 169 us -> 88.3 us
  matrix products: 54.1 us -> 4.85 us
  Pallas kernels: 88.5 us -> 118 us
  other arithmetic: 28.8 us -> 5.45 us
  starting transfers between devices: 47.5 us -> 41.2 us
    ppermute x43 -> x42, waiting for transfers between devices: 169 us -> 88.3 us  [swap(): return lax.ppermute(tensor, axis, [(i, i ^ 1 << bit) for i in range(count)])]
    dot_general x28 -> x0, matrix products: 46.5 us -> none  [mm_tn(): lax.dot_general(left, right, (((0,), (0,)), ((), ())), preferred_element_...]
    pallas_call x3 -> x18, Pallas kernels: 21 us -> 57.8 us  [the longest x6 17.1 us: send(): call(functools.partial(stage_kernel, len(self.parts)), (lead,), [pl.Block...]
    convert_element_type x29 -> x1, other arithmetic: 17 us -> 0.01 us  [narrow(): return tensor.astype(BF)]
    unnamed x126 -> x176, local copies, waits for them, and re-layouts: 15 us -> 31.4 us
    ppermute x43 -> x42, starting transfers between devices: 47.5 us -> 41.2 us  [swap(): return lax.ppermute(tensor, axis, [(i, i ^ 1 << bit) for i in range(count)])]
    concatenate x11 -> x0, other arithmetic: 5.76 us -> none  [the longest x3 2.61 us: merge_core(): jnp.concatenate([pair[0] for pair in pairs], 1)]
  transfers between devices with their start and end apart: 43 -> 42, of which waited for: 22 -> 20; matrix products, arithmetic and copies ran while one was open for 16% -> 3% of each run, Pallas kernels for 6% -> 15%
where the time goes in v2:
time: 297 us; the launch traced here: 292 us
  Pallas kernels  118 us (40%)
  waiting for transfers between devices  88.3 us (30%)
  starting transfers between devices  41.2 us (14%)
  local copies, waits for them, and re-layouts  32.3 us (11%)
  other arithmetic  5.45 us (2%)
  matrix products  4.85 us (2%)
    ppermute x42, waiting for transfers between devices, swap(): return lax.ppermute(tensor, axis, [(i, i ^ 1 << bit) for i in range(count)])  88.3 us
    ppermute x42, starting transfers between devices, swap(): return lax.ppermute(tensor, axis, [(i, i ^ 1 << bit) for i in range(count)])  41.2 us
    pallas_call x1, Pallas kernels, body(): call(functools.partial(patch_kernel, D), grid, [patch_spec, patch_spec, p...  39.3 us
    unnamed x176, local copies, waits for them, and re-layouts  31.4 us
    pallas_call x6, Pallas kernels, send(): call(functools.partial(stage_kernel, len(self.parts)), (lead,), [pl.Block...  17.1 us
    pallas_call x2, Pallas kernels, feed_grad(): pl.pallas_call(feed_kernel, grid_spec=pltpu.PrefetchScalarGridSpec(num_sc...  15.7 us
    pallas_call x1, Pallas kernels, body(): call(read_forward_kernel, grid, [patch_spec, lat_spec, norm_spec, three,...  9.58 us
    pallas_call x2, Pallas kernels, unit_grads(): call(kernel, (1,), [smem] + [whole_patch] * len(patch_sized) + [lat_spec]...  9.34 us
  transfers between devices with their start and end apart: 42, of which 20 were waited for; matrix products, arithmetic and copies ran while one was open for 3% of the time, Pallas kernels for 15%

profile of v2, /device:TPU:0, one launch (start us, length us, event | category | flops | bytes accessed | tf_op | source)
XLA Modules:
  0.0 291.5 jit_solution(497184409048879889)
XLA Ops:
  2.4 9.6 %shard_map.272 = (bf16[32,768]{1,0:T(8,128)(2,1)S(1)}, f32[32,768]{1,0:T(8,128)S(1)}, bf16[1024,768]{1,0:T(8,128)(2,1)S(1)}, bf16[1024,768]{1,0:T(8,128)(2,1)S(1...) custom-call(bf16[1024,768]{1,0:T(8,128)(2,1)} %bitcast.129, ...), custom_call_target="tpu_custom_call" | custom-call | flops 2415919104 | bytes 9437184 | tf_op jit(solution)/shard_map/pallas_call | solution.py:705
  12.0 4.1 %collective-permute-start = (bf16[32,768]{1,0:T(8,128)(2,1)S(1)}, bf16[32,768]{1,0:T(8,128)(2,1)S(1)}, u32[]{:S(2)}, u32[]{:S(2)}) collective-permute-start(bf16[32,768]{1,0:T(8,128)(2,1)S(1)} %get-tuple-element.397.a2_ref), channel_id=1, source_target_pairs={{0,16},{2,18},{4,20},{6,22},{8,24},{10,26},{12,28},{14,30},{16,0},... | collective-permute-start | bytes 147464 | tf_op jit(solution)/shard_map/ppermute | solution.py:528
  16.2 2.5 convolution_convert_fusion.q3_ref
  19.5 1.6 collective-permute-start.1
  21.1 3.3 %collective-permute-done.1 = bf16[2,32,768]{2,1,0:T(8,128)(2,1)} collective-permute-done((bf16[2,32,768]{2,1,0:T(8,128)(2,1)}, bf16[2,32,768]{2,1,0:T(8,128)(2,1)}, u32[]{:S(2)}, u32[]{:S(2)}) %collective-permute-start.1) | collective-permute-done | bytes 98336 | tf_op jit(solution)/shard_map/ppermute | solution.py:528
  25.3 1.8 collective-permute-start.2
  27.1 1.5 collective-permute-start.3
  30.0 2.0 collective-permute-done.3
  32.1 1.7 collective-permute-start.4
  33.8 3.9 %collective-permute-done.5 = bf16[2,2,2,16,768]{4,3,0,1,2:T(8,128)(2,1)S(1)} collective-permute-done((bf16[2,2,2,16,768]{4,3,0,1,2:T(8,128)(2,1)S(1)}, bf16[2,2,2,16,768]{4,3,0,1,2:T(8,128)(2,1)S(1)}, u32[]{:S(2)}, u32[]{:S(2)}) %collective-permute-start.5) | collective-permute-done | bytes 196640 | tf_op jit(solution)/shard_map/ppermute | solution.py:528
  37.9 2.0 copy-done.5
  39.9 4.1 %shard_map.273 = (bf16[512,768]{1,0:T(8,128)(2,1)S(1)}, f32[384,512]{1,0:T(8,128)S(1)}, bf16[512,768]{1,0:T(8,128)(2,1)S(1)}, bf16[512,768]{1,0:T(8,128)(2,1)S(1...) custom-call(s32[1,64]{1,0:T(1,128)S(1)} %copy-done.83, ...), custom_call_target="tpu_custom_call" | custom-call | flops 2415919104 | bytes 11796480 | tf_op jit(solution)/shard_map/pallas_call | solution.py:732
  46.5 39.3 %shard_map.274 = (bf16[1024,768]{1,0:T(8,128)(2,1)}, bf16[2,1024,768]{2,1,0:T(8,128)(2,1)S(1)}, bf16[2,1024,3072]{2,1,0:T(8,128)(2,1)}, bf16[1024,768]{1,0:T(8,1...) custom-call(bf16[1024,768]{1,0:T(8,128)(2,1)} %bitcast.130, ...), custom_call_target="tpu_custom_call" | custom-call | flops 24159191040 | bytes 31457280 | tf_op jit(solution)/shard_map/pallas_call | solution.py:745
  87.0 2.5 shard_map.275
  89.7 2.8 collective-permute-start.6
  92.4 7.7 %shard_map.276 = bf16[16,192,768]{2,1,0:T(8,128)(2,1)S(1)} custom-call(s32[1]{0:T(128)S(6)} %sub.3.which_ref, bf16[2,1024,3072]{2,1,0:T(8,128)(2,1)} %get-tuple-element.296.gd_ref, bf16[2,1024,768]{2,1,0:T(8,128)(2,1)} %copy-done.7), custom_call_target="tpu_custom_call" | custom-call | flops 4831838208 | bytes 15728640 | tf_op jit(solution)/shard_map/pallas_call | solution.py:768
  100.3 2.2 collective-permute-start.7
  102.5 7.9 %shard_map.277 = bf16[16,192,768]{2,1,0:T(8,128)(2,1)S(1)} custom-call(s32[1]{0:T(128)} %bitcast.22.which_ref.core_ref, bf16[2,1024,3072]{2,1,0:T(8,128)(2,1)} %get-tuple-element.296.gd_ref, bf16[2,1024,768]{2,1,0:T(8,128)(2,1)} %copy-done.7), custom_call_target="tpu_custom_call" | custom-call | flops 4831838208 | bytes 15728640 | tf_op jit(solution)/shard_map/pallas_call | solution.py:768
  110.5 2.1 copy-done.1
  113.3 2.1 copy-done.3
  115.4 1.9 collective-permute-start.9
  117.4 1.5 collective-permute-start.10
  118.9 4.7 %shard_map.278 = (bf16[16,96,768]{2,1,0:T(8,128)(2,1)}, bf16[16,96,768]{2,1,0:T(8,128)(2,1)S(1)}) custom-call(s32[1]{0:T(128)} %bitcast.22.which_ref.core_ref, bf16[1024,768]{1,0:T(8,128)(2,1)S(1)} %get-tuple-element.307.o3_ref, bf16[1024,768]{1,0:T(8,128)(2,1)S(1)} %get-tuple-element.308.e3_ref, bf16[1024,768]{1,0:T(8,128)(2,1)S(1)} %copy-done.10, ...), custom_call_target="tpu_custom_call" | custom-call | flops 1207959552 | bytes 6291456 | tf_op jit(solution)/shard_map/pallas_call | solution.py:791
  127.7 2.3 convolution_convert_fusion.1.q_all_ref
  130.0 5.1 %collective-permute-done.11 = bf16[2,2,2,16,896]{4,3,0,1,2:T(8,128)(2,1)S(1)} collective-permute-done((bf16[2,2,2,16,896]{4,3,0,1,2:T(8,128)(2,1)S(1)}, bf16[2,2,2,16,896]{4,3,0,1,2:T(8,128)(2,1)S(1)}, u32[]{:S(2)}, u32[]{:S(2)}) %collective-permute-start.11) | collective-permute-done | bytes 229408 | tf_op jit(solution)/shard_map/ppermute | solution.py:528
  135.3 2.3 copy-done.2
  137.7 2.3 copy-done.4
  140.0 6.5 %shard_map.279 = (bf16[8,96,768]{2,1,0:T(8,128)(2,1)S(1)}, bf16[8,96,768]{2,1,0:T(8,128)(2,1)S(1)}, bf16[8,96,768]{2,1,0:T(8,128)(2,1)S(1)}, bf16[8,96,768]{2,1,...) custom-call(s32[3]{0:T(128)S(1)} %pad_add_fusion.pick_ref, ...), custom_call_target="tpu_custom_call" | custom-call | bytes 21233664 | tf_op jit(solution)/shard_map/pallas_call | solution.py:636
  146.6 1.6 collective-permute-start.14
  149.0 8.6 %shard_map.280 = (bf16[32,768]{1,0:T(8,128)(2,1)S(1)}, bf16[32,768]{1,0:T(8,128)(2,1)S(1)}, f32[32,768]{1,0:T(8,128)S(1)}, bf16[32,768]{1,0:T(8,128)(2,1)S(1)}, ...) custom-call(bf16[8,16,896]{2,1,0:T(8,128)(2,1)S(1)} %bitcast.101, ...), custom_call_target="tpu_custom_call" | custom-call | flops 2415919104 | bytes 7864320 | tf_op jit(solution)/shard_map/pallas_call | solution.py:827
  157.6 16.4 %collective-permute-done.14 = bf16[8,96,768]{2,1,0:T(8,128)(2,1)S(1)} collective-permute-done((bf16[8,96,768]{2,1,0:T(8,128)(2,1)S(1)}, bf16[8,96,768]{2,1,0:T(8,128)(2,1)S(1)}, u32[]{:S(2)}, u32[]{:S(2)}) %collective-permute-start.14) | collective-permute-done | bytes 1179680 | tf_op jit(solution)/shard_map/ppermute | solution.py:528
  175.4 1.7 shard_map.281
  177.2 1.6 collective-permute-start.17
  179.8 4.7 %shard_map.282 = (bf16[16,192,768]{2,1,0:T(8,128)(2,1)S(1)}, bf16[16,192,768]{2,1,0:T(8,128)(2,1)S(1)}) custom-call(s32[1]{0:T(128)} %bitcast.22.which_ref.core_ref, bf16[1024,768]{1,0:T(8,128)(2,1)S(1)} %copy-done.11, bf16[1024,768]{1,0:T(8,128)(2,1)S(1)} %get-tuple-element.420.dk1_ref, bf16[1024,768]{1,0:T(8,128)(2,1)S(1)} %get-tuple-element.421.dv1_ref, ...), custom_call_target="tpu_custom_call" | custom-call | flops 1207959552 | bytes 6291456 | tf_op jit(solution)/shard_map/pallas_call | solution.py:791
  184.4 6.2 %collective-permute-done.17 = bf16[4,96,768]{2,1,0:T(8,128)(2,1)S(1)} collective-permute-done((bf16[4,96,768]{2,1,0:T(8,128)(2,1)S(1)}, bf16[4,96,768]{2,1,0:T(8,128)(2,1)S(1)}, u32[]{:S(2)}, u32[]{:S(2)}) %collective-permute-start.17) | collective-permute-done | bytes 589856 | tf_op jit(solution)/shard_map/ppermute | solution.py:528
  194.9 1.7 collective-permute-start.21
  197.9 8.4 %shard_map.284 = (bf16[1024,768]{1,0:T(8,128)(2,1)}, bf16[32,768]{1,0:T(8,128)(2,1)}, f32[16,768]{1,0:T(8,128)S(1)}) custom-call(bf16[1024,768]{1,0:T(8,128)(2,1)} %bitcast.131, f32[1024,768]{1,0:T(8,128)} %copy-done.14, bf16[1024,768]{1,0:T(8,128)(2,1)} %copy-done.8, bf16[1024,768]{1,0:T(8,128)(2,1)S(1)} %get-tuple-element.420.dk1_ref, ...), custom_call_target="tpu_custom_call" | custom-call | flops 3623878656 | bytes 11010048 | tf_op jit(solution)/shard_map/pallas_call | solution.py:848
  206.4 4.2 %shard_map.285 = (bf16[8,64,768]{2,1,0:T(8,128)(2,1)}, bf16[8,64,768]{2,1,0:T(8,128)(2,1)S(1)}, bf16[8,64,768]{2,1,0:T(8,128)(2,1)}, bf16[8,64,768]{2,1,0:T(8,12...) custom-call(s32[3]{0:T(128)S(1)} %pad_add_fusion.pick_ref, ...), custom_call_target="tpu_custom_call" | custom-call | bytes 14155776 | tf_op jit(solution)/shard_map/pallas_call | solution.py:636
  213.3 1.5 collective-permute-start.26
  225.2 8.5 %collective-permute-done.25 = f32[16,768]{1,0:T(8,128)S(1)} collective-permute-done((f32[16,768]{1,0:T(8,128)S(1)}, f32[16,768]{1,0:T(8,128)S(1)}, u32[]{:S(2)}, u32[]{:S(2)}) %collective-permute-start.25) | collective-permute-done | bytes 49184 | tf_op jit(solution)/shard_map/ppermute | solution.py:528
  233.7 10.4 %collective-permute-done.29.got_ref = bf16[288,768]{1,0:T(8,128)(2,1)S(1)} collective-permute-done((bf16[288,768]{1,0:T(8,128)(2,1)S(1)}, bf16[288,768]{1,0:T(8,128)(2,1)S(1)}, u32[]{:S(2)}, u32[]{:S(2)}) %collective-permute-start.29) | collective-permute-done | bytes 442400 | tf_op jit(solution)/shard_map/ppermute | solution.py:528
  247.3 2.7 shard_map.287
  252.0 1.4 collective-permute-start.30
  254.8 8.1 %collective-permute-done.30 = f32[16,768]{1,0:T(8,128)S(1)} collective-permute-done((f32[16,768]{1,0:T(8,128)S(1)}, f32[16,768]{1,0:T(8,128)S(1)}, u32[]{:S(2)}, u32[]{:S(2)}) %collective-permute-start.30) | collective-permute-done | bytes 49184 | tf_op jit(solution)/shard_map/ppermute | solution.py:528
  265.5 1.4 collective-permute-start.38
  267.3 4.0 %collective-permute-done.35 = f32[16,768]{1,0:T(8,128)S(1)} collective-permute-done((f32[16,768]{1,0:T(8,128)S(1)}, f32[16,768]{1,0:T(8,128)S(1)}, u32[]{:S(2)}, u32[]{:S(2)}) %collective-permute-start.35) | collective-permute-done | bytes 49184 | tf_op jit(solution)/shard_map/ppermute | solution.py:528
  271.5 1.6 collective-permute-start.40
  274.5 14.0 %collective-permute-done.39 = f32[16,768]{1,0:T(8,128)S(1)} collective-permute-done((f32[16,768]{1,0:T(8,128)S(1)}, f32[16,768]{1,0:T(8,128)S(1)}, u32[]{:S(2)}, u32[]{:S(2)}) %collective-permute-start.39) | collective-permute-done | bytes 49184 | tf_op jit(solution)/shard_map/ppermute | solution.py:528
  (267 shorter events, 49.4 us)
Async XLA Ops:
  12.0 6.7 %collective-permute-start = (bf16[32,768]{1,0:T(8,128)(2,1)S(1)}, bf16[32,768]{1,0:T(8,128)(2,1)S(1)}, u32[]{:S(2)}, u32[]{:S(2)}) collective-permute-start(bf16[32,768]{1,0:T(8,128)(2,1)S(1)} %get-tuple-element.397.a2_ref), channel_id=1, source_target_pairs={{0,16},{2,18},{4,20},{6,22},{8,24},{10,26},{12,28},{14,30},{16,0},... | collective-permute-start | bytes 147464 | tf_op jit(solution)/shard_map/ppermute | solution.py:528
  19.5 4.9 %collective-permute-start.1 = (bf16[2,32,768]{2,1,0:T(8,128)(2,1)}, bf16[2,32,768]{2,1,0:T(8,128)(2,1)}, u32[]{:S(2)}, u32[]{:S(2)}) collective-permute-start(bf16[2,32,768]{2,1,0:T(8,128)(2,1)} %get-tuple-element.268), channel_id=1, source_target_pairs={{0,8},{2,10},{4,12},{6,14},{8,0},{10,2},{12,4},{14,6},{16,24},{18,... | collective-permute-start | bytes 294920 | tf_op jit(solution)/shard_map/ppermute | solution.py:528
  25.3 4.7 %collective-permute-start.2 = (bf16[2,2,16,768]{3,2,0,1:T(8,128)(2,1)S(1)}, bf16[2,2,16,768]{3,2,0,1:T(8,128)(2,1)S(1)}, u32[]{:S(2)}, u32[]{:S(2)}) collective-permute-start(bf16[2,2,16,768]{3,2,0,1:T(8,128)(2,1)S(1)} %get-tuple-element.269), channel_id=1, source_target_pairs={{0,4},{2,6},{4,0},{6,2},{8,12},{10,14},{12,8},{14,10},{16,20},{18,... | collective-permute-start | bytes 294920 | tf_op jit(solution)/shard_map/ppermute | solution.py:528
  27.1 4.9 %collective-permute-start.3 = (bf16[2,2,16,768]{3,2,0,1:T(8,128)(2,1)S(1)}, bf16[2,2,16,768]{3,2,0,1:T(8,128)(2,1)S(1)}, u32[]{:S(2)}, u32[]{:S(2)}) collective-permute-start(bf16[2,2,16,768]{3,2,0,1:T(8,128)(2,1)S(1)} %get-tuple-element.270), channel_id=1, source_target_pairs={{0,2},{2,0},{4,6},{6,4},{8,10},{10,8},{12,14},{14,12},{16,18},{18,... | collective-permute-start | bytes 294920 | tf_op jit(solution)/shard_map/ppermute | solution.py:528
  32.0 5.7 %collective-permute-start.5 = (bf16[2,2,2,16,768]{4,3,0,1,2:T(8,128)(2,1)S(1)}, bf16[2,2,2,16,768]{4,3,0,1,2:T(8,128)(2,1)S(1)}, u32[]{:S(2)}, u32[]{:S(2)}) collective-permute-start(bf16[2,2,2,16,768]{4,3,0,1,2:T(8,128)(2,1)S(1)} %pad_maximum_fusion.3), channel_id=1, source_target_pairs={{0,4},{2,6},{4,0},{6,2},{8,12},{10,14},{12,8},{14,10},{16,20},{18,... | collective-permute-start | bytes 589832 | tf_op jit(solution)/shard_map/ppermute | solution.py:528
  32.1 5.7 %collective-permute-start.4 = (bf16[2,2,2,16,768]{4,3,0,1,2:T(8,128)(2,1)S(1)}, bf16[2,2,2,16,768]{4,3,0,1,2:T(8,128)(2,1)S(1)}, u32[]{:S(2)}, u32[]{:S(2)}) collective-permute-start(bf16[2,2,2,16,768]{4,3,0,1,2:T(8,128)(2,1)S(1)} %pad_maximum_fusion.2), channel_id=1, source_target_pairs={{0,2},{2,0},{4,6},{6,4},{8,10},{10,8},{12,14},{14,12},{16,18},{18,... | collective-permute-start | bytes 589832 | tf_op jit(solution)/shard_map/ppermute | solution.py:528
  45.6 41.4 %copy-start.15 = (bf16[512,768]{1,0:T(8,128)(2,1)}, bf16[512,768]{1,0:T(8,128)(2,1)S(1)}, u32[]{:S(2)}) copy-start(bf16[512,768]{1,0:T(8,128)(2,1)S(1)} %get-tuple-element.347.k2_ref) | copy-start | bytes 2359300
  45.6 41.4 %copy-start.17 = (bf16[512,768]{1,0:T(8,128)(2,1)}, bf16[512,768]{1,0:T(8,128)(2,1)S(1)}, u32[]{:S(2)}) copy-start(bf16[512,768]{1,0:T(8,128)(2,1)S(1)} %get-tuple-element.348.v2_ref) | copy-start | bytes 2359300
  46.5 40.6 %copy-start.62 = (bf16[1,32,768]{2,1,0:T(8,128)(2,1)S(1)}, bf16[1,32,768]{2,1,0:T(8,128)(2,1)}, u32[]{:S(2)}) copy-start(bf16[1,32,768]{2,1,0:T(8,128)(2,1)} %param.31) | copy-start | bytes 147460
  87.0 31.8 %copy-start.8 = (bf16[1024,768]{1,0:T(8,128)(2,1)}, bf16[1024,768]{1,0:T(8,128)(2,1)S(1)}, u32[]{:S(2)}) copy-start(bf16[1024,768]{1,0:T(8,128)(2,1)S(1)} %get-tuple-element.419.dq3_ref) | copy-start | bytes 4718596
  89.7 10.5 %collective-permute-start.6 = (bf16[32,896]{1,0:T(8,128)(2,1)S(1)}, bf16[32,896]{1,0:T(8,128)(2,1)S(1)}, u32[]{:S(2)}, u32[]{:S(2)}) collective-permute-start(bf16[32,896]{1,0:T(8,128)(2,1)S(1)} %get-tuple-element.288), channel_id=1, source_target_pairs={{0,16},{2,18},{4,20},{6,22},{8,24},{10,26},{12,28},{14,30},{16,0},... | collective-permute-start | bytes 172040 | tf_op jit(solution)/shard_map/ppermute | solution.py:528
  100.2 13.1 %collective-permute-start.8 = (bf16[16,192,768]{2,1,0:T(8,128)(2,1)S(1)}, bf16[16,192,768]{2,1,0:T(8,128)(2,1)S(1)}, u32[]{:S(2)}, u32[]{:S(2)}) collective-permute-start(bf16[16,192,768]{2,1,0:T(8,128)(2,1)S(1)} %shard_map.276), channel_id=1, source_target_pairs={{0,1},{1,0},{2,3},{3,2},{4,5},{5,4},{6,7},{7,6},{8,9},{9,8},{10,11... | collective-permute-start | bytes 14155784 | tf_op jit(solution)/shard_map/ppermute | solution.py:528
  100.3 12.2 %collective-permute-start.7 = (bf16[2,32,896]{2,1,0:T(8,128)(2,1)S(1)}, bf16[2,32,896]{2,1,0:T(8,128)(2,1)S(1)}, u32[]{:S(2)}, u32[]{:S(2)}) collective-permute-start(bf16[2,32,896]{2,1,0:T(8,128)(2,1)S(1)} %get-tuple-element.294), channel_id=1, source_target_pairs={{0,8},{2,10},{4,12},{6,14},{8,0},{10,2},{12,4},{14,6},{16,24},{18,... | collective-permute-start | bytes 344072 | tf_op jit(solution)/shard_map/ppermute | solution.py:528
  115.4 9.5 %collective-permute-start.9 = (bf16[2,2,16,896]{3,2,0,1:T(8,128)(2,1)}, bf16[2,2,16,896]{3,2,0,1:T(8,128)(2,1)}, u32[]{:S(2)}, u32[]{:S(2)}) collective-permute-start(bf16[2,2,16,896]{3,2,0,1:T(8,128)(2,1)} %get-tuple-element.299), channel_id=1, source_target_pairs={{0,4},{2,6},{4,0},{6,2},{8,12},{10,14},{12,8},{14,10},{16,20},{18,... | collective-permute-start | bytes 344072 | tf_op jit(solution)/shard_map/ppermute | solution.py:528
  117.4 7.6 %collective-permute-start.10 = (bf16[2,2,16,896]{3,2,0,1:T(8,128)(2,1)}, bf16[2,2,16,896]{3,2,0,1:T(8,128)(2,1)}, u32[]{:S(2)}, u32[]{:S(2)}) collective-permute-start(bf16[2,2,16,896]{3,2,0,1:T(8,128)(2,1)} %get-tuple-element.300), channel_id=1, source_target_pairs={{0,2},{2,0},{4,6},{6,4},{8,10},{10,8},{12,14},{14,12},{16,18},{18,... | collective-permute-start | bytes 344072 | tf_op jit(solution)/shard_map/ppermute | solution.py:528
  124.9 10.4 %collective-permute-start.13 = (bf16[16,96,768]{2,1,0:T(8,128)(2,1)}, bf16[16,96,768]{2,1,0:T(8,128)(2,1)}, u32[]{:S(2)}, u32[]{:S(2)}) collective-permute-start(bf16[16,96,768]{2,1,0:T(8,128)(2,1)} %get-tuple-element.327), channel_id=1, source_target_pairs={{0,1},{1,0},{2,3},{3,2},{4,5},{5,4},{6,7},{7,6},{8,9},{9,8},{10,11... | collective-permute-start | bytes 7077896 | tf_op jit(solution)/shard_map/ppermute | solution.py:528
  127.0 8.1 %collective-permute-start.11 = (bf16[2,2,2,16,896]{4,3,0,1,2:T(8,128)(2,1)S(1)}, bf16[2,2,2,16,896]{4,3,0,1,2:T(8,128)(2,1)S(1)}, u32[]{:S(2)}, u32[]{:S(2)}) collective-permute-start(bf16[2,2,2,16,896]{4,3,0,1,2:T(8,128)(2,1)S(1)} %pad_maximum_fusion), channel_id=1, source_target_pairs={{0,2},{2,0},{4,6},{6,4},{8,10},{10,8},{12,14},{14,12},{16,18},{18,... | collective-permute-start | bytes 688136 | tf_op jit(solution)/shard_map/ppermute | solution.py:528
  127.6 7.7 %collective-permute-start.12 = (bf16[2,2,2,16,896]{4,3,0,1,2:T(8,128)(2,1)S(1)}, bf16[2,2,2,16,896]{4,3,0,1,2:T(8,128)(2,1)S(1)}, u32[]{:S(2)}, u32[]{:S(2)}) collective-permute-start(bf16[2,2,2,16,896]{4,3,0,1,2:T(8,128)(2,1)S(1)} %pad_maximum_fusion.1), channel_id=1, source_target_pairs={{0,4},{2,6},{4,0},{6,2},{8,12},{10,14},{12,8},{14,10},{16,20},{18,... | collective-permute-start | bytes 688136 | tf_op jit(solution)/shard_map/ppermute | solution.py:528
  146.6 27.4 %collective-permute-start.14 = (bf16[8,96,768]{2,1,0:T(8,128)(2,1)S(1)}, bf16[8,96,768]{2,1,0:T(8,128)(2,1)S(1)}, u32[]{:S(2)}, u32[]{:S(2)}) collective-permute-start(bf16[8,96,768]{2,1,0:T(8,128)(2,1)S(1)} %get-tuple-element.335), channel_id=1, source_target_pairs={{0,2},{2,0},{4,6},{6,4},{8,10},{10,8},{12,14},{14,12},{16,18},{18,... | collective-permute-start | bytes 3538952 | tf_op jit(solution)/shard_map/ppermute | solution.py:528
  148.2 27.0 %collective-permute-start.15 = (bf16[8,96,768]{2,1,0:T(8,128)(2,1)S(1)}, bf16[8,96,768]{2,1,0:T(8,128)(2,1)S(1)}, u32[]{:S(2)}, u32[]{:S(2)}) collective-permute-start(bf16[8,96,768]{2,1,0:T(8,128)(2,1)S(1)} %get-tuple-element.337), channel_id=1, source_target_pairs={{0,4},{2,6},{4,0},{6,2},{8,12},{10,14},{12,8},{14,10},{16,20},{18,... | collective-permute-start | bytes 3538952 | tf_op jit(solution)/shard_map/ppermute | solution.py:528
  148.5 26.9 %collective-permute-start.16 = (bf16[8,96,768]{2,1,0:T(8,128)(2,1)S(1)}, bf16[8,96,768]{2,1,0:T(8,128)(2,1)S(1)}, u32[]{:S(2)}, u32[]{:S(2)}) collective-permute-start(bf16[8,96,768]{2,1,0:T(8,128)(2,1)S(1)} %get-tuple-element.339), channel_id=1, source_target_pairs={{0,8},{2,10},{4,12},{6,14},{8,0},{10,2},{12,4},{14,6},{16,24},{18,... | collective-permute-start | bytes 3538952 | tf_op jit(solution)/shard_map/ppermute | solution.py:528
  177.2 13.4 %collective-permute-start.17 = (bf16[4,96,768]{2,1,0:T(8,128)(2,1)S(1)}, bf16[4,96,768]{2,1,0:T(8,128)(2,1)S(1)}, u32[]{:S(2)}, u32[]{:S(2)}) collective-permute-start(bf16[4,96,768]{2,1,0:T(8,128)(2,1)S(1)} %get-tuple-element.377), channel_id=1, source_target_pairs={{0,4},{2,6},{4,0},{6,2},{8,12},{10,14},{12,8},{14,10},{16,20},{18,... | collective-permute-start | bytes 1769480 | tf_op jit(solution)/shard_map/ppermute | solution.py:528
  178.8 12.9 %collective-permute-start.18 = (bf16[4,96,768]{2,1,0:T(8,128)(2,1)S(1)}, bf16[4,96,768]{2,1,0:T(8,128)(2,1)S(1)}, u32[]{:S(2)}, u32[]{:S(2)}) collective-permute-start(bf16[4,96,768]{2,1,0:T(8,128)(2,1)S(1)} %get-tuple-element.379), channel_id=1, source_target_pairs={{0,8},{2,10},{4,12},{6,14},{8,0},{10,2},{12,4},{14,6},{16,24},{18,... | collective-permute-start | bytes 1769480 | tf_op jit(solution)/shard_map/ppermute | solution.py:528
  179.1 12.7 %collective-permute-start.19 = (bf16[4,96,768]{2,1,0:T(8,128)(2,1)S(1)}, bf16[4,96,768]{2,1,0:T(8,128)(2,1)S(1)}, u32[]{:S(2)}, u32[]{:S(2)}) collective-permute-start(bf16[4,96,768]{2,1,0:T(8,128)(2,1)S(1)} %get-tuple-element.381), channel_id=1, source_target_pairs={{0,2},{2,0},{4,6},{6,4},{8,10},{10,8},{12,14},{14,12},{16,18},{18,... | collective-permute-start | bytes 1769480 | tf_op jit(solution)/shard_map/ppermute | solution.py:528
  191.7 14.7 %collective-permute-start.24 = (bf16[16,192,768]{2,1,0:T(8,128)(2,1)S(1)}, bf16[16,192,768]{2,1,0:T(8,128)(2,1)S(1)}, u32[]{:S(2)}, u32[]{:S(2)}) collective-permute-start(bf16[16,192,768]{2,1,0:T(8,128)(2,1)S(1)} %get-tuple-element.438), channel_id=1, source_target_pairs={{0,1},{1,0},{2,3},{3,2},{4,5},{5,4},{6,7},{7,6},{8,9},{9,8},{10,11... | collective-permute-start | bytes 14155784 | tf_op jit(solution)/shard_map/ppermute | solution.py:528
  194.9 11.4 %collective-permute-start.21 = (bf16[2,96,768]{2,1,0:T(8,128)(2,1)S(1)}, bf16[2,96,768]{2,1,0:T(8,128)(2,1)S(1)}, u32[]{:S(2)}, u32[]{:S(2)}) collective-permute-start(bf16[2,96,768]{2,1,0:T(8,128)(2,1)S(1)} %get-tuple-element.411), channel_id=1, source_target_pairs={{0,8},{2,10},{4,12},{6,14},{8,0},{10,2},{12,4},{14,6},{16,24},{18,... | collective-permute-start | bytes 884744 | tf_op jit(solution)/shard_map/ppermute | solution.py:528
  196.6 9.8 %collective-permute-start.22 = (bf16[2,96,768]{2,1,0:T(8,128)(2,1)S(1)}, bf16[2,96,768]{2,1,0:T(8,128)(2,1)S(1)}, u32[]{:S(2)}, u32[]{:S(2)}) collective-permute-start(bf16[2,96,768]{2,1,0:T(8,128)(2,1)S(1)} %get-tuple-element.413), channel_id=1, source_target_pairs={{0,2},{2,0},{4,6},{6,4},{8,10},{10,8},{12,14},{14,12},{16,18},{18,... | collective-permute-start | bytes 884744 | tf_op jit(solution)/shard_map/ppermute | solution.py:528
  197.3 9.1 %collective-permute-start.23 = (bf16[2,96,768]{2,1,0:T(8,128)(2,1)S(1)}, bf16[2,96,768]{2,1,0:T(8,128)(2,1)S(1)}, u32[]{:S(2)}, u32[]{:S(2)}) collective-permute-start(bf16[2,96,768]{2,1,0:T(8,128)(2,1)S(1)} %get-tuple-element.415), channel_id=1, source_target_pairs={{0,4},{2,6},{4,0},{6,2},{8,12},{10,14},{12,8},{14,10},{16,20},{18,... | collective-permute-start | bytes 884744 | tf_op jit(solution)/shard_map/ppermute | solution.py:528
  213.3 30.7 %collective-permute-start.26 = (bf16[8,64,768]{2,1,0:T(8,128)(2,1)}, bf16[8,64,768]{2,1,0:T(8,128)(2,1)S(1)}, u32[]{:S(2)}, u32[]{:S(2)}) collective-permute-start(bf16[8,64,768]{2,1,0:T(8,128)(2,1)} %get-tuple-element.446), channel_id=1, source_target_pairs={{0,2},{2,0},{4,6},{6,4},{8,10},{10,8},{12,14},{14,12},{16,18},{18,... | collective-permute-start | bytes 2359304 | tf_op jit(solution)/shard_map/ppermute | solution.py:528
  214.8 30.2 %collective-permute-start.27 = (bf16[8,64,768]{2,1,0:T(8,128)(2,1)}, bf16[8,64,768]{2,1,0:T(8,128)(2,1)}, u32[]{:S(2)}, u32[]{:S(2)}) collective-permute-start(bf16[8,64,768]{2,1,0:T(8,128)(2,1)} %get-tuple-element.448), channel_id=1, source_target_pairs={{0,4},{2,6},{4,0},{6,2},{8,12},{10,14},{12,8},{14,10},{16,20},{18,... | collective-permute-start | bytes 2359304 | tf_op jit(solution)/shard_map/ppermute | solution.py:528
  216.1 28.9 %collective-permute-start.28 = (bf16[8,64,768]{2,1,0:T(8,128)(2,1)}, bf16[8,64,768]{2,1,0:T(8,128)(2,1)}, u32[]{:S(2)}, u32[]{:S(2)}) collective-permute-start(bf16[8,64,768]{2,1,0:T(8,128)(2,1)} %get-tuple-element.450), channel_id=1, source_target_pairs={{0,8},{2,10},{4,12},{6,14},{8,0},{10,2},{12,4},{14,6},{16,24},{18,... | collective-permute-start | bytes 2359304 | tf_op jit(solution)/shard_map/ppermute | solution.py:528
  216.5 28.6 %copy-start.30 = (bf16[8,64,768]{2,1,0:T(8,128)(2,1)S(1)}, bf16[8,64,768]{2,1,0:T(8,128)(2,1)}, u32[]{:S(2)}) copy-start(bf16[8,64,768]{2,1,0:T(8,128)(2,1)} %copy-done.29) | copy-start | bytes 2359300
  216.5 28.6 %copy-start.32 = (bf16[8,64,768]{2,1,0:T(8,128)(2,1)S(1)}, bf16[8,64,768]{2,1,0:T(8,128)(2,1)}, u32[]{:S(2)}) copy-start(bf16[8,64,768]{2,1,0:T(8,128)(2,1)} %copy-done.31) | copy-start | bytes 2359300
  222.6 21.5 %collective-permute-start.29 = (bf16[288,768]{1,0:T(8,128)(2,1)S(1)}, bf16[288,768]{1,0:T(8,128)(2,1)S(1)}, u32[]{:S(2)}, u32[]{:S(2)}) collective-permute-start(bf16[288,768]{1,0:T(8,128)(2,1)S(1)} %get-tuple-element.461), channel_id=1, source_target_pairs={{0,16},{2,18},{4,20},{6,22},{8,24},{10,26},{12,28},{14,30},{16,0},... | collective-permute-start | bytes 1327112 | tf_op jit(solution)/shard_map/ppermute | solution.py:528
  223.2 1.2 collective-permute-start.20
  224.4 9.3 %collective-permute-start.25 = (f32[16,768]{1,0:T(8,128)S(1)}, f32[16,768]{1,0:T(8,128)S(1)}, u32[]{:S(2)}, u32[]{:S(2)}) collective-permute-start(f32[16,768]{1,0:T(8,128)S(1)} %add.30), channel_id=1, source_target_pairs={{0,2},{2,0},{4,6},{6,4},{8,10},{10,8},{12,14},{14,12},{16,18},{18,... | collective-permute-start | bytes 147464 | tf_op jit(solution)/shard_map/ppermute | solution.py:528
  250.2 3.3 %collective-permute-start.34 = (bf16[288,768]{1,0:T(8,128)(2,1)S(1)}, bf16[288,768]{1,0:T(8,128)(2,1)S(1)}, u32[]{:S(2)}, u32[]{:S(2)}) collective-permute-start(bf16[288,768]{1,0:T(8,128)(2,1)S(1)} %shard_map.288.mine_ref), channel_id=1, source_target_pairs={{0,1},{1,0},{2,3},{3,2},{4,5},{5,4},{6,7},{7,6},{8,9},{9,8},{10,11... | collective-permute-start | bytes 1327112 | tf_op jit(solution)/shard_map/ppermute | solution.py:528
  250.3 12.6 %collective-permute-start.31 = (bf16[4,64,768]{2,1,0:T(8,128)(2,1)S(1)}, bf16[4,64,768]{2,1,0:T(8,128)(2,1)S(1)}, u32[]{:S(2)}, u32[]{:S(2)}) collective-permute-start(bf16[4,64,768]{2,1,0:T(8,128)(2,1)S(1)} %get-tuple-element.470), channel_id=1, source_target_pairs={{0,4},{2,6},{4,0},{6,2},{8,12},{10,14},{12,8},{14,10},{16,20},{18,... | collective-permute-start | bytes 1179656 | tf_op jit(solution)/shard_map/ppermute | solution.py:528
  251.1 11.8 %collective-permute-start.32 = (bf16[4,64,768]{2,1,0:T(8,128)(2,1)S(1)}, bf16[4,64,768]{2,1,0:T(8,128)(2,1)S(1)}, u32[]{:S(2)}, u32[]{:S(2)}) collective-permute-start(bf16[4,64,768]{2,1,0:T(8,128)(2,1)S(1)} %get-tuple-element.471), channel_id=1, source_target_pairs={{0,8},{2,10},{4,12},{6,14},{8,0},{10,2},{12,4},{14,6},{16,24},{18,... | collective-permute-start | bytes 1179656 | tf_op jit(solution)/shard_map/ppermute | solution.py:528
  251.5 11.4 %collective-permute-start.33 = (bf16[4,64,768]{2,1,0:T(8,128)(2,1)S(1)}, bf16[4,64,768]{2,1,0:T(8,128)(2,1)S(1)}, u32[]{:S(2)}, u32[]{:S(2)}) collective-permute-start(bf16[4,64,768]{2,1,0:T(8,128)(2,1)S(1)} %get-tuple-element.472), channel_id=1, source_target_pairs={{0,2},{2,0},{4,6},{6,4},{8,10},{10,8},{12,14},{14,12},{16,18},{18,... | collective-permute-start | bytes 1179656 | tf_op jit(solution)/shard_map/ppermute | solution.py:528
  252.0 10.8 %collective-permute-start.30 = (f32[16,768]{1,0:T(8,128)S(1)}, f32[16,768]{1,0:T(8,128)S(1)}, u32[]{:S(2)}, u32[]{:S(2)}) collective-permute-start(f32[16,768]{1,0:T(8,128)S(1)} %add.31), channel_id=1, source_target_pairs={{0,4},{2,6},{4,0},{6,2},{8,12},{10,14},{12,8},{14,10},{16,20},{18,... | collective-permute-start | bytes 147464 | tf_op jit(solution)/shard_map/ppermute | solution.py:528
  263.7 7.6 %collective-permute-start.36 = (bf16[2,64,768]{2,1,0:T(8,128)(2,1)S(1)}, bf16[2,64,768]{2,1,0:T(8,128)(2,1)S(1)}, u32[]{:S(2)}, u32[]{:S(2)}) collective-permute-start(bf16[2,64,768]{2,1,0:T(8,128)(2,1)S(1)} %get-tuple-element.490), channel_id=1, source_target_pairs={{0,8},{2,10},{4,12},{6,14},{8,0},{10,2},{12,4},{14,6},{16,24},{18,... | collective-permute-start | bytes 589832 | tf_op jit(solution)/shard_map/ppermute | solution.py:528
  264.9 6.4 %collective-permute-start.37 = (bf16[2,64,768]{2,1,0:T(8,128)(2,1)S(1)}, bf16[2,64,768]{2,1,0:T(8,128)(2,1)S(1)}, u32[]{:S(2)}, u32[]{:S(2)}) collective-permute-start(bf16[2,64,768]{2,1,0:T(8,128)(2,1)S(1)} %get-tuple-element.491), channel_id=1, source_target_pairs={{0,2},{2,0},{4,6},{6,4},{8,10},{10,8},{12,14},{14,12},{16,18},{18,... | collective-permute-start | bytes 589832 | tf_op jit(solution)/shard_map/ppermute | solution.py:528
  265.5 5.9 %collective-permute-start.38 = (bf16[2,64,768]{2,1,0:T(8,128)(2,1)S(1)}, bf16[2,64,768]{2,1,0:T(8,128)(2,1)S(1)}, u32[]{:S(2)}, u32[]{:S(2)}) collective-permute-start(bf16[2,64,768]{2,1,0:T(8,128)(2,1)S(1)} %get-tuple-element.492), channel_id=1, source_target_pairs={{0,4},{2,6},{4,0},{6,2},{8,12},{10,14},{12,8},{14,10},{16,20},{18,... | collective-permute-start | bytes 589832 | tf_op jit(solution)/shard_map/ppermute | solution.py:528
  266.9 4.4 %collective-permute-start.35 = (f32[16,768]{1,0:T(8,128)S(1)}, f32[16,768]{1,0:T(8,128)S(1)}, u32[]{:S(2)}, u32[]{:S(2)}) collective-permute-start(f32[16,768]{1,0:T(8,128)S(1)} %add.32), channel_id=1, source_target_pairs={{0,8},{2,10},{4,12},{6,14},{8,0},{10,2},{12,4},{14,6},{16,24},{18,... | collective-permute-start | bytes 147464 | tf_op jit(solution)/shard_map/ppermute | solution.py:528
  271.5 17.0 %collective-permute-start.40 = (bf16[192,768]{1,0:T(8,128)(2,1)S(1)}, bf16[192,768]{1,0:T(8,128)(2,1)S(1)}, u32[]{:S(2)}, u32[]{:S(2)}) collective-permute-start(bf16[192,768]{1,0:T(8,128)(2,1)S(1)} %get-tuple-element.505), channel_id=1, source_target_pairs={{0,16},{2,18},{4,20},{6,22},{8,24},{10,26},{12,28},{14,30},{16,0},... | collective-permute-start | bytes 884744 | tf_op jit(solution)/shard_map/ppermute | solution.py:528
  273.1 15.4 %collective-permute-start.39 = (f32[16,768]{1,0:T(8,128)S(1)}, f32[16,768]{1,0:T(8,128)S(1)}, u32[]{:S(2)}, u32[]{:S(2)}) collective-permute-start(f32[16,768]{1,0:T(8,128)S(1)} %add.33), channel_id=1, source_target_pairs={{0,16},{2,18},{4,20},{6,22},{8,24},{10,26},{12,28},{14,30},{16,0},... | collective-permute-start | bytes 147464 | tf_op jit(solution)/shard_map/ppermute | solution.py:528
  288.6 1.6 collective-permute-start.41
  (82 other events, 506.2 us)

commit v3 on v2

--- a/solution.py
+++ b/solution.py
@@ -205,29 +205,34 @@
 
 
 def patch_kernel(
-    chunk, x_ref, q3_ref, cot_ref, k3_ref, v3_ref, norm_ref, wo_ref, up_ref, down_ref,
-    out_ref, he_ref, gd_ref, o3_ref, e3_ref, dq3_ref, dx1_ref, dk3_ref, dv3_ref,
-    gain_ref, shift_ref,
+    chunk, size, core_ref, x_ref, q3_ref, cot_ref, k3_ref, v3_ref, norm_ref, wo_ref, up_ref, down_ref, b1_ref, b3_ref,
+    out_ref, h_ref, gd_ref, dq3_ref, dx1_ref, dk3_ref, dv3_ref, other_ref, mine_ref,
+    gain_ref, shift_ref, o3_ref, e3_ref,
 ):
     step = pl.program_id(0)
-    own = pl.ds(pl.multiple_of(step * LAT, LAT), LAT)
-    kx = expand(k3_ref[own, :])
-    vx = expand(v3_ref[own, :])
-    q3 = q3_ref[...]
-    tokens = q3.shape[0]
-    scores = (mm_nt(kx, q3) * FACTOR).reshape(HEADS, LAT, tokens)
-    powers = jnp.exp(scores - jnp.max(scores, axis=1, keepdims=True))
-    shares = powers / jnp.sum(powers, axis=1, keepdims=True)
-    shares_low = narrow(shares.reshape(HL, tokens))
-    o3 = narrow(mm_tn(shares_low, vx))
-    o3_ref[...] = o3
+    tokens = x_ref.shape[0]
+    each = tokens // size
+    here = pl.ds(pl.multiple_of(step * tokens, tokens), tokens)
+    keys, values, weights = [], [], []
+    for index in range(each):
+        own = pl.ds(pl.multiple_of((step * each + index) * LAT, LAT), LAT)
+        kx, vx = expand(k3_ref[own, :]), expand(v3_ref[own, :])
+        rows = slice(index * size, (index + 1) * size)
+        scores = (mm_nt(kx, q3_ref[rows]) * FACTOR).reshape(HEADS, LAT, size)
+        powers = jnp.exp(scores - jnp.max(scores, axis=1, keepdims=True))
+        shares = powers / jnp.sum(powers, axis=1, keepdims=True)
+        keys.append(kx)
+        values.append(vx)
+        weights.append(shares)
+    mixed = [narrow(mm_tn(narrow(w.reshape(HL, size)), v)) for w, v in zip(weights, values)]
+    o3 = jnp.concatenate(mixed, 0) if each > 1 else mixed[0]
+    o3_ref[here, :] = o3
     x1 = x_ref[...].astype(F32) + mm(o3, wo_ref[...])
     unit, inverse = norm_parts(x1)
     gain = norm_ref[4:5]
     h = narrow(unit * gain + norm_ref[9:10])
+    h_ref[...] = h
     e4 = cot_ref[...]
-    he_ref[0] = h
-    he_ref[1] = e4
     x2 = x1
     dh = jnp.zeros((tokens, D), F32)
     hidden = up_ref.shape[1]
@@ -254,14 +259,26 @@
     dx1 = e4.astype(F32) + norm_back(unit, inverse, gain, dh)
     dx1_ref[...] = dx1
     e3 = narrow(dx1)
-    e3_ref[...] = e3
+    e3_ref[here, :] = e3
     do3 = narrow(mm_nt(e3, wo_ref[...]))
-    dshares = mm_nt(vx, do3).reshape(HEADS, LAT, tokens)
-    inner = jnp.sum(shares * dshares, axis=1, keepdims=True)
-    dscores = narrow((shares * (dshares - inner)).reshape(HL, tokens))
-    dq3_ref[...] = narrow(mm_tn(dscores, kx) * FACTOR)
-    dv3_ref[...] = collapse(mm(shares_low, do3))
-    dk3_ref[...] = collapse(mm(dscores, q3)) * FACTOR
+    for index in range(each):
+        own = pl.ds(pl.multiple_of((step * each + index) * LAT, LAT), LAT)
+        place = pl.ds(pl.multiple_of((step * each + index) * size, size), size)
+        rows = slice(index * size, (index + 1) * size)
+        kx, vx, shares = keys[index], values[index], weights[index]
+        grad = do3[rows]
+        dshares = mm_nt(vx, grad).reshape(HEADS, LAT, size)
+        inner = jnp.sum(shares * dshares, axis=1, keepdims=True)
+        dscores = narrow((shares * (dshares - inner)).reshape(HL, size))
+        dq3_ref[place, :] = narrow(mm_tn(dscores, kx) * FACTOR)
+        dv3_ref[own, :] = narrow(collapse(mm(narrow(shares.reshape(HL, size)), grad))).astype(F32)
+        dk3_ref[own, :] = narrow(collapse(mm(dscores, q3_ref[rows])) * FACTOR).astype(F32)
+
+    @pl.when(step == pl.num_programs(0) - 1)
+    def _():
+        b3 = b3_ref[...]
+        put_units(core_ref, other_ref, mine_ref,
+                  [[(o3_ref, e3_ref), (b3, narrow(dk3_ref[...]))], [(b1_ref, dq3_ref), (b3, narrow(dv3_ref[...]))]])
 
 
 STAT = 2 * HEADS
@@ -269,12 +286,10 @@
 
 def latent_back_kernel(
     dk3_ref, dv3_ref, z2_ref, cot_ref, k2_ref, v2_ref, p2_ref, l2_ref, norm_ref, wk_ref, wv_ref, out_w_ref,
-    dk3_low_ref, dv3_low_ref, dz2_ref, e2_ref, send_ref, dq2_ref, gain_ref, shift_ref,
+    dz2_ref, e2_ref, send_ref, dq2_ref, gain_ref, shift_ref,
 ):
     dk3 = narrow(dk3_ref[...])
     dv3 = narrow(dv3_ref[...])
-    dk3_low_ref[...] = dk3
-    dv3_low_ref[...] = dv3
     upstream = mm_nt(dk3, wk_ref[...]) + mm_nt(dv3, wv_ref[...])
     unit, inverse = norm_parts(z2_ref[...])
     gain_ref[...] = fold_rows(upstream * unit)
@@ -318,6 +333,10 @@
     return mm_nt(narrow(jnp.where(chosen, 1.0, 0.0)), stats)
 
 
+def unit_grad(left, right, count):
+    return mm_tn(left[...], right[...]).reshape(count, D // count, D)
+
+
 def put_units(core_ref, other_ref, mine_ref, units):
     count = mine_ref.shape[0]
     rows = D // count
@@ -326,24 +345,14 @@
         def _():
             for ref, pairs in ((other_ref, units[1 - core]), (mine_ref, units[core])):
                 for index, (left, right) in enumerate(pairs):
-                    grad = narrow(mm_tn(left[...], right[...]).reshape(count, rows, D))
-                    ref[:, index * rows : (index + 1) * rows, :] = grad
-
-
-def early_kernel(
-    core_ref, o3_ref, e3_ref, b1_ref, dq3_ref, b3_ref, dk3_ref, dv3_ref, other_ref, mine_ref
-):
-    put_units(core_ref, other_ref, mine_ref,
-              [[(o3_ref, e3_ref), (b3_ref, dk3_ref)], [(b1_ref, dq3_ref), (b3_ref, dv3_ref)]])
-
-
-def late_kernel(
-    core_ref, b1_ref, dk1_ref, dv1_ref, a1_ref, dq1_ref, o1_ref, e1_ref, a2_ref, dq2_ref, o2_ref, e2_ref,
-    dk2_ref, dv2_ref, other_ref, mine_ref,
-):
-    put_units(core_ref, other_ref, mine_ref,
-              [[(b1_ref, dk1_ref), (a1_ref, dq1_ref), (a2_ref, dq2_ref), (o2_ref, e2_ref)],
-               [(b1_ref, dv1_ref), (o1_ref, e1_ref), (a2_ref, dk2_ref), (a2_ref, dv2_ref)]])
+                    ref[:, index * rows : (index + 1) * rows, :] = narrow(unit_grad(left, right, count))
+
+
+def cut_kernel(bit, pick_ref, keep_ref, got_ref, send_ref, stay_ref):
+    zero, one = halves(keep_ref[...].astype(F32) + got_ref[...].astype(F32), bit)
+    mine = pick_ref[0] == 0
+    send_ref[...] = narrow(jnp.where(mine, one, zero))
+    stay_ref[...] = narrow(jnp.where(mine, zero, one))
 
 
 def stage_kernel(parts, pick_ref, *refs):
@@ -408,39 +417,81 @@
             self_out_ref[...] = unit(zero, 3)
 
 
-def feed_kernel(which_ref, gd_ref, he_ref, out_ref):
+def feed_kernel(which_ref, gd_ref, h_ref, e4_ref, out_ref):
     part = pl.program_id(0)
     count, rows, _ = out_ref.shape
     slab = D // count
 
     @pl.when(which_ref[0] == 0)
     def _():
-        grad = narrow(mm_tn(he_ref[...], gd_ref[...]).reshape(count, slab, D))
+        grad = narrow(mm_tn(h_ref[...], gd_ref[...]).reshape(count, slab, D))
         out_ref[:, pl.ds(pl.multiple_of(part * slab, 8), slab), :] = grad
 
     @pl.when(which_ref[0] == 1)
     def _():
-        grad = narrow(mm_tn(gd_ref[...], he_ref[...]).reshape(D // rows, rows, D))
+        grad = narrow(mm_tn(gd_ref[...], e4_ref[...]).reshape(D // rows, rows, D))
         out_ref[pl.ds(part * (D // rows), D // rows)] = grad
 
 
-def inner_back_kernel(
-    piece0_ref, piece1_ref, piece2_ref, piece3_ref, q_all_ref, allowed_ref, k2_ref, v2_ref,
-    dq2_ref, z1_ref, dz2_ref, norm_ref, in_ref, out_w_ref, q1_ref, p1_ref, k1_ref, v1_ref,
-    dk2_ref, dv2_ref, dz1_ref, e1_ref, gain_ref, shift_ref, dq1_ref, dk1_ref, dv1_ref,
-    do1_ref,
+def halves(tensor, bit):
+    count, rows, cols = tensor.shape
+    cut = tensor.reshape(count >> (bit + 1), 2, 1 << bit, rows, cols)
+    return cut[:, 0].reshape(count // 2, rows, cols), cut[:, 1].reshape(count // 2, rows, cols)
+
+
+def feed_sum_kernel(
+    bits, which_ref, gd_ref, h_ref, e4_ref, got_up_ref, got_down_ref, send0_ref, stay0_ref, send1_ref, stay1_ref
+):
+    part = pl.program_id(0)
+    count, slab, _ = got_up_ref.shape
+    near, rows, _ = got_down_ref.shape
+    half = rows // 2
+    per_part = half // slab
+
+    def store(refs, index, value, bit):
+        zero, one = halves(value, bit)
+        mine = which_ref[1 + (0 if bit == bits[0] else 1)] == 0
+        refs[0][index] = narrow(jnp.where(mine, one, zero))
+        refs[1][index] = narrow(jnp.where(mine, zero, one))
+
+    pairs = ((send0_ref, stay0_ref), (send1_ref, stay1_ref))
+
+    @pl.when(which_ref[0] == 0)
+    def _():
+        grad = mm_tn(h_ref[...], gd_ref[...]).reshape(count, slab, D) + got_up_ref[...].astype(F32)
+        for index in range(2):
+            @pl.when(part // per_part == index)
+            def _():
+                place = pl.ds(pl.multiple_of(lax.rem(part, per_part) * slab, 8), slab)
+                store(pairs[index], (slice(None), place), grad, bits[index])
+
+    @pl.when(which_ref[0] == 1)
+    def _():
+        grad = mm_tn(gd_ref[...], e4_ref[...]).reshape(near, rows, D) + got_down_ref[...].astype(F32)
+        for index in range(2):
+            store(pairs[index], (pl.ds(part * (near // 2), near // 2),),
+                  grad[:, index * half : (index + 1) * half], bits[index])
+
+
+def tail_kernel(
+    core_ref, piece0_ref, piece1_ref, piece2_ref, piece3_ref, everyone_ref, allowed_ref, k2_ref, v2_ref,
+    dq2_ref, z1_ref, dz2_ref, norm_ref, self_in_ref, read_out_ref, q1_ref, p1_ref, k1_ref, v1_ref,
+    b1_ref, a1_ref, o1_ref, a2_ref, o2_ref, e2_ref,
+    other_ref, mine_ref, dk1_ref, dv1_ref, dq1_ref, dz1_ref, gain_ref, shift_ref,
+    do1_ref, e1_ref, dk2_ref, dv2_ref,
 ):
     step = pl.program_id(0)
+    last = pl.num_programs(0) - 1
 
     @pl.when(step == 0)
     def _():
         count = dq2_ref.shape[0]
-        half, total = count // 2, q_all_ref.shape[0]
+        half, everything = count // 2, everyone_ref.shape[0]
 
         def own_rows(ref):
-            return jnp.concatenate([ref[:half], ref[total // 2 : total // 2 + half]], 0).astype(F32)
-
-        q_all = q_all_ref[...]
+            return jnp.concatenate([ref[:half], ref[everything // 2 : everything // 2 + half]], 0).astype(F32)
+
+        q_all = narrow(mm(everyone_ref[...], self_in_ref[0]))
         spread = gathered((piece0_ref, piece1_ref, piece2_ref, piece3_ref))
         do_all = spread[:, :D]
         stats = spread[:, D:]
@@ -454,7 +505,9 @@
         dk2 = narrow(collapse(mm(dscores, q_all)) * FACTOR)
         dk2_ref[...] = dk2
         dv2_ref[...] = dv2
-        upstream = mm_nt(dq2_ref[...], in_ref[0]) + mm_nt(dk2, in_ref[1]) + mm_nt(dv2, in_ref[2])
+        upstream = (
+            mm_nt(dq2_ref[...], self_in_ref[0]) + mm_nt(dk2, self_in_ref[1]) + mm_nt(dv2, self_in_ref[2])
+        )
         unit, inverse = norm_parts(z1_ref[...])
         gain_ref[...] = fold_rows(upstream * unit)
         shift_ref[...] = fold_rows(upstream)
@@ -462,7 +515,7 @@
         dz1_ref[...] = dz1
         e1 = narrow(dz1)
         e1_ref[...] = e1
-        do1_ref[...] = narrow(mm_nt(e1, out_w_ref[...])).astype(F32)
+        do1_ref[...] = narrow(mm_nt(e1, read_out_ref[...])).astype(F32)
 
     own = pl.ds(pl.multiple_of(step * LAT, LAT), LAT)
     qx = expand(q1_ref[own, :])
@@ -471,9 +524,20 @@
     dshares = mm_nt(dox, v1_ref[...])
     inner = jnp.sum(shares * dshares, axis=-1, keepdims=True)
     dscores = narrow(shares * (dshares - inner))
-    dv1_ref[...] = narrow(mm_tn(narrow(shares), dox))
-    dk1_ref[...] = narrow(mm_tn(dscores, qx) * FACTOR)
+    size = k1_ref.shape[0]
+    here = pl.ds(pl.multiple_of(step * size, size), size)
+    dv1 = narrow(mm_tn(narrow(shares), dox))
+    dk1 = narrow(mm_tn(dscores, qx) * FACTOR)
+    dv1_ref[here, :] = dv1
+    dk1_ref[here, :] = dk1
     dq1_ref[own, :] = collapse(mm(dscores, k1_ref[...])) * FACTOR
+
+    @pl.when(step == last)
+    def _():
+        dq1 = narrow(dq1_ref[...])
+        put_units(core_ref, other_ref, mine_ref,
+                  [[(b1_ref, dk1_ref), (a1_ref, dq1), (a2_ref, dq2_ref), (o2_ref, e2_ref)],
+                   [(b1_ref, dv1_ref), (o1_ref, e1_ref), (a2_ref, dk2_ref), (a2_ref, dv2_ref)]])
 
 
 def input_back_kernel(
@@ -611,25 +675,33 @@
         self.parts = parts
         self.send()
 
+    def begin_cut(self, parts):
+        self.parts = []
+        for (sent, stay, rows), left, order in zip(parts, self.left, self.orders):
+            bit = order[0]
+            left.remove(bit)
+            self.parts.append((stay, swap(self.line.gate(sent), "blk", bit, self.count), rows, 0))
+        self.step += 1
+
     def send(self):
         if self.step == len(self.orders[0]) - 1 and len({order[-1] for order in self.orders}) == 1:
             self.send_last()
             return
         lead = (self.count >> self.step) // 2
         picks, in_specs, operands, out_specs, out_shape, bits = [], [], [], [], [], []
-        for (kept, got, rows, block), left, order in zip(self.parts, self.left, self.orders):
-            bit = order[self.step]
-            place = left.index(bit)
-            left.pop(place)
+        for left, order in zip(self.left, self.orders):
+            bits.append((order[self.step], left.index(order[self.step])))
+            left.remove(order[self.step])
+        for (kept, got, rows, block), (bit, place) in zip(self.parts, bits):
             inner = lead >> place
             picks.append(own_bit(bit))
-            bits.append(bit)
             spec = pl.BlockSpec(
                 (None, 2, None, rows, D),
                 lambda i, inner=inner, block=block: (i // inner, 0, i % inner, block, 0),
             )
             in_specs += [spec, spec]
-            operands += [t.reshape(lead // inner, 2, inner, -1, D) for t in (kept, got)]
+            kept, got = (t.reshape(lead // inner, 2, inner, -1, D) for t in (kept, got))
+            operands += [in_hbm(kept), in_hbm(got)] if self.step == 0 else [kept, got]
             out_specs += [pl.BlockSpec((None, rows, D), lambda i: (i, 0, 0))] * 2
             out_shape += [shaped((lead, rows, D), BF)] * 2
         moved = sum(3 * 4 * lead * part[2] * D for part in self.parts)
@@ -637,10 +709,11 @@
             functools.partial(stage_kernel, len(self.parts)), (lead,),
             [pl.BlockSpec(memory_space=pltpu.SMEM)] + in_specs, out_specs, out_shape, 0, moved, vmem=10,
         )(*self.line.gate((jnp.stack(picks).astype(jnp.int32), *operands)))
+        cut = [(sent, stay, part[2]) for sent, stay, part in zip(out[::2], out[1::2], self.parts)]
         self.line.note(out)
-        got = [swap(sent, "blk", bit, self.count) for sent, bit in zip(out[::2], bits)]
         self.parts = [
-            (stay, arrived, part[2], 0) for stay, arrived, part in zip(out[1::2], got, self.parts)
+            (stay, swap(sent, "blk", bit, self.count), rows, 0)
+            for (sent, stay, rows), (bit, _) in zip(cut, bits)
         ]
         self.step += 1
 
@@ -741,110 +814,126 @@
             unit_flops * 2, 10 * D * D * 2,
         )(group_image, places, own_at, *pieces, a2, z1, norms, self_in, self_out, write_in, write_in)
 
+        resident = pl.BlockSpec(memory_space=pltpu.VMEM)
         pair_spec = pl.BlockSpec((2, size, D), lambda g: (0, g, 0))
-        out_patches, he, gd, o3, e3, dq3, dx1, dk3, dv3, gain4, shift4 = call(
-            functools.partial(patch_kernel, D), grid,
-            [patch_spec, patch_spec, patch_spec, lat_spec, lat_spec, norm_spec, square,
-             whole((D, hidden)), whole((hidden, D))],
-            [patch_spec, pair_spec, pl.BlockSpec((2, size, hidden), lambda g: (0, g, 0)), patch_spec, patch_spec,
-             patch_spec, patch_spec, rows_of((LAT, D)), rows_of((LAT, D)), fold_spec, fold_spec],
-            [low_patch, shaped((2, tokens, D), BF), shaped((2, tokens, hidden), BF),
-             low_patch, low_patch, low_patch, shaped((tokens, D), F32), full_lat, full_lat, fold, fold],
-            unit_flops * 20, 40 * tokens * D, vmem=40,
-        )(in_hbm(x), in_hbm(q3), in_hbm(cot), k3, v3, norms, write_out, feed_up, feed_down)
+        early_shape = (n_blk, 2 * rows, D)
+        each = 1
+        spans = rows_of((each * size, D))
+        out_patches, h, gd, dq3, dx1, dk3, dv3, early_other, early_mine, gain4, shift4 = call(
+            functools.partial(patch_kernel, D, size), (groups // each,),
+            [smem] + [spans, spans, spans, lat_spec, lat_spec, norm_spec, square,
+             resident, resident, whole((tokens, D)), lat_spec],
+            [spans, spans,
+             pl.BlockSpec((2, each * size, hidden), lambda g: (0, g, 0), pipeline_mode=pl.Buffered(1 if each > 1 else 2)),
+             whole((tokens, D)), spans, lat_spec, lat_spec, whole(early_shape), whole(early_shape), fold_spec, fold_spec],
+            [low_patch, low_patch, shaped((2, tokens, hidden), BF),
+             low_patch, shaped((tokens, D), F32), full_lat, full_lat, shaped(early_shape, BF), shaped(early_shape, BF),
+             fold, fold],
+            unit_flops * 22, 40 * tokens * D, [pltpu.VMEM((tokens, D), BF)] * 2, vmem=46,
+        )(core_at, in_hbm(x), in_hbm(q3), in_hbm(cot), k3, v3, norms, write_out, feed_up, feed_down, in_hbm(b1), b3)
 
         width = D + 128
-        dk3, dv3, dz2, e2, payload, dq2, gain3, shift3 = call(
+        dz2, e2, payload, dq2, gain3, shift3 = call(
             latent_back_kernel, (1,),
             [lat_spec] * 4 + [whole((total, D))] * 2
             + [whole((hl2, total)), whole((hl2, 1)), norm_spec, one_of(1), one_of(2), square],
-            [lat_spec] * 4 + [whole((lat, width)), lat_spec, fold_spec, fold_spec],
-            [low_lat, low_lat, full_lat, low_lat, shaped((lat, width), BF), low_lat, fold, fold],
+            [lat_spec] * 2 + [whole((lat, width)), lat_spec, fold_spec, fold_spec],
+            [full_lat, low_lat, shaped((lat, width), BF), low_lat, fold, fold],
             unit_flops, 10 * D * D,
         )(dk3, dv3, z2, cot_z, k2, v2, p2, l2, norms, write_in, write_in, self_out)
         line.note(payload)
 
-        def feed_grad(which):
+        feed_specs = [
+            pl.BlockSpec((None, tokens, D), lambda j, w: (w[0], 0, j)),
+            pl.BlockSpec((tokens, D), lambda j, w: (0, 0), pipeline_mode=pl.Buffered(1)),
+            pl.BlockSpec((tokens, D), lambda j, w: (0, 0), pipeline_mode=pl.Buffered(1)),
+        ]
+
+        def feed_call(kernel, in_specs, out_specs, out_shape, operands):
             return pl.pallas_call(
-                feed_kernel,
+                kernel,
                 grid_spec=pltpu.PrefetchScalarGridSpec(
-                    num_scalar_prefetch=1,
-                    grid=(hidden // D,),
-                    in_specs=[
-                        pl.BlockSpec((None, tokens, D), lambda j, w: (w[0], 0, j)),
-                        pl.BlockSpec((None, tokens, D), lambda j, w: (w[0], 0, 0), pipeline_mode=pl.Buffered(1)),
-                    ],
-                    out_specs=pl.BlockSpec((n_blk, feed_rows, D), lambda j, w: (0, 0, 0), pipeline_mode=pl.Buffered(1)),
+                    num_scalar_prefetch=1, grid=(hidden // D,), in_specs=in_specs, out_specs=out_specs
                 ),
-                out_shape=shaped((n_blk, feed_rows, D), BF),
+                out_shape=out_shape,
                 compiler_params=pltpu.CompilerParams(
-                    vmem_limit_bytes=20 << 20, dimension_semantics=("arbitrary",)
+                    vmem_limit_bytes=24 << 20, dimension_semantics=("arbitrary",)
                 ),
                 cost_estimate=pl.CostEstimate(
                     flops=unit_flops * 4, bytes_accessed=20 * tokens * D, transcendentals=0
                 ),
-            )(*line.gate((which, in_hbm(gd), in_hbm(he))))
+            )(*line.gate(operands))
+
+        def once(shape):
+            return pl.BlockSpec(shape, lambda j, w: (0,) * len(shape), pipeline_mode=pl.Buffered(1))
+
+        gd, h, e4 = in_hbm(gd), in_hbm(h), in_hbm(cot)
+        half = feed_rows // 2
+        first = Scatter(line, n_blk, orders)
+        firsts = (orders[0][0], orders[1][0])
+
+        def feed_other():
+            shape = (n_blk, feed_rows, D)
+            return feed_call(feed_kernel, feed_specs, once(shape), shaped(shape, BF), (other_at, gd, h, e4))
+
+        def feed_mine(got):
+            which = jnp.stack([core, own_bit(firsts[0]), own_bit(firsts[1])]).astype(jnp.int32)
+            near = D // feed_rows
+            shape = (n_blk // 2, half, D)
+            return feed_call(
+                functools.partial(feed_sum_kernel, firsts),
+                feed_specs
+                + [pl.BlockSpec((n_blk, rows, D), lambda j, w: (0, j, 0)),
+                   pl.BlockSpec((near, feed_rows, D), lambda j, w: (j, 0, 0))],
+                [once(shape)] * 4, [shaped(shape, BF)] * 4, (which, gd, h, e4, got, got),
+            )
 
         whole_patch = whole((tokens, D))
-
-        def unit_grads(kernel, patch_sized, lat_sized, count):
-            return call(
-                kernel, (1,),
-                [smem] + [whole_patch] * len(patch_sized) + [lat_spec] * len(lat_sized),
-                [whole((n_blk, count * rows, D))] * 2, [shaped((n_blk, count * rows, D), BF)] * 2,
-                unit_flops, 8 * tokens * D,
-            )(*line.gate((core_at, *patch_sized, *lat_sized)))
 
         def core_swap(tensor):
             return swap(line.gate(tensor), "rep", 0, n_rep)
 
         early = {}
-        first = Scatter(line, n_blk, orders)
 
         def fill_second(step):
             if step == 0:
-                early["feed_other"] = feed_grad(other_at)
-                return early["feed_other"]
+                early["got"] = core_swap(early_other)
+                early["feed_other"] = feed_other()
+                return early["feed_other"], early["got"]
             if step == 1:
                 early["feed_got"] = core_swap(early["feed_other"])
-                early["feed_mine"] = feed_grad(core_at)
-                return early["feed_mine"], early["feed_got"]
+                bit = orders[2][0]
+                shape = (n_blk // 2, 2 * rows, D)
+                early["sum"] = call(
+                    functools.partial(cut_kernel, bit), (1,), [smem] + [whole(early_shape)] * 2,
+                    [whole(shape)] * 2, [shaped(shape, BF)] * 2, 0, 12 * tokens * D,
+                )(*line.gate((own_bit(bit).reshape(1).astype(jnp.int32), early_mine, early["got"])))
+                return early["sum"], early["feed_got"]
             if step == 2:
-                early["other"], early["mine"] = unit_grads(early_kernel, (o3, e3, b1, dq3), (b3, dk3, dv3), 2)
-                return early["mine"]
-            early["got"] = core_swap(early["other"])
-            early["q2_all"] = narrow(mm(line.gate(a2_all), self_in[0]))
-            return early["q2_all"], early["got"]
+                early["feed"] = feed_mine(early["feed_got"])
+                return early["feed"]
+            return None
 
         spread_pieces = gather_rows(payload, n_blk, line, fill_second)
-        half = feed_rows // 2
-        first.begin([
-            (early["feed_mine"], early["feed_got"], half, 0),
-            (early["feed_mine"], early["feed_got"], half, 1),
-            (early["mine"], early["got"], 2 * rows, 0),
-        ])
-
-        dk2, dv2, dz1, e1, gain2, shift2, dq1, dk1, dv1 = call(
-            inner_back_kernel, grid,
-            [whole(piece_shape + (width,))] * 4 + [whole((total, D)), whole((hl2, total))]
-            + [whole((total, D))] * 2 + [lat_spec] * 3 + [norm_spec, three, square, lat_spec, share_spec]
-            + [patch_spec] * 2,
-            [lat_spec] * 4 + [fold_spec] * 2 + [lat_spec] + [patch_spec] * 2,
-            [low_lat, low_lat, full_lat, low_lat, fold, fold, full_lat, low_patch, low_patch],
-            2 * unit_flops, 10 * tokens * D,
-            [pltpu.VMEM((lat, D), F32)],
-        )(*line.gate((*spread_pieces, early["q2_all"], allowed, k2, v2,
-                      dq2, z1, dz2, norms, self_in, read_out, q1, in_hbm(p1), in_hbm(k1), in_hbm(v1))))
-        line.note((dk1, first.flying()))
-        first.send()
-
-        late_other, late_mine = unit_grads(
-            late_kernel, (b1, dk1, dv1), (a1, narrow(dq1), o1, e1, a2, dq2, o2, e2, dk2, dv2), 4
-        )
-        line.note((late_mine, first.flying()))
+        feed0, feed1, feed2, feed3 = early["feed"]
+        first.begin_cut([(feed0, feed1, half), (feed2, feed3, half), (*early["sum"], 2 * rows)])
+
+        late_shape = (n_blk, 4 * rows, D)
+        late_other, late_mine, dk1, dv1, dq1, dz1, gain2, shift2 = call(
+            tail_kernel, grid,
+            [smem] + [whole(piece_shape + (width,))] * 4
+            + [whole((total, D)), whole((hl2, total)), whole((total, D)), whole((total, D))] + [lat_spec] * 3
+            + [norm_spec, three, square, lat_spec, share_spec, patch_spec, patch_spec, whole_patch] + [lat_spec] * 5,
+            [whole(late_shape)] * 2 + [whole_patch] * 2 + [lat_spec] * 2 + [fold_spec] * 2,
+            [shaped(late_shape, BF), shaped(late_shape, BF), low_patch, low_patch, full_lat, full_lat, fold, fold],
+            4 * unit_flops, 30 * tokens * D,
+            [pltpu.VMEM((lat, D), F32)] + [pltpu.VMEM((lat, D), BF)] * 3,
+            vmem=40,
+        )(*line.gate((core_at, *spread_pieces, a2_all, allowed, k2, v2, dq2, z1, dz2, norms, self_in, read_out,
+                      q1, in_hbm(p1), in_hbm(k1), in_hbm(v1), b1, a1, o1, a2, o2, e2)))
+        line.note((late_other, first.flying()))
         late_got = core_swap(late_other)
         first.send()
-
         dx, dz, norm_grads = call(
             input_back_kernel, grid,
             [patch_spec] * 5 + [lat_spec] * 3 + [norm_spec, three, one_of(0)] + [fold_spec] * 6,
@@ -854,13 +943,15 @@
             [pltpu.VMEM((8, D), F32)] * 2,
         )(*line.gate((in_hbm(x), in_hbm(dx1), in_hbm(dq3), dk1, dv1, z, dz1, dq1, norms, read_in, write_in,
                       gain2, shift2, gain3, shift3, gain4, shift4)))
-        norm_got = swap(norm_grads, "rep", 0, n_rep)
         line.note((dx, late_got, first.flying()))
+        first.send()
+        norm_got = swap(line.gate(norm_grads), "rep", 0, n_rep)
+        line.note((norm_got, first.flying()))
+        norm_grads = norm_grads + norm_got
+        first.send()
         last = Scatter(line, n_blk, orders)
         last_rows = 4 * rows // 3
         last.begin([(late_mine, late_got, last_rows, i) for i in range(3)])
-        first.send()
-        norm_grads = norm_grads + norm_got
         for bit in range(1, rep_bits):
             norm_grads = norm_grads + swap(line.gate(norm_grads), "rep", bit, n_rep)
         bits = bits_of(n_blk)

time: 297 us -> 284 us (0.956)
  local copies, waits for them, and re-layouts: 32.3 us -> 14 us
  Pallas kernels: 118 us -> 127 us
  waiting for transfers between devices: 88.3 us -> 80.5 us
  starting transfers between devices: 41.2 us -> 47.7 us
    unnamed x176 -> x136, local copies, waits for them, and re-layouts: 31.4 us -> 13.2 us
    pallas_call x6 -> x5, Pallas kernels: 73 us -> 87.5 us  [the longest x1 45.2 us: body(): call(functools.partial(patch_kernel, D, size), (groups // each,), [smem]...]
    ppermute x42, waiting for transfers between devices: 88.3 us -> 80.5 us  [swap(): return lax.ppermute(tensor, axis, [(i, i ^ 1 << bit) for i in range(count)])]
    ppermute x42, starting transfers between devices: 41.2 us -> 47.7 us  [swap(): return lax.ppermute(tensor, axis, [(i, i ^ 1 << bit) for i in range(count)])]
    pallas_call x6 -> x5, Pallas kernels: 17.1 us -> 11.7 us  [send(): call(functools.partial(stage_kernel, len(self.parts)), (lead,), [pl.Block...]
  transfers between devices with their start and end apart: 42 -> 42, of which waited for: 20 -> 25; matrix products, arithmetic and copies ran while one was open for 3% -> 2% of each run, Pallas kernels for 15% -> 19%
where the time goes in v3:
time: 284 us; the launch traced here: 279 us
  Pallas kernels  127 us (45%)
  waiting for transfers between devices  80.5 us (28%)
  starting transfers between devices  47.7 us (17%)
  local copies, waits for them, and re-layouts  14 us (5%)
  other arithmetic  5.26 us (2%)
    ppermute x42, waiting for transfers between devices, swap(): return lax.ppermute(tensor, axis, [(i, i ^ 1 << bit) for i in range(count)])  80.5 us
    ppermute x42, starting transfers between devices, swap(): return lax.ppermute(tensor, axis, [(i, i ^ 1 << bit) for i in range(count)])  47.7 us
    pallas_call x1, Pallas kernels, body(): call(functools.partial(patch_kernel, D, size), (groups // each,), [smem]...  45.2 us
    pallas_call x2, Pallas kernels, feed_call(): pl.pallas_call(kernel, grid_spec=pltpu.PrefetchScalarGridSpec(num_scalar_...  22.9 us
    pallas_call x1, Pallas kernels, body(): call(tail_kernel, grid, [smem] + [whole(piece_shape + (width,))] * 4 + [w...  17.8 us
    unnamed x136, local copies, waits for them, and re-layouts  13.2 us
    pallas_call x5, Pallas kernels, send(): call(functools.partial(stage_kernel, len(self.parts)), (lead,), [pl.Block...  11.7 us
    pallas_call x1, Pallas kernels, body(): call(read_forward_kernel, grid, [patch_spec, lat_spec, norm_spec, three,...  9.58 us
  transfers between devices with their start and end apart: 42, of which 25 were waited for; matrix products, arithmetic and copies ran while one was open for 2% of the time, Pallas kernels for 19%

profile of v3, /device:TPU:0, one launch (start us, length us, event | category | flops | bytes accessed | tf_op | source)
XLA Modules:
  0.0 278.7 jit_solution(4230084277651680226)
XLA Ops:
  2.4 9.6 %shard_map.272 = (bf16[32,768]{1,0:T(8,128)(2,1)S(1)}, f32[32,768]{1,0:T(8,128)S(1)}, bf16[1024,768]{1,0:T(8,128)(2,1)S(1)}, bf16[1024,768]{1,0:T(8,128)(2,1)S(1...) custom-call(bf16[1024,768]{1,0:T(8,128)(2,1)} %bitcast.119, ...), custom_call_target="tpu_custom_call" | custom-call | flops 2415919104 | bytes 9437184 | tf_op jit(solution)/shard_map/pallas_call | solution.py:778
  12.0 4.1 %collective-permute-start = (bf16[32,768]{1,0:T(8,128)(2,1)S(1)}, bf16[32,768]{1,0:T(8,128)(2,1)S(1)}, u32[]{:S(2)}, u32[]{:S(2)}) collective-permute-start(bf16[32,768]{1,0:T(8,128)(2,1)S(1)} %get-tuple-element.335.a2_ref), channel_id=1, source_target_pairs={{0,16},{2,18},{4,20},{6,22},{8,24},{10,26},{12,28},{14,30},{16,0},... | collective-permute-start | bytes 147464 | tf_op jit(solution)/shard_map/ppermute | solution.py:592
  16.2 2.5 convolution_convert_fusion.q3_ref
  19.5 1.6 collective-permute-start.1
  21.1 3.3 %collective-permute-done.1 = bf16[2,32,768]{2,1,0:T(8,128)(2,1)} collective-permute-done((bf16[2,32,768]{2,1,0:T(8,128)(2,1)}, bf16[2,32,768]{2,1,0:T(8,128)(2,1)}, u32[]{:S(2)}, u32[]{:S(2)}) %collective-permute-start.1) | collective-permute-done | bytes 98336 | tf_op jit(solution)/shard_map/ppermute | solution.py:592
  25.3 1.8 collective-permute-start.2
  27.1 1.5 collective-permute-start.3
  28.5 1.4 collective-permute-done.2
  30.0 2.0 collective-permute-done.3
  32.1 1.7 collective-permute-start.4
  33.8 3.9 %collective-permute-done.5 = bf16[2,2,2,16,768]{4,3,0,1,2:T(8,128)(2,1)S(1)} collective-permute-done((bf16[2,2,2,16,768]{4,3,0,1,2:T(8,128)(2,1)S(1)}, bf16[2,2,2,16,768]{4,3,0,1,2:T(8,128)(2,1)S(1)}, u32[]{:S(2)}, u32[]{:S(2)}) %collective-permute-start.5) | collective-permute-done | bytes 196640 | tf_op jit(solution)/shard_map/ppermute | solution.py:592
  37.9 2.0 copy-done.4
  39.9 4.2 %shard_map.273 = (bf16[512,768]{1,0:T(8,128)(2,1)S(1)}, f32[384,512]{1,0:T(8,128)S(1)}, bf16[512,768]{1,0:T(8,128)(2,1)S(1)}, bf16[512,768]{1,0:T(8,128)(2,1)S(1...) custom-call(s32[1,64]{1,0:T(1,128)S(1)} %copy-done.38, ...), custom_call_target="tpu_custom_call" | custom-call | flops 2415919104 | bytes 11796480 | tf_op jit(solution)/shard_map/pallas_call | solution.py:805
  46.5 45.2 %shard_map.274 = (bf16[1024,768]{1,0:T(8,128)(2,1)}, bf16[1024,768]{1,0:T(8,128)(2,1)S(1)}, bf16[2,1024,3072]{2,1,0:T(8,128)(2,1)}, bf16[1024,768]{1,0:T(8,128)(...) custom-call(s32[1]{0:T(128)} %bitcast.core_ref, ...), custom_call_target="tpu_custom_call" | custom-call | flops 26575110144 | bytes 31457280 | tf_op jit(solution)/shard_map/pallas_call | solution.py:822
  91.8 2.5 shard_map.275
  96.2 2.7 collective-permute-start.6
  98.9 10.4 %shard_map.276 = bf16[16,192,768]{2,1,0:T(8,128)(2,1)} custom-call(s32[1]{0:T(128)S(6)} %sub.3.which_ref, bf16[2,1024,3072]{2,1,0:T(8,128)(2,1)} %get-tuple-element.290.gd_ref, bf16[1024,768]{1,0:T(8,128)(2,1)} %copy-done.1, bf16[1024,768]{1,0:T(8,128)(2,1)} %bitcast.117), custom_call_target="tpu_custom_call" | custom-call | flops 4831838208 | bytes 15728640 | tf_op jit(solution)/shard_map/pallas_call | solution.py:853
  111.6 2.1 collective-permute-start.8
  113.8 1.7 copy-done.6
  115.5 1.7 copy-done.8
  117.1 1.6 shard_map.277
  119.7 2.0 collective-permute-start.10
  121.7 1.5 collective-permute-start.11
  123.2 12.6 %shard_map.278 = (bf16[8,96,768]{2,1,0:T(8,128)(2,1)}, bf16[8,96,768]{2,1,0:T(8,128)(2,1)S(1)}, bf16[8,96,768]{2,1,0:T(8,128)(2,1)}, bf16[8,96,768]{2,1,0:T(8,128)(2,1)S(1)}) custom-call(s32[3]{0:T(128)S(1)} %add_add_fusion.which_ref, bf16[2,1024,3072]{2,1,0:T(8,128)(2,1)} %get-tuple-element.290.gd_ref, bf16[1024,768]{1,0:T(8,128)(2,1)} %copy-done.1, ...), custom_call_target="tpu_custom_call" | custom-call | flops 4831838208 | bytes 15728640 | tf_op jit(solution)/shard_map/pallas_call | solution.py:853
  136.7 6.0 %collective-permute-done.13 = bf16[2,2,2,16,896]{4,3,0,1,2:T(8,128)(2,1)S(1)} collective-permute-done((bf16[2,2,2,16,896]{4,3,0,1,2:T(8,128)(2,1)S(1)}, bf16[2,2,2,16,896]{4,3,0,1,2:T(8,128)(2,1)S(1)}, u32[]{:S(2)}, u32[]{:S(2)}) %collective-permute-start.13) | collective-permute-done | bytes 229408 | tf_op jit(solution)/shard_map/ppermute | solution.py:592
  143.3 1.7 collective-permute-start.15
  145.0 1.6 collective-permute-start.16
  146.8 17.8 %shard_map.279 = (bf16[16,192,768]{2,1,0:T(8,128)(2,1)}, bf16[16,192,768]{2,1,0:T(8,128)(2,1)}, bf16[1024,768]{1,0:T(8,128)(2,1)S(1)}, bf16[1024,768]{1,0:T(8,12...) custom-call(s32[1]{0:T(128)} %bitcast.core_ref, ...), custom_call_target="tpu_custom_call" | custom-call | flops 4831838208 | bytes 23592960 | tf_op jit(solution)/shard_map/pallas_call | solution.py:922
  165.8 3.3 %collective-permute-done.14 = bf16[8,96,768]{2,1,0:T(8,128)(2,1)S(1)} collective-permute-done((bf16[8,96,768]{2,1,0:T(8,128)(2,1)}, bf16[8,96,768]{2,1,0:T(8,128)(2,1)S(1)}, u32[]{:S(2)}, u32[]{:S(2)}) %collective-permute-start.14) | collective-permute-done | bytes 1179680 | tf_op jit(solution)/shard_map/ppermute | solution.py:592
  170.6 1.9 shard_map.280
  173.2 1.7 collective-permute-start.18
  175.0 1.5 collective-permute-start.19
  176.6 8.5 %shard_map.281 = (bf16[1024,768]{1,0:T(8,128)(2,1)}, bf16[32,768]{1,0:T(8,128)(2,1)}, f32[16,768]{1,0:T(8,128)}) custom-call(bf16[1024,768]{1,0:T(8,128)(2,1)} %bitcast.121, f32[1024,768]{1,0:T(8,128)} %get-tuple-element.366.dx1_ref, bf16[1024,768]{1,0:T(8,128)(2,1)} %copy-done.9, bf16[1024,768]{1,0:T(8,128)(2,1)S(1)} %get-tuple-element.368.dk1_ref, ...), custom_call_target="tpu_custom_call" | custom-call | flops 3623878656 | bytes 11010048 | tf_op jit(solution)/shard_map/pallas_call | solution.py:937
  185.1 3.2 %collective-permute-done.17 = bf16[4,96,768]{2,1,0:T(8,128)(2,1)S(1)} collective-permute-done((bf16[4,96,768]{2,1,0:T(8,128)(2,1)S(1)}, bf16[4,96,768]{2,1,0:T(8,128)(2,1)S(1)}, u32[]{:S(2)}, u32[]{:S(2)}) %collective-permute-start.17) | collective-permute-done | bytes 589856 | tf_op jit(solution)/shard_map/ppermute | solution.py:592
  188.7 1.5 collective-permute-done.19
  191.5 1.5 collective-permute-start.23
  195.9 3.4 %collective-permute-done.22.refs_1_ = bf16[2,96,768]{2,1,0:T(8,128)(2,1)S(1)} collective-permute-done((bf16[2,96,768]{2,1,0:T(8,128)(2,1)S(1)}, bf16[2,96,768]{2,1,0:T(8,128)(2,1)S(1)}, u32[]{:S(2)}, u32[]{:S(2)}) %collective-permute-start.22) | collective-permute-done | bytes 294944 | tf_op jit(solution)/shard_map/ppermute | solution.py:592
  201.0 6.5 %shard_map.284 = (bf16[8,64,768]{2,1,0:T(8,128)(2,1)S(1)}, bf16[8,64,768]{2,1,0:T(8,128)(2,1)S(1)}, bf16[8,64,768]{2,1,0:T(8,128)(2,1)S(1)}, bf16[8,64,768]{2,1,...) custom-call(s32[3]{0:T(128)S(1)} %pad_add_fusion.1.pick_ref, ...), custom_call_target="tpu_custom_call" | custom-call | bytes 14155776 | tf_op jit(solution)/shard_map/pallas_call | solution.py:708
  209.5 1.4 collective-permute-start.28
  212.1 1.5 collective-permute-start.25
  213.6 12.4 %collective-permute-done.25 = f32[16,768]{1,0:T(8,128)S(1)} collective-permute-done((f32[16,768]{1,0:T(8,128)S(1)}, f32[16,768]{1,0:T(8,128)S(1)}, u32[]{:S(2)}, u32[]{:S(2)}) %collective-permute-start.25) | collective-permute-done | bytes 49184 | tf_op jit(solution)/shard_map/ppermute | solution.py:592
  226.0 8.4 %collective-permute-done.29.got_ref = bf16[288,768]{1,0:T(8,128)(2,1)S(1)} collective-permute-done((bf16[288,768]{1,0:T(8,128)(2,1)S(1)}, bf16[288,768]{1,0:T(8,128)(2,1)S(1)}, u32[]{:S(2)}, u32[]{:S(2)}) %collective-permute-start.29) | collective-permute-done | bytes 442400 | tf_op jit(solution)/shard_map/ppermute | solution.py:592
  238.5 1.5 collective-permute-start.33
  242.7 7.2 %collective-permute-done.30 = f32[16,768]{1,0:T(8,128)S(1)} collective-permute-done((f32[16,768]{1,0:T(8,128)S(1)}, f32[16,768]{1,0:T(8,128)S(1)}, u32[]{:S(2)}, u32[]{:S(2)}) %collective-permute-start.30) | collective-permute-done | bytes 49184 | tf_op jit(solution)/shard_map/ppermute | solution.py:592
  252.0 1.5 collective-permute-start.37
  255.3 3.6 %collective-permute-done.35 = f32[16,768]{1,0:T(8,128)S(1)} collective-permute-done((f32[16,768]{1,0:T(8,128)S(1)}, f32[16,768]{1,0:T(8,128)S(1)}, u32[]{:S(2)}, u32[]{:S(2)}) %collective-permute-start.35) | collective-permute-done | bytes 49184 | tf_op jit(solution)/shard_map/ppermute | solution.py:592
  259.2 2.1 collective-permute-start.40
  262.2 13.5 %collective-permute-done.39 = f32[16,768]{1,0:T(8,128)S(1)} collective-permute-done((f32[16,768]{1,0:T(8,128)S(1)}, f32[16,768]{1,0:T(8,128)S(1)}, u32[]{:S(2)}, u32[]{:S(2)}) %collective-permute-start.39) | collective-permute-done | bytes 49184 | tf_op jit(solution)/shard_map/ppermute | solution.py:592
  (224 shorter events, 40.3 us)
Async XLA Ops:
  12.0 6.7 %collective-permute-start = (bf16[32,768]{1,0:T(8,128)(2,1)S(1)}, bf16[32,768]{1,0:T(8,128)(2,1)S(1)}, u32[]{:S(2)}, u32[]{:S(2)}) collective-permute-start(bf16[32,768]{1,0:T(8,128)(2,1)S(1)} %get-tuple-element.335.a2_ref), channel_id=1, source_target_pairs={{0,16},{2,18},{4,20},{6,22},{8,24},{10,26},{12,28},{14,30},{16,0},... | collective-permute-start | bytes 147464 | tf_op jit(solution)/shard_map/ppermute | solution.py:592
  19.5 4.9 %collective-permute-start.1 = (bf16[2,32,768]{2,1,0:T(8,128)(2,1)}, bf16[2,32,768]{2,1,0:T(8,128)(2,1)}, u32[]{:S(2)}, u32[]{:S(2)}) collective-permute-start(bf16[2,32,768]{2,1,0:T(8,128)(2,1)} %get-tuple-element.249), channel_id=1, source_target_pairs={{0,8},{2,10},{4,12},{6,14},{8,0},{10,2},{12,4},{14,6},{16,24},{18,... | collective-permute-start | bytes 294920 | tf_op jit(solution)/shard_map/ppermute | solution.py:592
  25.3 4.7 %collective-permute-start.2 = (bf16[2,2,16,768]{3,2,0,1:T(8,128)(2,1)S(1)}, bf16[2,2,16,768]{3,2,0,1:T(8,128)(2,1)S(1)}, u32[]{:S(2)}, u32[]{:S(2)}) collective-permute-start(bf16[2,2,16,768]{3,2,0,1:T(8,128)(2,1)S(1)} %get-tuple-element.250), channel_id=1, source_target_pairs={{0,4},{2,6},{4,0},{6,2},{8,12},{10,14},{12,8},{14,10},{16,20},{18,... | collective-permute-start | bytes 294920 | tf_op jit(solution)/shard_map/ppermute | solution.py:592
  27.1 4.9 %collective-permute-start.3 = (bf16[2,2,16,768]{3,2,0,1:T(8,128)(2,1)S(1)}, bf16[2,2,16,768]{3,2,0,1:T(8,128)(2,1)S(1)}, u32[]{:S(2)}, u32[]{:S(2)}) collective-permute-start(bf16[2,2,16,768]{3,2,0,1:T(8,128)(2,1)S(1)} %get-tuple-element.251), channel_id=1, source_target_pairs={{0,2},{2,0},{4,6},{6,4},{8,10},{10,8},{12,14},{14,12},{16,18},{18,... | collective-permute-start | bytes 294920 | tf_op jit(solution)/shard_map/ppermute | solution.py:592
  32.0 5.7 %collective-permute-start.5 = (bf16[2,2,2,16,768]{4,3,0,1,2:T(8,128)(2,1)S(1)}, bf16[2,2,2,16,768]{4,3,0,1,2:T(8,128)(2,1)S(1)}, u32[]{:S(2)}, u32[]{:S(2)}) collective-permute-start(bf16[2,2,2,16,768]{4,3,0,1,2:T(8,128)(2,1)S(1)} %pad_maximum_fusion.3), channel_id=1, source_target_pairs={{0,4},{2,6},{4,0},{6,2},{8,12},{10,14},{12,8},{14,10},{16,20},{18,... | collective-permute-start | bytes 589832 | tf_op jit(solution)/shard_map/ppermute | solution.py:592
  32.1 5.7 %collective-permute-start.4 = (bf16[2,2,2,16,768]{4,3,0,1,2:T(8,128)(2,1)S(1)}, bf16[2,2,2,16,768]{4,3,0,1,2:T(8,128)(2,1)S(1)}, u32[]{:S(2)}, u32[]{:S(2)}) collective-permute-start(bf16[2,2,2,16,768]{4,3,0,1,2:T(8,128)(2,1)S(1)} %pad_maximum_fusion.2), channel_id=1, source_target_pairs={{0,2},{2,0},{4,6},{6,4},{8,10},{10,8},{12,14},{14,12},{16,18},{18,... | collective-permute-start | bytes 589832 | tf_op jit(solution)/shard_map/ppermute | solution.py:592
  46.5 45.2 %copy-start.10 = (bf16[512,768]{1,0:T(8,128)(2,1)}, bf16[512,768]{1,0:T(8,128)(2,1)S(1)}, u32[]{:S(2)}) copy-start(bf16[512,768]{1,0:T(8,128)(2,1)S(1)} %get-tuple-element.320.k2_ref) | copy-start | bytes 2359300
  46.5 45.3 %copy-start.12 = (bf16[512,768]{1,0:T(8,128)(2,1)}, bf16[512,768]{1,0:T(8,128)(2,1)S(1)}, u32[]{:S(2)}) copy-start(bf16[512,768]{1,0:T(8,128)(2,1)S(1)} %get-tuple-element.321.v2_ref) | copy-start | bytes 2359300
  46.5 45.3 %copy-start.23 = (bf16[1,32,768]{2,1,0:T(8,128)(2,1)S(1)}, bf16[1,32,768]{2,1,0:T(8,128)(2,1)}, u32[]{:S(2)}) copy-start(bf16[1,32,768]{2,1,0:T(8,128)(2,1)} %param.31) | copy-start | bytes 147460
  96.2 13.1 %collective-permute-start.7 = (bf16[16,96,768]{2,1,0:T(8,128)(2,1)S(1)}, bf16[16,96,768]{2,1,0:T(8,128)(2,1)S(1)}, u32[]{:S(2)}, u32[]{:S(2)}) collective-permute-start(bf16[16,96,768]{2,1,0:T(8,128)(2,1)S(1)} %get-tuple-element.278), channel_id=1, source_target_pairs={{0,1},{1,0},{2,3},{3,2},{4,5},{5,4},{6,7},{7,6},{8,9},{9,8},{10,11... | collective-permute-start | bytes 7077896 | tf_op jit(solution)/shard_map/ppermute | solution.py:592
  96.2 13.0 %collective-permute-start.6 = (bf16[32,896]{1,0:T(8,128)(2,1)S(1)}, bf16[32,896]{1,0:T(8,128)(2,1)S(1)}, u32[]{:S(2)}, u32[]{:S(2)}) collective-permute-start(bf16[32,896]{1,0:T(8,128)(2,1)S(1)} %get-tuple-element.270), channel_id=1, source_target_pairs={{0,16},{2,18},{4,20},{6,22},{8,24},{10,26},{12,28},{14,30},{16,0},... | collective-permute-start | bytes 172040 | tf_op jit(solution)/shard_map/ppermute | solution.py:592
  110.6 9.0 %collective-permute-start.9 = (bf16[16,192,768]{2,1,0:T(8,128)(2,1)}, bf16[16,192,768]{2,1,0:T(8,128)(2,1)}, u32[]{:S(2)}, u32[]{:S(2)}) collective-permute-start(bf16[16,192,768]{2,1,0:T(8,128)(2,1)} %shard_map.276), channel_id=1, source_target_pairs={{0,1},{1,0},{2,3},{3,2},{4,5},{5,4},{6,7},{7,6},{8,9},{9,8},{10,11... | collective-permute-start | bytes 14155784 | tf_op jit(solution)/shard_map/ppermute | solution.py:592
  111.6 7.2 %collective-permute-start.8 = (bf16[2,32,896]{2,1,0:T(8,128)(2,1)}, bf16[2,32,896]{2,1,0:T(8,128)(2,1)}, u32[]{:S(2)}, u32[]{:S(2)}) collective-permute-start(bf16[2,32,896]{2,1,0:T(8,128)(2,1)} %get-tuple-element.279), channel_id=1, source_target_pairs={{0,8},{2,10},{4,12},{6,14},{8,0},{10,2},{12,4},{14,6},{16,24},{18,... | collective-permute-start | bytes 344072 | tf_op jit(solution)/shard_map/ppermute | solution.py:592
  119.7 16.2 %collective-permute-start.10 = (bf16[2,2,16,896]{3,2,0,1:T(8,128)(2,1)S(1)}, bf16[2,2,16,896]{3,2,0,1:T(8,128)(2,1)S(1)}, u32[]{:S(2)}, u32[]{:S(2)}) collective-permute-start(bf16[2,2,16,896]{3,2,0,1:T(8,128)(2,1)S(1)} %get-tuple-element.287), channel_id=1, source_target_pairs={{0,4},{2,6},{4,0},{6,2},{8,12},{10,14},{12,8},{14,10},{16,20},{18,... | collective-permute-start | bytes 344072 | tf_op jit(solution)/shard_map/ppermute | solution.py:592
  121.7 14.3 %collective-permute-start.11 = (bf16[2,2,16,896]{3,2,0,1:T(8,128)(2,1)S(1)}, bf16[2,2,16,896]{3,2,0,1:T(8,128)(2,1)S(1)}, u32[]{:S(2)}, u32[]{:S(2)}) collective-permute-start(bf16[2,2,16,896]{3,2,0,1:T(8,128)(2,1)S(1)} %get-tuple-element.288), channel_id=1, source_target_pairs={{0,2},{2,0},{4,6},{6,4},{8,10},{10,8},{12,14},{14,12},{16,18},{18,... | collective-permute-start | bytes 344072 | tf_op jit(solution)/shard_map/ppermute | solution.py:592
  123.2 23.5 %copy-start.54 = (bf16[1024,768]{1,0:T(8,128)(2,1)S(1)}, bf16[1024,768]{1,0:T(8,128)(2,1)}, u32[]{:S(2)}) copy-start(bf16[1024,768]{1,0:T(8,128)(2,1)} %copy-done.53) | copy-start | bytes 4718596
  123.2 23.5 %copy-start.59 = (f32[32,768]{1,0:T(8,128)S(1)}, f32[32,768]{1,0:T(8,128)}, u32[]{:S(2)}) copy-start(f32[32,768]{1,0:T(8,128)} %copy-done.58) | copy-start | bytes 294916
  123.2 23.5 %copy-start.61 = (bf16[32,768]{1,0:T(8,128)(2,1)S(1)}, bf16[32,768]{1,0:T(8,128)(2,1)}, u32[]{:S(2)}) copy-start(bf16[32,768]{1,0:T(8,128)(2,1)} %copy-done.60) | copy-start | bytes 147460
  136.0 6.7 %collective-permute-start.13 = (bf16[2,2,2,16,896]{4,3,0,1,2:T(8,128)(2,1)S(1)}, bf16[2,2,2,16,896]{4,3,0,1,2:T(8,128)(2,1)S(1)}, u32[]{:S(2)}, u32[]{:S(2)}) collective-permute-start(bf16[2,2,2,16,896]{4,3,0,1,2:T(8,128)(2,1)S(1)} %pad_maximum_fusion.1), channel_id=1, source_target_pairs={{0,4},{2,6},{4,0},{6,2},{8,12},{10,14},{12,8},{14,10},{16,20},{18,... | collective-permute-start | bytes 688136 | tf_op jit(solution)/shard_map/ppermute | solution.py:592
  136.1 6.6 %collective-permute-start.12 = (bf16[2,2,2,16,896]{4,3,0,1,2:T(8,128)(2,1)S(1)}, bf16[2,2,2,16,896]{4,3,0,1,2:T(8,128)(2,1)S(1)}, u32[]{:S(2)}, u32[]{:S(2)}) collective-permute-start(bf16[2,2,2,16,896]{4,3,0,1,2:T(8,128)(2,1)S(1)} %pad_maximum_fusion), channel_id=1, source_target_pairs={{0,2},{2,0},{4,6},{6,4},{8,10},{10,8},{12,14},{14,12},{16,18},{18,... | collective-permute-start | bytes 688136 | tf_op jit(solution)/shard_map/ppermute | solution.py:592
  142.8 26.3 %collective-permute-start.14 = (bf16[8,96,768]{2,1,0:T(8,128)(2,1)}, bf16[8,96,768]{2,1,0:T(8,128)(2,1)S(1)}, u32[]{:S(2)}, u32[]{:S(2)}) collective-permute-start(bf16[8,96,768]{2,1,0:T(8,128)(2,1)} %get-tuple-element.348), channel_id=1, source_target_pairs={{0,2},{2,0},{4,6},{6,4},{8,10},{10,8},{12,14},{14,12},{16,18},{18,... | collective-permute-start | bytes 3538952 | tf_op jit(solution)/shard_map/ppermute | solution.py:592
  143.3 26.0 %collective-permute-start.15 = (bf16[8,96,768]{2,1,0:T(8,128)(2,1)}, bf16[8,96,768]{2,1,0:T(8,128)(2,1)S(1)}, u32[]{:S(2)}, u32[]{:S(2)}) collective-permute-start(bf16[8,96,768]{2,1,0:T(8,128)(2,1)} %get-tuple-element.349), channel_id=1, source_target_pairs={{0,4},{2,6},{4,0},{6,2},{8,12},{10,14},{12,8},{14,10},{16,20},{18,... | collective-permute-start | bytes 3538952 | tf_op jit(solution)/shard_map/ppermute | solution.py:592
  145.0 25.5 %collective-permute-start.16 = (bf16[8,96,768]{2,1,0:T(8,128)(2,1)}, bf16[8,96,768]{2,1,0:T(8,128)(2,1)S(1)}, u32[]{:S(2)}, u32[]{:S(2)}) collective-permute-start(bf16[8,96,768]{2,1,0:T(8,128)(2,1)} %get-tuple-element.350), channel_id=1, source_target_pairs={{0,8},{2,10},{4,12},{6,14},{8,0},{10,2},{12,4},{14,6},{16,24},{18,... | collective-permute-start | bytes 3538952 | tf_op jit(solution)/shard_map/ppermute | solution.py:592
  170.5 19.7 %collective-permute-start.20 = (bf16[16,192,768]{2,1,0:T(8,128)(2,1)}, bf16[16,192,768]{2,1,0:T(8,128)(2,1)S(1)}, u32[]{:S(2)}, u32[]{:S(2)}) collective-permute-start(bf16[16,192,768]{2,1,0:T(8,128)(2,1)} %get-tuple-element.385), channel_id=1, source_target_pairs={{0,1},{1,0},{2,3},{3,2},{4,5},{5,4},{6,7},{7,6},{8,9},{9,8},{10,11... | collective-permute-start | bytes 14155784 | tf_op jit(solution)/shard_map/ppermute | solution.py:592
  172.5 15.8 %collective-permute-start.17 = (bf16[4,96,768]{2,1,0:T(8,128)(2,1)S(1)}, bf16[4,96,768]{2,1,0:T(8,128)(2,1)S(1)}, u32[]{:S(2)}, u32[]{:S(2)}) collective-permute-start(bf16[4,96,768]{2,1,0:T(8,128)(2,1)S(1)} %get-tuple-element.359), channel_id=1, source_target_pairs={{0,4},{2,6},{4,0},{6,2},{8,12},{10,14},{12,8},{14,10},{16,20},{18,... | collective-permute-start | bytes 1769480 | tf_op jit(solution)/shard_map/ppermute | solution.py:592
  173.2 15.5 %collective-permute-start.18 = (bf16[4,96,768]{2,1,0:T(8,128)(2,1)S(1)}, bf16[4,96,768]{2,1,0:T(8,128)(2,1)S(1)}, u32[]{:S(2)}, u32[]{:S(2)}) collective-permute-start(bf16[4,96,768]{2,1,0:T(8,128)(2,1)S(1)} %get-tuple-element.361), channel_id=1, source_target_pairs={{0,8},{2,10},{4,12},{6,14},{8,0},{10,2},{12,4},{14,6},{16,24},{18,... | collective-permute-start | bytes 1769480 | tf_op jit(solution)/shard_map/ppermute | solution.py:592
  175.0 15.2 %collective-permute-start.19 = (bf16[4,96,768]{2,1,0:T(8,128)(2,1)S(1)}, bf16[4,96,768]{2,1,0:T(8,128)(2,1)S(1)}, u32[]{:S(2)}, u32[]{:S(2)}) collective-permute-start(bf16[4,96,768]{2,1,0:T(8,128)(2,1)S(1)} %get-tuple-element.363), channel_id=1, source_target_pairs={{0,2},{2,0},{4,6},{6,4},{8,10},{10,8},{12,14},{14,12},{16,18},{18,... | collective-permute-start | bytes 1769480 | tf_op jit(solution)/shard_map/ppermute | solution.py:592
  191.2 8.1 %collective-permute-start.22 = (bf16[2,96,768]{2,1,0:T(8,128)(2,1)S(1)}, bf16[2,96,768]{2,1,0:T(8,128)(2,1)S(1)}, u32[]{:S(2)}, u32[]{:S(2)}) collective-permute-start(bf16[2,96,768]{2,1,0:T(8,128)(2,1)S(1)} %get-tuple-element.393), channel_id=1, source_target_pairs={{0,8},{2,10},{4,12},{6,14},{8,0},{10,2},{12,4},{14,6},{16,24},{18,... | collective-permute-start | bytes 884744 | tf_op jit(solution)/shard_map/ppermute | solution.py:592
  191.5 8.0 %collective-permute-start.23 = (bf16[2,96,768]{2,1,0:T(8,128)(2,1)S(1)}, bf16[2,96,768]{2,1,0:T(8,128)(2,1)S(1)}, u32[]{:S(2)}, u32[]{:S(2)}) collective-permute-start(bf16[2,96,768]{2,1,0:T(8,128)(2,1)S(1)} %get-tuple-element.395), channel_id=1, source_target_pairs={{0,2},{2,0},{4,6},{6,4},{8,10},{10,8},{12,14},{14,12},{16,18},{18,... | collective-permute-start | bytes 884744 | tf_op jit(solution)/shard_map/ppermute | solution.py:592
  193.0 7.8 %collective-permute-start.24 = (bf16[2,96,768]{2,1,0:T(8,128)(2,1)S(1)}, bf16[2,96,768]{2,1,0:T(8,128)(2,1)S(1)}, u32[]{:S(2)}, u32[]{:S(2)}) collective-permute-start(bf16[2,96,768]{2,1,0:T(8,128)(2,1)S(1)} %get-tuple-element.397), channel_id=1, source_target_pairs={{0,4},{2,6},{4,0},{6,2},{8,12},{10,14},{12,8},{14,10},{16,20},{18,... | collective-permute-start | bytes 884744 | tf_op jit(solution)/shard_map/ppermute | solution.py:592
  194.4 1.4 collective-permute-start.21
  207.5 26.9 %collective-permute-start.26 = (bf16[8,64,768]{2,1,0:T(8,128)(2,1)S(1)}, bf16[8,64,768]{2,1,0:T(8,128)(2,1)S(1)}, u32[]{:S(2)}, u32[]{:S(2)}) collective-permute-start(bf16[8,64,768]{2,1,0:T(8,128)(2,1)S(1)} %get-tuple-element.416), channel_id=1, source_target_pairs={{0,2},{2,0},{4,6},{6,4},{8,10},{10,8},{12,14},{14,12},{16,18},{18,... | collective-permute-start | bytes 2359304 | tf_op jit(solution)/shard_map/ppermute | solution.py:592
  208.1 26.3 %collective-permute-start.27 = (bf16[8,64,768]{2,1,0:T(8,128)(2,1)S(1)}, bf16[8,64,768]{2,1,0:T(8,128)(2,1)S(1)}, u32[]{:S(2)}, u32[]{:S(2)}) collective-permute-start(bf16[8,64,768]{2,1,0:T(8,128)(2,1)S(1)} %get-tuple-element.418), channel_id=1, source_target_pairs={{0,4},{2,6},{4,0},{6,2},{8,12},{10,14},{12,8},{14,10},{16,20},{18,... | collective-permute-start | bytes 2359304 | tf_op jit(solution)/shard_map/ppermute | solution.py:592
  209.5 26.3 %collective-permute-start.28 = (bf16[8,64,768]{2,1,0:T(8,128)(2,1)S(1)}, bf16[8,64,768]{2,1,0:T(8,128)(2,1)S(1)}, u32[]{:S(2)}, u32[]{:S(2)}) collective-permute-start(bf16[8,64,768]{2,1,0:T(8,128)(2,1)S(1)} %get-tuple-element.420), channel_id=1, source_target_pairs={{0,8},{2,10},{4,12},{6,14},{8,0},{10,2},{12,4},{14,6},{16,24},{18,... | collective-permute-start | bytes 2359304 | tf_op jit(solution)/shard_map/ppermute | solution.py:592
  210.9 23.5 %collective-permute-start.29 = (bf16[288,768]{1,0:T(8,128)(2,1)S(1)}, bf16[288,768]{1,0:T(8,128)(2,1)S(1)}, u32[]{:S(2)}, u32[]{:S(2)}) collective-permute-start(bf16[288,768]{1,0:T(8,128)(2,1)S(1)} %get-tuple-element.423), channel_id=1, source_target_pairs={{0,16},{2,18},{4,20},{6,22},{8,24},{10,26},{12,28},{14,30},{16,0},... | collective-permute-start | bytes 1327112 | tf_op jit(solution)/shard_map/ppermute | solution.py:592
  212.1 13.9 %collective-permute-start.25 = (f32[16,768]{1,0:T(8,128)S(1)}, f32[16,768]{1,0:T(8,128)S(1)}, u32[]{:S(2)}, u32[]{:S(2)}) collective-permute-start(f32[16,768]{1,0:T(8,128)S(1)} %add.30), channel_id=1, source_target_pairs={{0,2},{2,0},{4,6},{6,4},{8,10},{10,8},{12,14},{14,12},{16,18},{18,... | collective-permute-start | bytes 147464 | tf_op jit(solution)/shard_map/ppermute | solution.py:592
  237.3 4.1 %collective-permute-start.34 = (bf16[288,768]{1,0:T(8,128)(2,1)S(1)}, bf16[288,768]{1,0:T(8,128)(2,1)S(1)}, u32[]{:S(2)}, u32[]{:S(2)}) collective-permute-start(bf16[288,768]{1,0:T(8,128)(2,1)S(1)} %shard_map.286.mine_ref), channel_id=1, source_target_pairs={{0,1},{1,0},{2,3},{3,2},{4,5},{5,4},{6,7},{7,6},{8,9},{9,8},{10,11... | collective-permute-start | bytes 1327112 | tf_op jit(solution)/shard_map/ppermute | solution.py:592
  237.4 12.6 %collective-permute-start.31 = (bf16[4,64,768]{2,1,0:T(8,128)(2,1)S(1)}, bf16[4,64,768]{2,1,0:T(8,128)(2,1)S(1)}, u32[]{:S(2)}, u32[]{:S(2)}) collective-permute-start(bf16[4,64,768]{2,1,0:T(8,128)(2,1)S(1)} %get-tuple-element.432), channel_id=1, source_target_pairs={{0,4},{2,6},{4,0},{6,2},{8,12},{10,14},{12,8},{14,10},{16,20},{18,... | collective-permute-start | bytes 1179656 | tf_op jit(solution)/shard_map/ppermute | solution.py:592
  238.1 11.9 %collective-permute-start.32 = (bf16[4,64,768]{2,1,0:T(8,128)(2,1)S(1)}, bf16[4,64,768]{2,1,0:T(8,128)(2,1)S(1)}, u32[]{:S(2)}, u32[]{:S(2)}) collective-permute-start(bf16[4,64,768]{2,1,0:T(8,128)(2,1)S(1)} %get-tuple-element.433), channel_id=1, source_target_pairs={{0,8},{2,10},{4,12},{6,14},{8,0},{10,2},{12,4},{14,6},{16,24},{18,... | collective-permute-start | bytes 1179656 | tf_op jit(solution)/shard_map/ppermute | solution.py:592
  238.5 11.4 %collective-permute-start.33 = (bf16[4,64,768]{2,1,0:T(8,128)(2,1)S(1)}, bf16[4,64,768]{2,1,0:T(8,128)(2,1)S(1)}, u32[]{:S(2)}, u32[]{:S(2)}) collective-permute-start(bf16[4,64,768]{2,1,0:T(8,128)(2,1)S(1)} %get-tuple-element.434), channel_id=1, source_target_pairs={{0,2},{2,0},{4,6},{6,4},{8,10},{10,8},{12,14},{14,12},{16,18},{18,... | collective-permute-start | bytes 1179656 | tf_op jit(solution)/shard_map/ppermute | solution.py:592
  240.0 10.0 %collective-permute-start.30 = (f32[16,768]{1,0:T(8,128)S(1)}, f32[16,768]{1,0:T(8,128)S(1)}, u32[]{:S(2)}, u32[]{:S(2)}) collective-permute-start(f32[16,768]{1,0:T(8,128)S(1)} %add.31), channel_id=1, source_target_pairs={{0,4},{2,6},{4,0},{6,2},{8,12},{10,14},{12,8},{14,10},{16,20},{18,... | collective-permute-start | bytes 147464 | tf_op jit(solution)/shard_map/ppermute | solution.py:592
  250.9 8.0 %collective-permute-start.36 = (bf16[2,64,768]{2,1,0:T(8,128)(2,1)S(1)}, bf16[2,64,768]{2,1,0:T(8,128)(2,1)S(1)}, u32[]{:S(2)}, u32[]{:S(2)}) collective-permute-start(bf16[2,64,768]{2,1,0:T(8,128)(2,1)S(1)} %get-tuple-element.452), channel_id=1, source_target_pairs={{0,8},{2,10},{4,12},{6,14},{8,0},{10,2},{12,4},{14,6},{16,24},{18,... | collective-permute-start | bytes 589832 | tf_op jit(solution)/shard_map/ppermute | solution.py:592
  252.0 7.0 %collective-permute-start.37 = (bf16[2,64,768]{2,1,0:T(8,128)(2,1)S(1)}, bf16[2,64,768]{2,1,0:T(8,128)(2,1)S(1)}, u32[]{:S(2)}, u32[]{:S(2)}) collective-permute-start(bf16[2,64,768]{2,1,0:T(8,128)(2,1)S(1)} %get-tuple-element.453), channel_id=1, source_target_pairs={{0,2},{2,0},{4,6},{6,4},{8,10},{10,8},{12,14},{14,12},{16,18},{18,... | collective-permute-start | bytes 589832 | tf_op jit(solution)/shard_map/ppermute | solution.py:592
  253.4 5.7 %collective-permute-start.38 = (bf16[2,64,768]{2,1,0:T(8,128)(2,1)S(1)}, bf16[2,64,768]{2,1,0:T(8,128)(2,1)S(1)}, u32[]{:S(2)}, u32[]{:S(2)}) collective-permute-start(bf16[2,64,768]{2,1,0:T(8,128)(2,1)S(1)} %get-tuple-element.454), channel_id=1, source_target_pairs={{0,4},{2,6},{4,0},{6,2},{8,12},{10,14},{12,8},{14,10},{16,20},{18,... | collective-permute-start | bytes 589832 | tf_op jit(solution)/shard_map/ppermute | solution.py:592
  254.8 4.1 %collective-permute-start.35 = (f32[16,768]{1,0:T(8,128)S(1)}, f32[16,768]{1,0:T(8,128)S(1)}, u32[]{:S(2)}, u32[]{:S(2)}) collective-permute-start(f32[16,768]{1,0:T(8,128)S(1)} %add.32), channel_id=1, source_target_pairs={{0,8},{2,10},{4,12},{6,14},{8,0},{10,2},{12,4},{14,6},{16,24},{18,... | collective-permute-start | bytes 147464 | tf_op jit(solution)/shard_map/ppermute | solution.py:592
  259.2 16.5 %collective-permute-start.40 = (bf16[192,768]{1,0:T(8,128)(2,1)S(1)}, bf16[192,768]{1,0:T(8,128)(2,1)S(1)}, u32[]{:S(2)}, u32[]{:S(2)}) collective-permute-start(bf16[192,768]{1,0:T(8,128)(2,1)S(1)} %get-tuple-element.467), channel_id=1, source_target_pairs={{0,16},{2,18},{4,20},{6,22},{8,24},{10,26},{12,28},{14,30},{16,0},... | collective-permute-start | bytes 884744 | tf_op jit(solution)/shard_map/ppermute | solution.py:592
  261.3 14.4 %collective-permute-start.39 = (f32[16,768]{1,0:T(8,128)S(1)}, f32[16,768]{1,0:T(8,128)S(1)}, u32[]{:S(2)}, u32[]{:S(2)}) collective-permute-start(f32[16,768]{1,0:T(8,128)S(1)} %add.33), channel_id=1, source_target_pairs={{0,16},{2,18},{4,20},{6,22},{8,24},{10,26},{12,28},{14,30},{16,0},... | collective-permute-start | bytes 147464 | tf_op jit(solution)/shard_map/ppermute | solution.py:592
  275.8 1.6 collective-permute-start.41
  (62 other events, 532.1 us)

commit v4 on v3

--- a/solution.py
+++ b/solution.py
@@ -13,6 +13,7 @@
 LAT = 8
 FACTOR = HEAD ** (-0.5)
 HL = HEADS * LAT
+LANES = 768
 BF = jnp.bfloat16
 F32 = jnp.float32
 
@@ -417,20 +418,27 @@
             self_out_ref[...] = unit(zero, 3)
 
 
+def lane_spans():
+    return [slice(start, start + LANES) for start in range(0, D, LANES)]
+
+
 def feed_kernel(which_ref, gd_ref, h_ref, e4_ref, out_ref):
     part = pl.program_id(0)
     count, rows, _ = out_ref.shape
     slab = D // count
+    near = D // rows
 
     @pl.when(which_ref[0] == 0)
     def _():
-        grad = narrow(mm_tn(h_ref[...], gd_ref[...]).reshape(count, slab, D))
-        out_ref[:, pl.ds(pl.multiple_of(part * slab, 8), slab), :] = grad
+        for lanes in lane_spans():
+            grad = narrow(mm_tn(h_ref[...], gd_ref[:, lanes]).reshape(count, slab, LANES))
+            out_ref[:, pl.ds(pl.multiple_of(part * slab, 8), slab), lanes] = grad
 
     @pl.when(which_ref[0] == 1)
     def _():
-        grad = narrow(mm_tn(gd_ref[...], e4_ref[...]).reshape(D // rows, rows, D))
-        out_ref[pl.ds(part * (D // rows), D // rows)] = grad
+        for lanes in lane_spans():
+            grad = narrow(mm_tn(gd_ref[...], e4_ref[:, lanes]).reshape(near, rows, LANES))
+            out_ref[pl.ds(part * near, near), :, lanes] = grad
 
 
 def halves(tensor, bit):
@@ -448,29 +456,29 @@
     half = rows // 2
     per_part = half // slab
 
-    def store(refs, index, value, bit):
-        zero, one = halves(value, bit)
-        mine = which_ref[1 + (0 if bit == bits[0] else 1)] == 0
-        refs[0][index] = narrow(jnp.where(mine, one, zero))
-        refs[1][index] = narrow(jnp.where(mine, zero, one))
-
-    pairs = ((send0_ref, stay0_ref), (send1_ref, stay1_ref))
-
-    @pl.when(which_ref[0] == 0)
-    def _():
-        grad = mm_tn(h_ref[...], gd_ref[...]).reshape(count, slab, D) + got_up_ref[...].astype(F32)
-        for index in range(2):
-            @pl.when(part // per_part == index)
-            def _():
-                place = pl.ds(pl.multiple_of(lax.rem(part, per_part) * slab, 8), slab)
-                store(pairs[index], (slice(None), place), grad, bits[index])
+    def store(index, place, value):
+        zero, one = halves(value, bits[index])
+        mine = which_ref[1 + index] == 0
+        send, stay = ((send0_ref, stay0_ref), (send1_ref, stay1_ref))[index]
+        send[place] = narrow(jnp.where(mine, one, zero))
+        stay[place] = narrow(jnp.where(mine, zero, one))
+
+    for index in range(2):
+        @pl.when((which_ref[0] == 0) & (part // per_part == index))
+        def _():
+            rows_at = pl.ds(pl.multiple_of(lax.rem(part, per_part) * slab, 8), slab)
+            for lanes in lane_spans():
+                grad = mm_tn(h_ref[...], gd_ref[:, lanes]).reshape(count, slab, LANES)
+                store(index, (slice(None), rows_at, lanes), grad + got_up_ref[:, :, lanes].astype(F32))
 
     @pl.when(which_ref[0] == 1)
     def _():
-        grad = mm_tn(gd_ref[...], e4_ref[...]).reshape(near, rows, D) + got_down_ref[...].astype(F32)
-        for index in range(2):
-            store(pairs[index], (pl.ds(part * (near // 2), near // 2),),
-                  grad[:, index * half : (index + 1) * half], bits[index])
+        place = pl.ds(part * (near // 2), near // 2)
+        for lanes in lane_spans():
+            grad = mm_tn(gd_ref[...], e4_ref[:, lanes]).reshape(near, rows, LANES)
+            grad = grad + got_down_ref[:, :, lanes].astype(F32)
+            for index in range(2):
+                store(index, (place, slice(None), lanes), grad[:, index * half : (index + 1) * half])
 
 
 def tail_kernel(
@@ -671,9 +679,37 @@
         self.left = [list(range(bits_of(count) - 1, -1, -1)) for _ in orders]
         self.step = 0
 
-    def begin(self, parts):
-        self.parts = parts
-        self.send()
+    def cut(self, parts):
+        lead = self.count // 2
+        picks, in_specs, operands, out_specs, out_shape = [], [], [], [], []
+        for (kept, got, rows, block), order in zip(parts, self.orders):
+            inner = 1 << order[0]
+            after = [bit for bit in range(bits_of(self.count) - 1, -1, -1) if bit != order[0]]
+            near = (lead // 2) >> after.index(order[1])
+            picks.append(own_bit(order[0]))
+            spec = pl.BlockSpec(
+                (None, 2, None, rows, D),
+                lambda i, inner=inner, block=block: (i // inner, 0, i % inner, block, 0),
+            )
+            in_specs += [spec, spec]
+            kept, got = (t.reshape(lead // inner, 2, inner, -1, D) for t in (kept, got))
+            operands += [in_hbm(kept), got]
+            out_specs += [
+                pl.BlockSpec((None, rows, D), lambda i: (i, 0, 0)),
+                pl.BlockSpec(
+                    (None, None, None, rows, D),
+                    lambda i, near=near: (i // (2 * near), (i // near) % 2, i % near, 0, 0),
+                ),
+            ]
+            out_shape += [
+                shaped((lead, rows, D), BF), pltpu.HBM((lead // (2 * near), 2, near, rows, D), BF)
+            ]
+        out = call(
+            functools.partial(stage_kernel, len(parts)), (lead,),
+            [pl.BlockSpec(memory_space=pltpu.SMEM)] + in_specs, out_specs, out_shape, 0, 0, vmem=10,
+        )(*self.line.gate((jnp.stack(picks).astype(jnp.int32), *operands)))
+        self.line.note(out)
+        return [(sent, stay, part[2]) for sent, stay, part in zip(out[::2], out[1::2], parts)]
 
     def begin_cut(self, parts):
         self.parts = []
@@ -683,9 +719,9 @@
             self.parts.append((stay, swap(self.line.gate(sent), "blk", bit, self.count), rows, 0))
         self.step += 1
 
-    def send(self):
+    def send(self, pin=lambda tensor: tensor, far=False):
         if self.step == len(self.orders[0]) - 1 and len({order[-1] for order in self.orders}) == 1:
-            self.send_last()
+            self.send_last(pin)
             return
         lead = (self.count >> self.step) // 2
         picks, in_specs, operands, out_specs, out_shape, bits = [], [], [], [], [], []
@@ -700,10 +736,11 @@
                 lambda i, inner=inner, block=block: (i // inner, 0, i % inner, block, 0),
             )
             in_specs += [spec, spec]
-            kept, got = (t.reshape(lead // inner, 2, inner, -1, D) for t in (kept, got))
-            operands += [in_hbm(kept), in_hbm(got)] if self.step == 0 else [kept, got]
+            got = got.reshape(lead // inner, 2, inner, -1, D)
+            kept = in_hbm(kept) if kept.ndim == 5 else kept.reshape(got.shape)
+            operands += [kept, got]
             out_specs += [pl.BlockSpec((None, rows, D), lambda i: (i, 0, 0))] * 2
-            out_shape += [shaped((lead, rows, D), BF)] * 2
+            out_shape += [shaped((lead, rows, D), BF), (pltpu.HBM if far else shaped)((lead, rows, D), BF)]
         moved = sum(3 * 4 * lead * part[2] * D for part in self.parts)
         out = call(
             functools.partial(stage_kernel, len(self.parts)), (lead,),
@@ -717,10 +754,10 @@
         ]
         self.step += 1
 
-    def send_last(self):
+    def send_last(self, pin=lambda tensor: tensor):
         bit = self.orders[0][-1]
         rows = [part[2] for part in self.parts]
-        operands = [t for kept, got, _, _ in self.parts for t in (kept, got)]
+        operands = [pin(t) for kept, got, _, _ in self.parts for t in (kept, got)]
         shape = (sum(rows), D)
         send, stay = call(
             functools.partial(last_stage_kernel, len(rows)), (1,),
@@ -773,14 +810,16 @@
         unit_flops = 2 * tokens * D * D
         low_lat, full_lat, fold = shaped((lat, D), BF), shaped((lat, D), F32), shaped((8, D), F32)
         low_patch = shaped((tokens, D), BF)
+        far_patch, far_lat, far_full = pltpu.HBM((tokens, D), BF), pltpu.HBM((lat, D), BF), pltpu.HBM((lat, D), F32)
+        far_fold = pltpu.HBM((8, D), F32)
         line = Line()
 
         a1, q1, b1, k1, v1, p1, o1, z1, a2 = call(
             read_forward_kernel, grid,
             [patch_spec, lat_spec, norm_spec, three, square],
             [lat_spec, lat_spec, patch_spec, patch_spec, patch_spec, share_spec, lat_spec, lat_spec, lat_spec],
-            [low_lat, full_lat, low_patch, low_patch, low_patch, shaped((groups, HL, size), F32),
-             low_lat, full_lat, low_lat],
+            [far_lat, far_full, low_patch, far_patch, far_patch, pltpu.HBM((groups, HL, size), F32),
+             far_lat, full_lat, low_lat],
             2 * unit_flops, 12 * tokens * D,
             [pltpu.VMEM((lat, D), F32)],
         )(in_hbm(x), z, norms, in_hbm(read_in), in_hbm(read_out))
@@ -808,9 +847,9 @@
              one_of(1), one_of(2)],
             [whole((total, D)), whole((hl2, total)), whole((total, D)), whole((total, D)), whole((hl2, total)),
              whole((hl2, 1))] + [lat_spec] * 6,
-            [shaped((total, D), BF), shaped((hl2, total), F32), shaped((total, D), BF), shaped((total, D), BF),
+            [pltpu.HBM((total, D), BF), pltpu.HBM((hl2, total), F32), shaped((total, D), BF), shaped((total, D), BF),
              shaped((hl2, total), F32), shaped((hl2, 1), F32),
-             low_lat, full_lat, low_lat, low_lat, full_lat, full_lat],
+             far_lat, full_lat, low_lat, low_lat, full_lat, full_lat],
             unit_flops * 2, 10 * D * D * 2,
         )(group_image, places, own_at, *pieces, a2, z1, norms, self_in, self_out, write_in, write_in)
 
@@ -826,9 +865,9 @@
             [spans, spans,
              pl.BlockSpec((2, each * size, hidden), lambda g: (0, g, 0), pipeline_mode=pl.Buffered(1 if each > 1 else 2)),
              whole((tokens, D)), spans, lat_spec, lat_spec, whole(early_shape), whole(early_shape), fold_spec, fold_spec],
-            [low_patch, low_patch, shaped((2, tokens, hidden), BF),
-             low_patch, shaped((tokens, D), F32), full_lat, full_lat, shaped(early_shape, BF), shaped(early_shape, BF),
-             fold, fold],
+            [low_patch, far_patch, pltpu.HBM((2, tokens, hidden), BF),
+             far_patch, pltpu.HBM((tokens, D), F32), full_lat, full_lat, shaped(early_shape, BF), shaped(early_shape, BF),
+             far_fold, far_fold],
             unit_flops * 22, 40 * tokens * D, [pltpu.VMEM((tokens, D), BF)] * 2, vmem=46,
         )(core_at, in_hbm(x), in_hbm(q3), in_hbm(cot), k3, v3, norms, write_out, feed_up, feed_down, in_hbm(b1), b3)
 
@@ -838,7 +877,7 @@
             [lat_spec] * 4 + [whole((total, D))] * 2
             + [whole((hl2, total)), whole((hl2, 1)), norm_spec, one_of(1), one_of(2), square],
             [lat_spec] * 2 + [whole((lat, width)), lat_spec, fold_spec, fold_spec],
-            [full_lat, low_lat, shaped((lat, width), BF), low_lat, fold, fold],
+            [far_full, far_lat, shaped((lat, width), BF), far_lat, far_fold, far_fold],
             unit_flops, 10 * D * D,
         )(dk3, dv3, z2, cot_z, k2, v2, p2, l2, norms, write_in, write_in, self_out)
         line.note(payload)
@@ -907,9 +946,9 @@
                 early["sum"] = call(
                     functools.partial(cut_kernel, bit), (1,), [smem] + [whole(early_shape)] * 2,
                     [whole(shape)] * 2, [shaped(shape, BF)] * 2, 0, 12 * tokens * D,
-                )(*line.gate((own_bit(bit).reshape(1).astype(jnp.int32), early_mine, early["got"])))
-                return early["sum"], early["feed_got"]
-            if step == 2:
+                )(*line.gate((own_bit(bit).reshape(1).astype(jnp.int32), in_hbm(early_mine), in_hbm(early["got"]))))
+                return early["sum"]
+            if step == 3:
                 early["feed"] = feed_mine(early["feed_got"])
                 return early["feed"]
             return None
@@ -925,15 +964,26 @@
             + [whole((total, D)), whole((hl2, total)), whole((total, D)), whole((total, D))] + [lat_spec] * 3
             + [norm_spec, three, square, lat_spec, share_spec, patch_spec, patch_spec, whole_patch] + [lat_spec] * 5,
             [whole(late_shape)] * 2 + [whole_patch] * 2 + [lat_spec] * 2 + [fold_spec] * 2,
-            [shaped(late_shape, BF), shaped(late_shape, BF), low_patch, low_patch, full_lat, full_lat, fold, fold],
+            [shaped(late_shape, BF), shaped(late_shape, BF), far_patch, far_patch, far_full, far_full, far_fold, far_fold],
             4 * unit_flops, 30 * tokens * D,
             [pltpu.VMEM((lat, D), F32)] + [pltpu.VMEM((lat, D), BF)] * 3,
             vmem=40,
-        )(*line.gate((core_at, *spread_pieces, a2_all, allowed, k2, v2, dq2, z1, dz2, norms, self_in, read_out,
-                      q1, in_hbm(p1), in_hbm(k1), in_hbm(v1), b1, a1, o1, a2, o2, e2)))
+        )(*line.gate((core_at, *spread_pieces, in_hbm(a2_all), in_hbm(allowed), k2, v2, in_hbm(dq2), in_hbm(z1), in_hbm(dz2), norms, self_in,
+                      read_out, in_hbm(q1), in_hbm(p1), in_hbm(k1), in_hbm(v1), in_hbm(b1), in_hbm(a1), in_hbm(o1), in_hbm(a2),
+                      in_hbm(o2), in_hbm(e2))))
         line.note((late_other, first.flying()))
         late_got = core_swap(late_other)
         first.send()
+        line.note(late_got)
+        last = Scatter(line, n_blk, orders)
+        last_rows = 4 * rows // 3
+        last_parts = last.cut([(late_mine, late_got, last_rows, i) for i in range(3)])
+        line.note((last_parts, first.flying()))
+        bits = bits_of(n_blk)
+        first.send(far=first.step == bits - 2)
+        line.note(first.flying())
+        first.send(in_hbm)
+        last.begin_cut(last_parts)
         dx, dz, norm_grads = call(
             input_back_kernel, grid,
             [patch_spec] * 5 + [lat_spec] * 3 + [norm_spec, three, one_of(0)] + [fold_spec] * 6,
@@ -941,18 +991,10 @@
             [low_patch, low_lat, shaped((16, D), F32)],
             unit_flops * 3, 14 * tokens * D,
             [pltpu.VMEM((8, D), F32)] * 2,
-        )(*line.gate((in_hbm(x), in_hbm(dx1), in_hbm(dq3), dk1, dv1, z, dz1, dq1, norms, read_in, write_in,
-                      gain2, shift2, gain3, shift3, gain4, shift4)))
-        line.note((dx, late_got, first.flying()))
-        first.send()
-        norm_got = swap(line.gate(norm_grads), "rep", 0, n_rep)
-        line.note((norm_got, first.flying()))
-        norm_grads = norm_grads + norm_got
-        first.send()
-        last = Scatter(line, n_blk, orders)
-        last_rows = 4 * rows // 3
-        last.begin([(late_mine, late_got, last_rows, i) for i in range(3)])
-        for bit in range(1, rep_bits):
+        )(*line.gate((in_hbm(x), in_hbm(dx1), in_hbm(dq3), in_hbm(dk1), in_hbm(dv1), z, in_hbm(dz1), in_hbm(dq1), norms, read_in, write_in,
+                      in_hbm(gain2), in_hbm(shift2), in_hbm(gain3), in_hbm(shift3), in_hbm(gain4), in_hbm(shift4))))
+        line.note(dx)
+        for bit in range(rep_bits):
             norm_grads = norm_grads + swap(line.gate(norm_grads), "rep", bit, n_rep)
         bits = bits_of(n_blk)
 

time: 284 us -> 279 us (0.982)
  Pallas kernels: 127 us -> 136 us
  starting transfers between devices: 47.7 us -> 41.7 us
  local copies, waits for them, and re-layouts: 14 us -> 8.03 us
  waiting for transfers between devices: 80.5 us -> 76.6 us
    pallas_call x0 -> x1, Pallas kernels: none -> 6.48 us  [cut(): call(functools.partial(stage_kernel, len(parts)), (lead,), [pl.BlockSpec(...]
    ppermute x42, starting transfers between devices: 47.7 us -> 41.7 us  [swap(): return lax.ppermute(tensor, axis, [(i, i ^ 1 << bit) for i in range(count)])]
    unnamed x136 -> x76, local copies, waits for them, and re-layouts: 13.2 us -> 7.21 us
    pallas_call x5 -> x4, Pallas kernels: 11.7 us -> 7.52 us  [send(): call(functools.partial(stage_kernel, len(self.parts)), (lead,), [pl.Block...]
    ppermute x42, waiting for transfers between devices: 80.5 us -> 76.6 us  [swap(): return lax.ppermute(tensor, axis, [(i, i ^ 1 << bit) for i in range(count)])]
  transfers between devices with their start and end apart: 42 -> 42, of which waited for: 25 -> 23; matrix products, arithmetic and copies ran while one was open for 2% -> 3% of each run, Pallas kernels for 19% -> 23%
where the time goes in v4:
time: 279 us; the launch traced here: 273 us
  Pallas kernels  136 us (49%)
  waiting for transfers between devices  76.6 us (27%)
  starting transfers between devices  41.7 us (15%)
  local copies, waits for them, and re-layouts  8.03 us (3%)
  other arithmetic  7.29 us (3%)
    ppermute x42, waiting for transfers between devices, swap(): return lax.ppermute(tensor, axis, [(i, i ^ 1 << bit) for i in range(count)])  76.6 us
    pallas_call x1, Pallas kernels, body(): call(functools.partial(patch_kernel, D, size), (groups // each,), [smem]...  45.2 us
    ppermute x42, starting transfers between devices, swap(): return lax.ppermute(tensor, axis, [(i, i ^ 1 << bit) for i in range(count)])  41.7 us
    pallas_call x2, Pallas kernels, feed_call(): pl.pallas_call(kernel, grid_spec=pltpu.PrefetchScalarGridSpec(num_scalar_...  22 us
    pallas_call x1, Pallas kernels, body(): call(tail_kernel, grid, [smem] + [whole(piece_shape + (width,))] * 4 + [w...  18.8 us
    pallas_call x1, Pallas kernels, body(): call(read_forward_kernel, grid, [patch_spec, lat_spec, norm_spec, three,...  10.6 us
    pallas_call x1, Pallas kernels, body(): call(input_back_kernel, grid, [patch_spec] * 5 + [lat_spec] * 3 + [norm_s...  9.52 us
    pallas_call x4, Pallas kernels, send(): call(functools.partial(stage_kernel, len(self.parts)), (lead,), [pl.Block...  7.52 us
  transfers between devices with their start and end apart: 42, of which 23 were waited for; matrix products, arithmetic and copies ran while one was open for 3% of the time, Pallas kernels for 23%

profile of v4, /device:TPU:0, one launch (start us, length us, event | category | flops | bytes accessed | tf_op | source)
XLA Modules:
  0.0 273.2 jit_solution(14994087130295255068)
XLA Ops:
  2.4 10.6 %shard_map.272 = (bf16[32,768]{1,0:T(8,128)(2,1)}, f32[32,768]{1,0:T(8,128)}, bf16[1024,768]{1,0:T(8,128)(2,1)S(1)}, bf16[1024,768]{1,0:T(8,128)(2,1)}, bf16[102...) custom-call(bf16[1024,768]{1,0:T(8,128)(2,1)} %bitcast.113, ...), custom_call_target="tpu_custom_call" | custom-call | flops 2415919104 | bytes 9437184 | tf_op jit(solution)/shard_map/pallas_call | solution.py:817
  13.0 4.1 %collective-permute-start = (bf16[32,768]{1,0:T(8,128)(2,1)S(1)}, bf16[32,768]{1,0:T(8,128)(2,1)S(1)}, u32[]{:S(2)}, u32[]{:S(2)}) collective-permute-start(bf16[32,768]{1,0:T(8,128)(2,1)S(1)} %get-tuple-element.338.a2_ref), channel_id=1, source_target_pairs={{0,16},{2,18},{4,20},{6,22},{8,24},{10,26},{12,28},{14,30},{16,0},... | collective-permute-start | bytes 147464 | tf_op jit(solution)/shard_map/ppermute | solution.py:600
  17.1 2.5 convolution_convert_fusion.q3_ref
  20.4 1.5 collective-permute-start.1
  22.0 3.4 %collective-permute-done.1 = bf16[2,32,768]{2,1,0:T(8,128)(2,1)} collective-permute-done((bf16[2,32,768]{2,1,0:T(8,128)(2,1)}, bf16[2,32,768]{2,1,0:T(8,128)(2,1)}, u32[]{:S(2)}, u32[]{:S(2)}) %collective-permute-start.1) | collective-permute-done | bytes 98336 | tf_op jit(solution)/shard_map/ppermute | solution.py:600
  26.2 1.8 collective-permute-start.2
  28.0 1.5 collective-permute-start.3
  30.9 2.5 collective-permute-done.3
  33.4 1.5 collective-permute-start.4
  35.5 3.5 %collective-permute-done.4 = bf16[2,2,2,16,768]{4,3,0,1,2:T(8,128)(2,1)S(1)} collective-permute-done((bf16[2,2,2,16,768]{4,3,0,1,2:T(8,128)(2,1)S(1)}, bf16[2,2,2,16,768]{4,3,0,1,2:T(8,128)(2,1)S(1)}, u32[]{:S(2)}, u32[]{:S(2)}) %collective-permute-start.4) | collective-permute-done | bytes 196640 | tf_op jit(solution)/shard_map/ppermute | solution.py:600
  39.1 1.6 collective-permute-done.5
  40.7 2.0 copy-done.3
  42.7 5.0 %shard_map.273 = (bf16[512,768]{1,0:T(8,128)(2,1)}, f32[384,512]{1,0:T(8,128)}, bf16[512,768]{1,0:T(8,128)(2,1)S(1)}, bf16[512,768]{1,0:T(8,128)(2,1)S(1)}, f32[...) custom-call(s32[1,64]{1,0:T(1,128)S(1)} %copy-done.23, ...), custom_call_target="tpu_custom_call" | custom-call | flops 2415919104 | bytes 11796480 | tf_op jit(solution)/shard_map/pallas_call | solution.py:844
  47.7 45.2 %shard_map.274 = (bf16[1024,768]{1,0:T(8,128)(2,1)}, bf16[1024,768]{1,0:T(8,128)(2,1)}, bf16[2,1024,3072]{2,1,0:T(8,128)(2,1)}, bf16[1024,768]{1,0:T(8,128)(2,1)...) custom-call(s32[1]{0:T(128)} %bitcast.core_ref, ...), custom_call_target="tpu_custom_call" | custom-call | flops 26575110144 | bytes 31457280 | tf_op jit(solution)/shard_map/pallas_call | solution.py:861
  92.9 3.2 %shard_map.275 = (f32[32,768]{1,0:T(8,128)}, bf16[32,768]{1,0:T(8,128)(2,1)}, bf16[32,896]{1,0:T(8,128)(2,1)S(1)}, bf16[32,768]{1,0:T(8,128)(2,1)}, f32[8,768]{1,0:T(8,128)}, /*index=5*/f32[8,768]{1,0:T(8,128)}) custom-call(f32[32,768]{1,0:T(8,128)S(1)} %get-tuple-element.265.dk3_ref, f32[32,768]{1,0:T(8,128)S(1)} %get-tuple-element.266.dv3_ref, ...), custom_call_target="tpu_custom_call" | custom-call | flops 1207959552 | bytes 5898240 | tf_op jit(solution)/shard_map/pallas_call | solution.py:875
  96.1 2.6 collective-permute-start.6
  98.7 10.4 %shard_map.276 = bf16[16,192,768]{2,1,0:T(8,128)(2,1)} custom-call(s32[1]{0:T(128)S(6)} %sub.3.which_ref, bf16[2,1024,3072]{2,1,0:T(8,128)(2,1)} %get-tuple-element.307.gd_ref, bf16[1024,768]{1,0:T(8,128)(2,1)} %get-tuple-element.308.h_ref, bf16[1024,768]{1,0:T(8,128)(2,1)} %bitcast.111), custom_call_target="tpu_custom_call" | custom-call | flops 4831838208 | bytes 15728640 | tf_op jit(solution)/shard_map/pallas_call | solution.py:892
  110.5 2.0 collective-permute-start.8
  112.5 3.2 %shard_map.277 = (bf16[8,96,768]{2,1,0:T(8,128)(2,1)S(1)}, bf16[8,96,768]{2,1,0:T(8,128)(2,1)S(1)}) custom-call(s32[1]{0:T(128)} %bitcast.25.pick_ref, bf16[16,96,768]{2,1,0:T(8,128)(2,1)} %copy-done.5, bf16[16,96,768]{2,1,0:T(8,128)(2,1)} %copy-done.34), custom_call_target="tpu_custom_call" | custom-call | bytes 9437184 | tf_op jit(solution)/shard_map/pallas_call | solution.py:946
  117.7 1.6 pad_maximum_fusion.4
  120.4 4.2 %collective-permute-done.9 = bf16[2,2,16,896]{3,2,0,1:T(8,128)(2,1)} collective-permute-done((bf16[2,2,16,896]{3,2,0,1:T(8,128)(2,1)}, bf16[2,2,16,896]{3,2,0,1:T(8,128)(2,1)}, u32[]{:S(2)}, u32[]{:S(2)}) %collective-permute-start.9) | collective-permute-done | bytes 114720 | tf_op jit(solution)/shard_map/ppermute | solution.py:600
  127.9 11.6 %shard_map.278 = (bf16[8,96,768]{2,1,0:T(8,128)(2,1)}, bf16[8,96,768]{2,1,0:T(8,128)(2,1)S(1)}, bf16[8,96,768]{2,1,0:T(8,128)(2,1)S(1)}, bf16[8,96,768]{2,1,0:T(8,128)(2,1)S(1)}) custom-call(s32[3]{0:T(128)S(1)} %add_add_fusion.which_ref, bf16[2,1024,3072]{2,1,0:T(8,128)(2,1)} %get-tuple-element.307.gd_ref, bf16[1024,768]{1,0:T(8,128)(2,1)} %get-tuple-element.308.h_ref, ...), custom_call_target="tpu_custom_call" | custom-call | flops 4831838208 | bytes 15728640 | tf_op jit(solution)/shard_map/pallas_call | solution.py:892
  139.6 1.6 collective-permute-start.14
  142.9 18.8 %shard_map.279 = (bf16[16,192,768]{2,1,0:T(8,128)(2,1)S(1)}, bf16[16,192,768]{2,1,0:T(8,128)(2,1)}, bf16[1024,768]{1,0:T(8,128)(2,1)}, bf16[1024,768]{1,0:T(8,12...) custom-call(s32[1]{0:T(128)} %bitcast.core_ref, ...), custom_call_target="tpu_custom_call" | custom-call | flops 4831838208 | bytes 23592960 | tf_op jit(solution)/shard_map/pallas_call | solution.py:961
  161.6 4.5 %collective-permute-done.14 = bf16[8,96,768]{2,1,0:T(8,128)(2,1)S(1)} collective-permute-done((bf16[8,96,768]{2,1,0:T(8,128)(2,1)}, bf16[8,96,768]{2,1,0:T(8,128)(2,1)S(1)}, u32[]{:S(2)}, u32[]{:S(2)}) %collective-permute-start.14) | collective-permute-done | bytes 1179680 | tf_op jit(solution)/shard_map/ppermute | solution.py:600
  168.4 1.9 shard_map.280
  171.8 4.3 %collective-permute-done.20 = bf16[16,192,768]{2,1,0:T(8,128)(2,1)S(1)} collective-permute-done((bf16[16,192,768]{2,1,0:T(8,128)(2,1)S(1)}, bf16[16,192,768]{2,1,0:T(8,128)(2,1)S(1)}, u32[]{:S(2)}, u32[]{:S(2)}) %collective-permute-start.20) | collective-permute-done | bytes 4718624 | tf_op jit(solution)/shard_map/ppermute | solution.py:600
  176.2 6.5 %shard_map.281 = (bf16[8,64,768]{2,1,0:T(8,128)(2,1)S(1)}, bf16[4,2,1,64,768]{4,3,2,1,0:T(8,128)(2,1)}, bf16[8,64,768]{2,1,0:T(8,128)(2,1)S(1)}, bf16[2,2,2,64,7...) custom-call(s32[3]{0:T(128)S(1)} %pad_add_fusion.1.pick_ref, ...), custom_call_target="tpu_custom_call" | custom-call | tf_op jit(solution)/shard_map/pallas_call | solution.py:707
  182.7 3.4 %collective-permute-done.17 = bf16[4,96,768]{2,1,0:T(8,128)(2,1)S(1)} collective-permute-done((bf16[4,96,768]{2,1,0:T(8,128)(2,1)S(1)}, bf16[4,96,768]{2,1,0:T(8,128)(2,1)S(1)}, u32[]{:S(2)}, u32[]{:S(2)}) %collective-permute-start.17) | collective-permute-done | bytes 589856 | tf_op jit(solution)/shard_map/ppermute | solution.py:600
  186.4 1.9 shard_map.282
  188.3 1.8 collective-permute-start.21
  190.6 1.5 collective-permute-start.23
  192.1 5.0 %collective-permute-done.21.refs_1_ = bf16[2,96,768]{2,1,0:T(8,128)(2,1)} collective-permute-done((bf16[2,96,768]{2,1,0:T(8,128)(2,1)}, bf16[2,96,768]{2,1,0:T(8,128)(2,1)}, u32[]{:S(2)}, u32[]{:S(2)}) %collective-permute-start.21) | collective-permute-done | bytes 294944 | tf_op jit(solution)/shard_map/ppermute | solution.py:600
  198.3 1.6 shard_map.283
  200.0 1.6 collective-permute-start.26
  201.5 1.5 collective-permute-start.27
  204.3 2.0 copy-done.2
  206.3 9.5 %shard_map.284 = (bf16[1024,768]{1,0:T(8,128)(2,1)}, bf16[32,768]{1,0:T(8,128)(2,1)}, f32[16,768]{1,0:T(8,128)S(1)}) custom-call(bf16[1024,768]{1,0:T(8,128)(2,1)} %bitcast.115, f32[1024,768]{1,0:T(8,128)} %get-tuple-element.405.dx1_ref, bf16[1024,768]{1,0:T(8,128)(2,1)} %get-tuple-element.406.dq3_ref, bf16[1024,768]{1,0:T(8,128)(2,1)} %get-tuple-element.407.dk1_ref, ...), custom_call_target="tpu_custom_call" | custom-call | flops 3623878656 | bytes 11010048 | tf_op jit(solution)/shard_map/pallas_call | solution.py:987
  217.7 3.6 %collective-permute-done.25 = f32[16,768]{1,0:T(8,128)S(1)} collective-permute-done((f32[16,768]{1,0:T(8,128)S(1)}, f32[16,768]{1,0:T(8,128)S(1)}, u32[]{:S(2)}, u32[]{:S(2)}) %collective-permute-start.25) | collective-permute-done | bytes 49184 | tf_op jit(solution)/shard_map/ppermute | solution.py:600
  221.2 6.2 %collective-permute-done.29.got_ref = bf16[288,768]{1,0:T(8,128)(2,1)S(1)} collective-permute-done((bf16[288,768]{1,0:T(8,128)(2,1)S(1)}, bf16[288,768]{1,0:T(8,128)(2,1)S(1)}, u32[]{:S(2)}, u32[]{:S(2)}) %collective-permute-start.29) | collective-permute-done | bytes 442400 | tf_op jit(solution)/shard_map/ppermute | solution.py:600
  227.4 1.5 collective-permute-done.28
  229.0 2.8 %shard_map.285 = (bf16[4,64,768]{2,1,0:T(8,128)(2,1)S(1)}, bf16[4,64,768]{2,1,0:T(8,128)(2,1)S(1)}, bf16[4,64,768]{2,1,0:T(8,128)(2,1)S(1)}, bf16[4,64,768]{2,1,...) custom-call(s32[3]{0:T(128)S(1)} %pad_add_fusion.pick_ref, ...), custom_call_target="tpu_custom_call" | custom-call | bytes 7077888 | tf_op jit(solution)/shard_map/pallas_call | solution.py:745
  233.9 1.5 collective-permute-start.30
  236.7 7.9 %collective-permute-done.30 = f32[16,768]{1,0:T(8,128)S(1)} collective-permute-done((f32[16,768]{1,0:T(8,128)S(1)}, f32[16,768]{1,0:T(8,128)S(1)}, u32[]{:S(2)}, u32[]{:S(2)}) %collective-permute-start.30) | collective-permute-done | bytes 49184 | tf_op jit(solution)/shard_map/ppermute | solution.py:600
  247.1 1.5 collective-permute-start.38
  249.2 3.9 %collective-permute-done.35 = f32[16,768]{1,0:T(8,128)S(1)} collective-permute-done((f32[16,768]{1,0:T(8,128)S(1)}, f32[16,768]{1,0:T(8,128)S(1)}, u32[]{:S(2)}, u32[]{:S(2)}) %collective-permute-start.35) | collective-permute-done | bytes 49184 | tf_op jit(solution)/shard_map/ppermute | solution.py:600
  253.2 2.0 collective-permute-start.40
  256.3 13.8 %collective-permute-done.39 = f32[16,768]{1,0:T(8,128)S(1)} collective-permute-done((f32[16,768]{1,0:T(8,128)S(1)}, f32[16,768]{1,0:T(8,128)S(1)}, u32[]{:S(2)}, u32[]{:S(2)}) %collective-permute-start.39) | collective-permute-done | bytes 49184 | tf_op jit(solution)/shard_map/ppermute | solution.py:600
  (164 shorter events, 34.7 us)
Async XLA Ops:
  13.0 6.7 %collective-permute-start = (bf16[32,768]{1,0:T(8,128)(2,1)S(1)}, bf16[32,768]{1,0:T(8,128)(2,1)S(1)}, u32[]{:S(2)}, u32[]{:S(2)}) collective-permute-start(bf16[32,768]{1,0:T(8,128)(2,1)S(1)} %get-tuple-element.338.a2_ref), channel_id=1, source_target_pairs={{0,16},{2,18},{4,20},{6,22},{8,24},{10,26},{12,28},{14,30},{16,0},... | collective-permute-start | bytes 147464 | tf_op jit(solution)/shard_map/ppermute | solution.py:600
  19.7 21.0 %copy-start.23 = (s32[1,64]{1,0:T(1,128)S(1)}, s32[1,64]{1,0:T(1,128)}, u32[]{:S(2)}) copy-start(s32[1,64]{1,0:T(1,128)} %image_ref.1) | copy-start | bytes 772
  20.4 4.9 %collective-permute-start.1 = (bf16[2,32,768]{2,1,0:T(8,128)(2,1)}, bf16[2,32,768]{2,1,0:T(8,128)(2,1)}, u32[]{:S(2)}, u32[]{:S(2)}) collective-permute-start(bf16[2,32,768]{2,1,0:T(8,128)(2,1)} %get-tuple-element.252), channel_id=1, source_target_pairs={{0,8},{2,10},{4,12},{6,14},{8,0},{10,2},{12,4},{14,6},{16,24},{18,... | collective-permute-start | bytes 294920 | tf_op jit(solution)/shard_map/ppermute | solution.py:600
  22.0 18.7 %copy-start.19 = (f32[32,768]{1,0:T(8,128)S(1)}, f32[32,768]{1,0:T(8,128)}, u32[]{:S(2)}) copy-start(f32[32,768]{1,0:T(8,128)} %copy-done.18) | copy-start | bytes 294916
  26.2 4.7 %collective-permute-start.2 = (bf16[2,2,16,768]{3,2,0,1:T(8,128)(2,1)S(1)}, bf16[2,2,16,768]{3,2,0,1:T(8,128)(2,1)S(1)}, u32[]{:S(2)}, u32[]{:S(2)}) collective-permute-start(bf16[2,2,16,768]{3,2,0,1:T(8,128)(2,1)S(1)} %get-tuple-element.253), channel_id=1, source_target_pairs={{0,4},{2,6},{4,0},{6,2},{8,12},{10,14},{12,8},{14,10},{16,20},{18,... | collective-permute-start | bytes 294920 | tf_op jit(solution)/shard_map/ppermute | solution.py:600
  28.0 5.4 %collective-permute-start.3 = (bf16[2,2,16,768]{3,2,0,1:T(8,128)(2,1)S(1)}, bf16[2,2,16,768]{3,2,0,1:T(8,128)(2,1)S(1)}, u32[]{:S(2)}, u32[]{:S(2)}) collective-permute-start(bf16[2,2,16,768]{3,2,0,1:T(8,128)(2,1)S(1)} %get-tuple-element.254), channel_id=1, source_target_pairs={{0,2},{2,0},{4,6},{6,4},{8,10},{10,8},{12,14},{14,12},{16,18},{18,... | collective-permute-start | bytes 294920 | tf_op jit(solution)/shard_map/ppermute | solution.py:600
  33.4 5.7 %collective-permute-start.4 = (bf16[2,2,2,16,768]{4,3,0,1,2:T(8,128)(2,1)S(1)}, bf16[2,2,2,16,768]{4,3,0,1,2:T(8,128)(2,1)S(1)}, u32[]{:S(2)}, u32[]{:S(2)}) collective-permute-start(bf16[2,2,2,16,768]{4,3,0,1,2:T(8,128)(2,1)S(1)} %pad_maximum_fusion.2), channel_id=1, source_target_pairs={{0,2},{2,0},{4,6},{6,4},{8,10},{10,8},{12,14},{14,12},{16,18},{18,... | collective-permute-start | bytes 589832 | tf_op jit(solution)/shard_map/ppermute | solution.py:600
  34.9 5.7 %collective-permute-start.5 = (bf16[2,2,2,16,768]{4,3,0,1,2:T(8,128)(2,1)S(1)}, bf16[2,2,2,16,768]{4,3,0,1,2:T(8,128)(2,1)S(1)}, u32[]{:S(2)}, u32[]{:S(2)}) collective-permute-start(bf16[2,2,2,16,768]{4,3,0,1,2:T(8,128)(2,1)S(1)} %pad_maximum_fusion.3), channel_id=1, source_target_pairs={{0,4},{2,6},{4,0},{6,2},{8,12},{10,14},{12,8},{14,10},{16,20},{18,... | collective-permute-start | bytes 589832 | tf_op jit(solution)/shard_map/ppermute | solution.py:600
  47.7 45.2 %copy-start.8 = (bf16[512,768]{1,0:T(8,128)(2,1)}, bf16[512,768]{1,0:T(8,128)(2,1)S(1)}, u32[]{:S(2)}) copy-start(bf16[512,768]{1,0:T(8,128)(2,1)S(1)} %get-tuple-element.323.k2_ref) | copy-start | bytes 2359300
  47.7 45.2 %copy-start.10 = (bf16[512,768]{1,0:T(8,128)(2,1)}, bf16[512,768]{1,0:T(8,128)(2,1)S(1)}, u32[]{:S(2)}) copy-start(bf16[512,768]{1,0:T(8,128)(2,1)S(1)} %get-tuple-element.324.v2_ref) | copy-start | bytes 2359300
  47.7 45.2 %copy-start.20 = (bf16[1,32,768]{2,1,0:T(8,128)(2,1)S(1)}, bf16[1,32,768]{2,1,0:T(8,128)(2,1)}, u32[]{:S(2)}) copy-start(bf16[1,32,768]{2,1,0:T(8,128)(2,1)} %param.31) | copy-start | bytes 147460
  96.1 13.0 %collective-permute-start.7 = (bf16[16,96,768]{2,1,0:T(8,128)(2,1)S(1)}, bf16[16,96,768]{2,1,0:T(8,128)(2,1)S(1)}, u32[]{:S(2)}, u32[]{:S(2)}) collective-permute-start(bf16[16,96,768]{2,1,0:T(8,128)(2,1)S(1)} %get-tuple-element.281), channel_id=1, source_target_pairs={{0,1},{1,0},{2,3},{3,2},{4,5},{5,4},{6,7},{7,6},{8,9},{9,8},{10,11... | collective-permute-start | bytes 7077896 | tf_op jit(solution)/shard_map/ppermute | solution.py:600
  96.1 12.9 %collective-permute-start.6 = (bf16[32,896]{1,0:T(8,128)(2,1)S(1)}, bf16[32,896]{1,0:T(8,128)(2,1)S(1)}, u32[]{:S(2)}, u32[]{:S(2)}) collective-permute-start(bf16[32,896]{1,0:T(8,128)(2,1)S(1)} %get-tuple-element.273), channel_id=1, source_target_pairs={{0,16},{2,18},{4,20},{6,22},{8,24},{10,26},{12,28},{14,30},{16,0},... | collective-permute-start | bytes 172040 | tf_op jit(solution)/shard_map/ppermute | solution.py:600
  109.0 18.9 %collective-permute-start.13 = (bf16[16,192,768]{2,1,0:T(8,128)(2,1)}, bf16[16,192,768]{2,1,0:T(8,128)(2,1)}, u32[]{:S(2)}, u32[]{:S(2)}) collective-permute-start(bf16[16,192,768]{2,1,0:T(8,128)(2,1)} %shard_map.276), channel_id=1, source_target_pairs={{0,1},{1,0},{2,3},{3,2},{4,5},{5,4},{6,7},{7,6},{8,9},{9,8},{10,11... | collective-permute-start | bytes 14155784 | tf_op jit(solution)/shard_map/ppermute | solution.py:600
  110.5 7.2 %collective-permute-start.8 = (bf16[2,32,896]{2,1,0:T(8,128)(2,1)}, bf16[2,32,896]{2,1,0:T(8,128)(2,1)}, u32[]{:S(2)}, u32[]{:S(2)}) collective-permute-start(bf16[2,32,896]{2,1,0:T(8,128)(2,1)} %get-tuple-element.282), channel_id=1, source_target_pairs={{0,8},{2,10},{4,12},{6,14},{8,0},{10,2},{12,4},{14,6},{16,24},{18,... | collective-permute-start | bytes 344072 | tf_op jit(solution)/shard_map/ppermute | solution.py:600
  119.3 5.3 %collective-permute-start.9 = (bf16[2,2,16,896]{3,2,0,1:T(8,128)(2,1)}, bf16[2,2,16,896]{3,2,0,1:T(8,128)(2,1)}, u32[]{:S(2)}, u32[]{:S(2)}) collective-permute-start(bf16[2,2,16,896]{3,2,0,1:T(8,128)(2,1)} %get-tuple-element.289), channel_id=1, source_target_pairs={{0,4},{2,6},{4,0},{6,2},{8,12},{10,14},{12,8},{14,10},{16,20},{18,... | collective-permute-start | bytes 344072 | tf_op jit(solution)/shard_map/ppermute | solution.py:600
  119.8 5.7 %collective-permute-start.10 = (bf16[2,2,16,896]{3,2,0,1:T(8,128)(2,1)}, bf16[2,2,16,896]{3,2,0,1:T(8,128)(2,1)S(1)}, u32[]{:S(2)}, u32[]{:S(2)}) collective-permute-start(bf16[2,2,16,896]{3,2,0,1:T(8,128)(2,1)} %get-tuple-element.290), channel_id=1, source_target_pairs={{0,2},{2,0},{4,6},{6,4},{8,10},{10,8},{12,14},{14,12},{16,18},{18,... | collective-permute-start | bytes 344072 | tf_op jit(solution)/shard_map/ppermute | solution.py:600
  125.5 14.0 %collective-permute-start.11 = (bf16[2,2,2,16,896]{4,3,0,1,2:T(8,128)(2,1)S(1)}, bf16[2,2,2,16,896]{4,3,0,1,2:T(8,128)(2,1)S(1)}, u32[]{:S(2)}, u32[]{:S(2)}) collective-permute-start(bf16[2,2,2,16,896]{4,3,0,1,2:T(8,128)(2,1)S(1)} %pad_maximum_fusion), channel_id=1, source_target_pairs={{0,2},{2,0},{4,6},{6,4},{8,10},{10,8},{12,14},{14,12},{16,18},{18,... | collective-permute-start | bytes 688136 | tf_op jit(solution)/shard_map/ppermute | solution.py:600
  127.1 12.5 %collective-permute-start.12 = (bf16[2,2,2,16,896]{4,3,0,1,2:T(8,128)(2,1)S(1)}, bf16[2,2,2,16,896]{4,3,0,1,2:T(8,128)(2,1)S(1)}, u32[]{:S(2)}, u32[]{:S(2)}) collective-permute-start(bf16[2,2,2,16,896]{4,3,0,1,2:T(8,128)(2,1)S(1)} %pad_maximum_fusion.1), channel_id=1, source_target_pairs={{0,4},{2,6},{4,0},{6,2},{8,12},{10,14},{12,8},{14,10},{16,20},{18,... | collective-permute-start | bytes 688136 | tf_op jit(solution)/shard_map/ppermute | solution.py:600
  139.6 26.5 %collective-permute-start.14 = (bf16[8,96,768]{2,1,0:T(8,128)(2,1)}, bf16[8,96,768]{2,1,0:T(8,128)(2,1)S(1)}, u32[]{:S(2)}, u32[]{:S(2)}) collective-permute-start(bf16[8,96,768]{2,1,0:T(8,128)(2,1)} %get-tuple-element.351), channel_id=1, source_target_pairs={{0,2},{2,0},{4,6},{6,4},{8,10},{10,8},{12,14},{14,12},{16,18},{18,... | collective-permute-start | bytes 3538952 | tf_op jit(solution)/shard_map/ppermute | solution.py:600
  141.2 25.9 %collective-permute-start.15 = (bf16[8,96,768]{2,1,0:T(8,128)(2,1)S(1)}, bf16[8,96,768]{2,1,0:T(8,128)(2,1)S(1)}, u32[]{:S(2)}, u32[]{:S(2)}) collective-permute-start(bf16[8,96,768]{2,1,0:T(8,128)(2,1)S(1)} %get-tuple-element.352), channel_id=1, source_target_pairs={{0,4},{2,6},{4,0},{6,2},{8,12},{10,14},{12,8},{14,10},{16,20},{18,... | collective-permute-start | bytes 3538952 | tf_op jit(solution)/shard_map/ppermute | solution.py:600
  142.4 25.9 %collective-permute-start.16 = (bf16[8,96,768]{2,1,0:T(8,128)(2,1)S(1)}, bf16[8,96,768]{2,1,0:T(8,128)(2,1)S(1)}, u32[]{:S(2)}, u32[]{:S(2)}) collective-permute-start(bf16[8,96,768]{2,1,0:T(8,128)(2,1)S(1)} %copy-done.27), channel_id=1, source_target_pairs={{0,8},{2,10},{4,12},{6,14},{8,0},{10,2},{12,4},{14,6},{16,24},{18,... | collective-permute-start | bytes 3538952 | tf_op jit(solution)/shard_map/ppermute | solution.py:600
  142.8 25.5 %copy-start.7 = (bf16[8,96,768]{2,1,0:T(8,128)(2,1)S(1)}, bf16[8,96,768]{2,1,0:T(8,128)(2,1)}, u32[]{:S(2)}) copy-start(bf16[8,96,768]{2,1,0:T(8,128)(2,1)} %copy-done.6) | copy-start | bytes 3538948
  168.3 7.9 %collective-permute-start.20 = (bf16[16,192,768]{2,1,0:T(8,128)(2,1)S(1)}, bf16[16,192,768]{2,1,0:T(8,128)(2,1)S(1)}, u32[]{:S(2)}, u32[]{:S(2)}) collective-permute-start(bf16[16,192,768]{2,1,0:T(8,128)(2,1)S(1)} %get-tuple-element.369), channel_id=1, source_target_pairs={{0,1},{1,0},{2,3},{3,2},{4,5},{5,4},{6,7},{7,6},{8,9},{9,8},{10,11... | collective-permute-start | bytes 14155784 | tf_op jit(solution)/shard_map/ppermute | solution.py:600
  170.3 15.8 %collective-permute-start.17 = (bf16[4,96,768]{2,1,0:T(8,128)(2,1)S(1)}, bf16[4,96,768]{2,1,0:T(8,128)(2,1)S(1)}, u32[]{:S(2)}, u32[]{:S(2)}) collective-permute-start(bf16[4,96,768]{2,1,0:T(8,128)(2,1)S(1)} %get-tuple-element.363), channel_id=1, source_target_pairs={{0,4},{2,6},{4,0},{6,2},{8,12},{10,14},{12,8},{14,10},{16,20},{18,... | collective-permute-start | bytes 1769480 | tf_op jit(solution)/shard_map/ppermute | solution.py:600
  170.9 15.5 %collective-permute-start.18 = (bf16[4,96,768]{2,1,0:T(8,128)(2,1)S(1)}, bf16[4,96,768]{2,1,0:T(8,128)(2,1)S(1)}, u32[]{:S(2)}, u32[]{:S(2)}) collective-permute-start(bf16[4,96,768]{2,1,0:T(8,128)(2,1)S(1)} %get-tuple-element.365), channel_id=1, source_target_pairs={{0,8},{2,10},{4,12},{6,14},{8,0},{10,2},{12,4},{14,6},{16,24},{18,... | collective-permute-start | bytes 1769480 | tf_op jit(solution)/shard_map/ppermute | solution.py:600
  171.2 15.2 %collective-permute-start.19 = (bf16[4,96,768]{2,1,0:T(8,128)(2,1)S(1)}, bf16[4,96,768]{2,1,0:T(8,128)(2,1)S(1)}, u32[]{:S(2)}, u32[]{:S(2)}) collective-permute-start(bf16[4,96,768]{2,1,0:T(8,128)(2,1)S(1)} %get-tuple-element.367), channel_id=1, source_target_pairs={{0,2},{2,0},{4,6},{6,4},{8,10},{10,8},{12,14},{14,12},{16,18},{18,... | collective-permute-start | bytes 1769480 | tf_op jit(solution)/shard_map/ppermute | solution.py:600
  188.3 8.7 %collective-permute-start.21 = (bf16[2,96,768]{2,1,0:T(8,128)(2,1)}, bf16[2,96,768]{2,1,0:T(8,128)(2,1)}, u32[]{:S(2)}, u32[]{:S(2)}) collective-permute-start(bf16[2,96,768]{2,1,0:T(8,128)(2,1)} %get-tuple-element.391), channel_id=1, source_target_pairs={{0,8},{2,10},{4,12},{6,14},{8,0},{10,2},{12,4},{14,6},{16,24},{18,... | collective-permute-start | bytes 884744 | tf_op jit(solution)/shard_map/ppermute | solution.py:600
  190.1 8.0 %collective-permute-start.22 = (bf16[2,96,768]{2,1,0:T(8,128)(2,1)}, bf16[2,96,768]{2,1,0:T(8,128)(2,1)}, u32[]{:S(2)}, u32[]{:S(2)}) collective-permute-start(bf16[2,96,768]{2,1,0:T(8,128)(2,1)} %get-tuple-element.393), channel_id=1, source_target_pairs={{0,2},{2,0},{4,6},{6,4},{8,10},{10,8},{12,14},{14,12},{16,18},{18,... | collective-permute-start | bytes 884744 | tf_op jit(solution)/shard_map/ppermute | solution.py:600
  190.6 7.8 %collective-permute-start.23 = (bf16[2,96,768]{2,1,0:T(8,128)(2,1)}, bf16[2,96,768]{2,1,0:T(8,128)(2,1)}, u32[]{:S(2)}, u32[]{:S(2)}) collective-permute-start(bf16[2,96,768]{2,1,0:T(8,128)(2,1)} %get-tuple-element.395), channel_id=1, source_target_pairs={{0,4},{2,6},{4,0},{6,2},{8,12},{10,14},{12,8},{14,10},{16,20},{18,... | collective-permute-start | bytes 884744 | tf_op jit(solution)/shard_map/ppermute | solution.py:600
  200.0 27.5 %collective-permute-start.26 = (bf16[8,64,768]{2,1,0:T(8,128)(2,1)}, bf16[8,64,768]{2,1,0:T(8,128)(2,1)S(1)}, u32[]{:S(2)}, u32[]{:S(2)}) collective-permute-start(bf16[8,64,768]{2,1,0:T(8,128)(2,1)} %copy-done.32), channel_id=1, source_target_pairs={{0,2},{2,0},{4,6},{6,4},{8,10},{10,8},{12,14},{14,12},{16,18},{18,... | collective-permute-start | bytes 2359304 | tf_op jit(solution)/shard_map/ppermute | solution.py:600
  201.5 25.9 %collective-permute-start.27 = (bf16[8,64,768]{2,1,0:T(8,128)(2,1)S(1)}, bf16[8,64,768]{2,1,0:T(8,128)(2,1)S(1)}, u32[]{:S(2)}, u32[]{:S(2)}) collective-permute-start(bf16[8,64,768]{2,1,0:T(8,128)(2,1)S(1)} %copy-done.31), channel_id=1, source_target_pairs={{0,4},{2,6},{4,0},{6,2},{8,12},{10,14},{12,8},{14,10},{16,20},{18,... | collective-permute-start | bytes 2359304 | tf_op jit(solution)/shard_map/ppermute | solution.py:600
  203.0 26.0 %collective-permute-start.28 = (bf16[8,64,768]{2,1,0:T(8,128)(2,1)S(1)}, bf16[8,64,768]{2,1,0:T(8,128)(2,1)S(1)}, u32[]{:S(2)}, u32[]{:S(2)}) collective-permute-start(bf16[8,64,768]{2,1,0:T(8,128)(2,1)S(1)} %copy-done.29), channel_id=1, source_target_pairs={{0,8},{2,10},{4,12},{6,14},{8,0},{10,2},{12,4},{14,6},{16,24},{18,... | collective-permute-start | bytes 2359304 | tf_op jit(solution)/shard_map/ppermute | solution.py:600
  203.6 23.8 %collective-permute-start.29 = (bf16[288,768]{1,0:T(8,128)(2,1)S(1)}, bf16[288,768]{1,0:T(8,128)(2,1)S(1)}, u32[]{:S(2)}, u32[]{:S(2)}) collective-permute-start(bf16[288,768]{1,0:T(8,128)(2,1)S(1)} %get-tuple-element.429), channel_id=1, source_target_pairs={{0,16},{2,18},{4,20},{6,22},{8,24},{10,26},{12,28},{14,30},{16,0},... | collective-permute-start | bytes 1327112 | tf_op jit(solution)/shard_map/ppermute | solution.py:600
  215.8 1.3 collective-permute-start.24
  217.1 4.2 %collective-permute-start.25 = (f32[16,768]{1,0:T(8,128)S(1)}, f32[16,768]{1,0:T(8,128)S(1)}, u32[]{:S(2)}, u32[]{:S(2)}) collective-permute-start(f32[16,768]{1,0:T(8,128)S(1)} %add.30), channel_id=1, source_target_pairs={{0,2},{2,0},{4,6},{6,4},{8,10},{10,8},{12,14},{14,12},{16,18},{18,... | collective-permute-start | bytes 147464 | tf_op jit(solution)/shard_map/ppermute | solution.py:600
  231.9 3.4 %collective-permute-start.34 = (bf16[288,768]{1,0:T(8,128)(2,1)S(1)}, bf16[288,768]{1,0:T(8,128)(2,1)S(1)}, u32[]{:S(2)}, u32[]{:S(2)}) collective-permute-start(bf16[288,768]{1,0:T(8,128)(2,1)S(1)} %shard_map.286.mine_ref), channel_id=1, source_target_pairs={{0,1},{1,0},{2,3},{3,2},{4,5},{5,4},{6,7},{7,6},{8,9},{9,8},{10,11... | collective-permute-start | bytes 1327112 | tf_op jit(solution)/shard_map/ppermute | solution.py:600
  232.0 12.6 %collective-permute-start.31 = (bf16[4,64,768]{2,1,0:T(8,128)(2,1)S(1)}, bf16[4,64,768]{2,1,0:T(8,128)(2,1)S(1)}, u32[]{:S(2)}, u32[]{:S(2)}) collective-permute-start(bf16[4,64,768]{2,1,0:T(8,128)(2,1)S(1)} %get-tuple-element.438), channel_id=1, source_target_pairs={{0,4},{2,6},{4,0},{6,2},{8,12},{10,14},{12,8},{14,10},{16,20},{18,... | collective-permute-start | bytes 1179656 | tf_op jit(solution)/shard_map/ppermute | solution.py:600
  232.6 12.0 %collective-permute-start.32 = (bf16[4,64,768]{2,1,0:T(8,128)(2,1)S(1)}, bf16[4,64,768]{2,1,0:T(8,128)(2,1)S(1)}, u32[]{:S(2)}, u32[]{:S(2)}) collective-permute-start(bf16[4,64,768]{2,1,0:T(8,128)(2,1)S(1)} %get-tuple-element.439), channel_id=1, source_target_pairs={{0,8},{2,10},{4,12},{6,14},{8,0},{10,2},{12,4},{14,6},{16,24},{18,... | collective-permute-start | bytes 1179656 | tf_op jit(solution)/shard_map/ppermute | solution.py:600
  233.3 11.3 %collective-permute-start.33 = (bf16[4,64,768]{2,1,0:T(8,128)(2,1)S(1)}, bf16[4,64,768]{2,1,0:T(8,128)(2,1)S(1)}, u32[]{:S(2)}, u32[]{:S(2)}) collective-permute-start(bf16[4,64,768]{2,1,0:T(8,128)(2,1)S(1)} %get-tuple-element.440), channel_id=1, source_target_pairs={{0,2},{2,0},{4,6},{6,4},{8,10},{10,8},{12,14},{14,12},{16,18},{18,... | collective-permute-start | bytes 1179656 | tf_op jit(solution)/shard_map/ppermute | solution.py:600
  233.9 10.7 %collective-permute-start.30 = (f32[16,768]{1,0:T(8,128)S(1)}, f32[16,768]{1,0:T(8,128)S(1)}, u32[]{:S(2)}, u32[]{:S(2)}) collective-permute-start(f32[16,768]{1,0:T(8,128)S(1)} %add.31), channel_id=1, source_target_pairs={{0,4},{2,6},{4,0},{6,2},{8,12},{10,14},{12,8},{14,10},{16,20},{18,... | collective-permute-start | bytes 147464 | tf_op jit(solution)/shard_map/ppermute | solution.py:600
  245.5 7.6 %collective-permute-start.36 = (bf16[2,64,768]{2,1,0:T(8,128)(2,1)S(1)}, bf16[2,64,768]{2,1,0:T(8,128)(2,1)S(1)}, u32[]{:S(2)}, u32[]{:S(2)}) collective-permute-start(bf16[2,64,768]{2,1,0:T(8,128)(2,1)S(1)} %get-tuple-element.458), channel_id=1, source_target_pairs={{0,8},{2,10},{4,12},{6,14},{8,0},{10,2},{12,4},{14,6},{16,24},{18,... | collective-permute-start | bytes 589832 | tf_op jit(solution)/shard_map/ppermute | solution.py:600
  246.5 6.6 %collective-permute-start.37 = (bf16[2,64,768]{2,1,0:T(8,128)(2,1)S(1)}, bf16[2,64,768]{2,1,0:T(8,128)(2,1)S(1)}, u32[]{:S(2)}, u32[]{:S(2)}) collective-permute-start(bf16[2,64,768]{2,1,0:T(8,128)(2,1)S(1)} %get-tuple-element.459), channel_id=1, source_target_pairs={{0,2},{2,0},{4,6},{6,4},{8,10},{10,8},{12,14},{14,12},{16,18},{18,... | collective-permute-start | bytes 589832 | tf_op jit(solution)/shard_map/ppermute | solution.py:600
  247.1 6.0 %collective-permute-start.38 = (bf16[2,64,768]{2,1,0:T(8,128)(2,1)S(1)}, bf16[2,64,768]{2,1,0:T(8,128)(2,1)S(1)}, u32[]{:S(2)}, u32[]{:S(2)}) collective-permute-start(bf16[2,64,768]{2,1,0:T(8,128)(2,1)S(1)} %get-tuple-element.460), channel_id=1, source_target_pairs={{0,4},{2,6},{4,0},{6,2},{8,12},{10,14},{12,8},{14,10},{16,20},{18,... | collective-permute-start | bytes 589832 | tf_op jit(solution)/shard_map/ppermute | solution.py:600
  248.5 4.5 %collective-permute-start.35 = (f32[16,768]{1,0:T(8,128)S(1)}, f32[16,768]{1,0:T(8,128)S(1)}, u32[]{:S(2)}, u32[]{:S(2)}) collective-permute-start(f32[16,768]{1,0:T(8,128)S(1)} %add.32), channel_id=1, source_target_pairs={{0,8},{2,10},{4,12},{6,14},{8,0},{10,2},{12,4},{14,6},{16,24},{18,... | collective-permute-start | bytes 147464 | tf_op jit(solution)/shard_map/ppermute | solution.py:600
  253.2 16.9 %collective-permute-start.40 = (bf16[192,768]{1,0:T(8,128)(2,1)S(1)}, bf16[192,768]{1,0:T(8,128)(2,1)S(1)}, u32[]{:S(2)}, u32[]{:S(2)}) collective-permute-start(bf16[192,768]{1,0:T(8,128)(2,1)S(1)} %get-tuple-element.473), channel_id=1, source_target_pairs={{0,16},{2,18},{4,20},{6,22},{8,24},{10,26},{12,28},{14,30},{16,0},... | collective-permute-start | bytes 884744 | tf_op jit(solution)/shard_map/ppermute | solution.py:600
  255.2 14.9 %collective-permute-start.39 = (f32[16,768]{1,0:T(8,128)S(1)}, f32[16,768]{1,0:T(8,128)S(1)}, u32[]{:S(2)}, u32[]{:S(2)}) collective-permute-start(f32[16,768]{1,0:T(8,128)S(1)} %add.33), channel_id=1, source_target_pairs={{0,16},{2,18},{4,20},{6,22},{8,24},{10,26},{12,28},{14,30},{16,0},... | collective-permute-start | bytes 147464 | tf_op jit(solution)/shard_map/ppermute | solution.py:600
  270.2 1.6 collective-permute-start.41
  (32 other events, 277.5 us)

commit v5 on v4

--- a/solution.py
+++ b/solution.py
@@ -208,7 +208,7 @@
 def patch_kernel(
     chunk, size, core_ref, x_ref, q3_ref, cot_ref, k3_ref, v3_ref, norm_ref, wo_ref, up_ref, down_ref, b1_ref, b3_ref,
     out_ref, h_ref, gd_ref, dq3_ref, dx1_ref, dk3_ref, dv3_ref, other_ref, mine_ref,
-    gain_ref, shift_ref, o3_ref, e3_ref,
+    gain_ref, shift_ref, o3_ref, e3_ref, b1_all_ref, dq3_all_ref,
 ):
     step = pl.program_id(0)
     tokens = x_ref.shape[0]
@@ -228,6 +228,7 @@
     mixed = [narrow(mm_tn(narrow(w.reshape(HL, size)), v)) for w, v in zip(weights, values)]
     o3 = jnp.concatenate(mixed, 0) if each > 1 else mixed[0]
     o3_ref[here, :] = o3
+    b1_all_ref[here, :] = b1_ref[...]
     x1 = x_ref[...].astype(F32) + mm(o3, wo_ref[...])
     unit, inverse = norm_parts(x1)
     gain = norm_ref[4:5]
@@ -271,7 +272,9 @@
         dshares = mm_nt(vx, grad).reshape(HEADS, LAT, size)
         inner = jnp.sum(shares * dshares, axis=1, keepdims=True)
         dscores = narrow((shares * (dshares - inner)).reshape(HL, size))
-        dq3_ref[place, :] = narrow(mm_tn(dscores, kx) * FACTOR)
+        dq3 = narrow(mm_tn(dscores, kx) * FACTOR)
+        dq3_ref[rows] = dq3
+        dq3_all_ref[place, :] = dq3
         dv3_ref[own, :] = narrow(collapse(mm(narrow(shares.reshape(HL, size)), grad))).astype(F32)
         dk3_ref[own, :] = narrow(collapse(mm(dscores, q3_ref[rows])) * FACTOR).astype(F32)
 
@@ -279,7 +282,7 @@
     def _():
         b3 = b3_ref[...]
         put_units(core_ref, other_ref, mine_ref,
-                  [[(o3_ref, e3_ref), (b3, narrow(dk3_ref[...]))], [(b1_ref, dq3_ref), (b3, narrow(dv3_ref[...]))]])
+                  [[(o3_ref, e3_ref), (b3, narrow(dk3_ref[...]))], [(b1_all_ref, dq3_all_ref), (b3, narrow(dv3_ref[...]))]])
 
 
 STAT = 2 * HEADS
@@ -822,7 +825,7 @@
              far_lat, full_lat, low_lat],
             2 * unit_flops, 12 * tokens * D,
             [pltpu.VMEM((lat, D), F32)],
-        )(in_hbm(x), z, norms, in_hbm(read_in), in_hbm(read_out))
+        )(in_hbm(x), in_hbm(z), norms, in_hbm(read_in), in_hbm(read_out))
 
         q3 = []
 
@@ -861,14 +864,14 @@
         out_patches, h, gd, dq3, dx1, dk3, dv3, early_other, early_mine, gain4, shift4 = call(
             functools.partial(patch_kernel, D, size), (groups // each,),
             [smem] + [spans, spans, spans, lat_spec, lat_spec, norm_spec, square,
-             resident, resident, whole((tokens, D)), lat_spec],
+             resident, resident, spans, lat_spec],
             [spans, spans,
              pl.BlockSpec((2, each * size, hidden), lambda g: (0, g, 0), pipeline_mode=pl.Buffered(1 if each > 1 else 2)),
-             whole((tokens, D)), spans, lat_spec, lat_spec, whole(early_shape), whole(early_shape), fold_spec, fold_spec],
+             spans, spans, lat_spec, lat_spec, whole(early_shape), whole(early_shape), fold_spec, fold_spec],
             [low_patch, far_patch, pltpu.HBM((2, tokens, hidden), BF),
              far_patch, pltpu.HBM((tokens, D), F32), full_lat, full_lat, shaped(early_shape, BF), shaped(early_shape, BF),
              far_fold, far_fold],
-            unit_flops * 22, 40 * tokens * D, [pltpu.VMEM((tokens, D), BF)] * 2, vmem=46,
+            unit_flops * 22, 40 * tokens * D, [pltpu.VMEM((tokens, D), BF)] * 4, vmem=48,
         )(core_at, in_hbm(x), in_hbm(q3), in_hbm(cot), k3, v3, norms, write_out, feed_up, feed_down, in_hbm(b1), b3)
 
         width = D + 128

time: 279 us -> 278 us (level)
    unnamed x76 -> x72, local copies, waits for them, and re-layouts: 7.21 us -> 6.32 us
where the time goes in v5:
time: 278 us; the launch traced here: 273 us
  Pallas kernels  136 us (49%)
  waiting for transfers between devices  76.4 us (27%)
  starting transfers between devices  41.8 us (15%)
  other arithmetic  7.3 us (3%)
  local copies, waits for them, and re-layouts  7.14 us (3%)
    ppermute x42, waiting for transfers between devices, swap(): return lax.ppermute(tensor, axis, [(i, i ^ 1 << bit) for i in range(count)])  76.4 us
    pallas_call x1, Pallas kernels, body(): call(functools.partial(patch_kernel, D, size), (groups // each,), [smem]...  45.2 us
    ppermute x42, starting transfers between devices, swap(): return lax.ppermute(tensor, axis, [(i, i ^ 1 << bit) for i in range(count)])  41.8 us
    pallas_call x2, Pallas kernels, feed_call(): pl.pallas_call(kernel, grid_spec=pltpu.PrefetchScalarGridSpec(num_scalar_...  22 us
    pallas_call x1, Pallas kernels, body(): call(tail_kernel, grid, [smem] + [whole(piece_shape + (width,))] * 4 + [w...  18.8 us
    pallas_call x1, Pallas kernels, body(): call(read_forward_kernel, grid, [patch_spec, lat_spec, norm_spec, three,...  10.7 us
    pallas_call x1, Pallas kernels, body(): call(input_back_kernel, grid, [patch_spec] * 5 + [lat_spec] * 3 + [norm_s...  9.52 us
    pallas_call x4, Pallas kernels, send(): call(functools.partial(stage_kernel, len(self.parts)), (lead,), [pl.Block...  7.51 us
  transfers between devices with their start and end apart: 42, of which 23 were waited for; matrix products, arithmetic and copies ran while one was open for 3% of the time, Pallas kernels for 23%

profile of v5, /device:TPU:0, one launch (start us, length us, event | category | flops | bytes accessed | tf_op | source)
XLA Modules:
  0.0 272.5 jit_solution(5349000325759839595)
XLA Ops:
  1.5 10.7 %shard_map.272 = (bf16[32,768]{1,0:T(8,128)(2,1)}, f32[32,768]{1,0:T(8,128)}, bf16[1024,768]{1,0:T(8,128)(2,1)S(1)}, bf16[1024,768]{1,0:T(8,128)(2,1)}, bf16[102...) custom-call(bf16[1024,768]{1,0:T(8,128)(2,1)} %bitcast.113, ...), custom_call_target="tpu_custom_call" | custom-call | flops 2415919104 | bytes 9437184 | tf_op jit(solution)/shard_map/pallas_call | solution.py:820
  12.2 4.1 %collective-permute-start = (bf16[32,768]{1,0:T(8,128)(2,1)S(1)}, bf16[32,768]{1,0:T(8,128)(2,1)S(1)}, u32[]{:S(2)}, u32[]{:S(2)}) collective-permute-start(bf16[32,768]{1,0:T(8,128)(2,1)S(1)} %get-tuple-element.338.a2_ref), channel_id=1, source_target_pairs={{0,16},{2,18},{4,20},{6,22},{8,24},{10,26},{12,28},{14,30},{16,0},... | collective-permute-start | bytes 147464 | tf_op jit(solution)/shard_map/ppermute | solution.py:603
  16.4 2.6 convolution_convert_fusion.q3_ref
  19.7 1.6 collective-permute-start.1
  21.3 3.3 %collective-permute-done.1 = bf16[2,32,768]{2,1,0:T(8,128)(2,1)} collective-permute-done((bf16[2,32,768]{2,1,0:T(8,128)(2,1)}, bf16[2,32,768]{2,1,0:T(8,128)(2,1)}, u32[]{:S(2)}, u32[]{:S(2)}) %collective-permute-start.1) | collective-permute-done | bytes 98336 | tf_op jit(solution)/shard_map/ppermute | solution.py:603
  25.5 1.7 collective-permute-start.2
  27.2 1.5 collective-permute-start.3
  30.2 2.3 collective-permute-done.3
  32.5 1.5 collective-permute-start.4
  34.7 3.5 %collective-permute-done.4 = bf16[2,2,2,16,768]{4,3,0,1,2:T(8,128)(2,1)S(1)} collective-permute-done((bf16[2,2,2,16,768]{4,3,0,1,2:T(8,128)(2,1)S(1)}, bf16[2,2,2,16,768]{4,3,0,1,2:T(8,128)(2,1)S(1)}, u32[]{:S(2)}, u32[]{:S(2)}) %collective-permute-start.4) | collective-permute-done | bytes 196640 | tf_op jit(solution)/shard_map/ppermute | solution.py:603
  38.2 1.6 collective-permute-done.5
  39.8 2.0 copy-done.3
  41.8 5.0 %shard_map.273 = (bf16[512,768]{1,0:T(8,128)(2,1)}, f32[384,512]{1,0:T(8,128)}, bf16[512,768]{1,0:T(8,128)(2,1)S(1)}, bf16[512,768]{1,0:T(8,128)(2,1)S(1)}, f32[...) custom-call(s32[1,64]{1,0:T(1,128)S(1)} %copy-done.21, ...), custom_call_target="tpu_custom_call" | custom-call | flops 2415919104 | bytes 11796480 | tf_op jit(solution)/shard_map/pallas_call | solution.py:847
  46.8 45.2 %shard_map.274 = (bf16[1024,768]{1,0:T(8,128)(2,1)}, bf16[1024,768]{1,0:T(8,128)(2,1)}, bf16[2,1024,3072]{2,1,0:T(8,128)(2,1)}, bf16[1024,768]{1,0:T(8,128)(2,1)...) custom-call(s32[1]{0:T(128)} %bitcast.core_ref, ...), custom_call_target="tpu_custom_call" | custom-call | flops 26575110144 | bytes 31457280 | tf_op jit(solution)/shard_map/pallas_call | solution.py:864
  92.1 3.2 %shard_map.275 = (f32[32,768]{1,0:T(8,128)}, bf16[32,768]{1,0:T(8,128)(2,1)}, bf16[32,896]{1,0:T(8,128)(2,1)S(1)}, bf16[32,768]{1,0:T(8,128)(2,1)}, f32[8,768]{1,0:T(8,128)}, /*index=5*/f32[8,768]{1,0:T(8,128)}) custom-call(f32[32,768]{1,0:T(8,128)S(1)} %get-tuple-element.265.dk3_ref, f32[32,768]{1,0:T(8,128)S(1)} %get-tuple-element.266.dv3_ref, ...), custom_call_target="tpu_custom_call" | custom-call | flops 1207959552 | bytes 5898240 | tf_op jit(solution)/shard_map/pallas_call | solution.py:878
  95.3 2.6 collective-permute-start.6
  97.9 10.4 %shard_map.276 = bf16[16,192,768]{2,1,0:T(8,128)(2,1)} custom-call(s32[1]{0:T(128)S(6)} %sub.3.which_ref, bf16[2,1024,3072]{2,1,0:T(8,128)(2,1)} %get-tuple-element.307.gd_ref, bf16[1024,768]{1,0:T(8,128)(2,1)} %get-tuple-element.308.h_ref, bf16[1024,768]{1,0:T(8,128)(2,1)} %bitcast.111), custom_call_target="tpu_custom_call" | custom-call | flops 4831838208 | bytes 15728640 | tf_op jit(solution)/shard_map/pallas_call | solution.py:895
  109.8 1.9 collective-permute-start.8
  111.7 3.2 %shard_map.277 = (bf16[8,96,768]{2,1,0:T(8,128)(2,1)S(1)}, bf16[8,96,768]{2,1,0:T(8,128)(2,1)S(1)}) custom-call(s32[1]{0:T(128)} %bitcast.25.pick_ref, bf16[16,96,768]{2,1,0:T(8,128)(2,1)} %get-tuple-element.285.keep_ref, bf16[16,96,768]{2,1,0:T(8,128)(2,1)} %copy-done.32), custom_call_target="tpu_custom_call" | custom-call | bytes 9437184 | tf_op jit(solution)/shard_map/pallas_call | solution.py:949
  117.0 1.6 pad_maximum_fusion.4
  119.6 4.2 %collective-permute-done.9 = bf16[2,2,16,896]{3,2,0,1:T(8,128)(2,1)} collective-permute-done((bf16[2,2,16,896]{3,2,0,1:T(8,128)(2,1)}, bf16[2,2,16,896]{3,2,0,1:T(8,128)(2,1)}, u32[]{:S(2)}, u32[]{:S(2)}) %collective-permute-start.9) | collective-permute-done | bytes 114720 | tf_op jit(solution)/shard_map/ppermute | solution.py:603
  127.2 11.7 %shard_map.278 = (bf16[8,96,768]{2,1,0:T(8,128)(2,1)}, bf16[8,96,768]{2,1,0:T(8,128)(2,1)S(1)}, bf16[8,96,768]{2,1,0:T(8,128)(2,1)S(1)}, bf16[8,96,768]{2,1,0:T(8,128)(2,1)S(1)}) custom-call(s32[3]{0:T(128)S(1)} %add_add_fusion.which_ref, bf16[2,1024,3072]{2,1,0:T(8,128)(2,1)} %get-tuple-element.307.gd_ref, bf16[1024,768]{1,0:T(8,128)(2,1)} %get-tuple-element.308.h_ref, ...), custom_call_target="tpu_custom_call" | custom-call | flops 4831838208 | bytes 15728640 | tf_op jit(solution)/shard_map/pallas_call | solution.py:895
  138.8 1.6 collective-permute-start.14
  142.1 18.8 %shard_map.279 = (bf16[16,192,768]{2,1,0:T(8,128)(2,1)S(1)}, bf16[16,192,768]{2,1,0:T(8,128)(2,1)}, bf16[1024,768]{1,0:T(8,128)(2,1)}, bf16[1024,768]{1,0:T(8,12...) custom-call(s32[1]{0:T(128)} %bitcast.core_ref, ...), custom_call_target="tpu_custom_call" | custom-call | flops 4831838208 | bytes 23592960 | tf_op jit(solution)/shard_map/pallas_call | solution.py:964
  160.9 4.5 %collective-permute-done.14 = bf16[8,96,768]{2,1,0:T(8,128)(2,1)S(1)} collective-permute-done((bf16[8,96,768]{2,1,0:T(8,128)(2,1)}, bf16[8,96,768]{2,1,0:T(8,128)(2,1)S(1)}, u32[]{:S(2)}, u32[]{:S(2)}) %collective-permute-start.14) | collective-permute-done | bytes 1179680 | tf_op jit(solution)/shard_map/ppermute | solution.py:603
  167.7 1.9 shard_map.280
  171.2 4.3 %collective-permute-done.20 = bf16[16,192,768]{2,1,0:T(8,128)(2,1)S(1)} collective-permute-done((bf16[16,192,768]{2,1,0:T(8,128)(2,1)S(1)}, bf16[16,192,768]{2,1,0:T(8,128)(2,1)S(1)}, u32[]{:S(2)}, u32[]{:S(2)}) %collective-permute-start.20) | collective-permute-done | bytes 4718624 | tf_op jit(solution)/shard_map/ppermute | solution.py:603
  175.5 6.5 %shard_map.281 = (bf16[8,64,768]{2,1,0:T(8,128)(2,1)S(1)}, bf16[4,2,1,64,768]{4,3,2,1,0:T(8,128)(2,1)}, bf16[8,64,768]{2,1,0:T(8,128)(2,1)S(1)}, bf16[2,2,2,64,7...) custom-call(s32[3]{0:T(128)S(1)} %pad_add_fusion.1.pick_ref, ...), custom_call_target="tpu_custom_call" | custom-call | tf_op jit(solution)/shard_map/pallas_call | solution.py:710
  182.1 3.4 %collective-permute-done.17 = bf16[4,96,768]{2,1,0:T(8,128)(2,1)S(1)} collective-permute-done((bf16[4,96,768]{2,1,0:T(8,128)(2,1)S(1)}, bf16[4,96,768]{2,1,0:T(8,128)(2,1)S(1)}, u32[]{:S(2)}, u32[]{:S(2)}) %collective-permute-start.17) | collective-permute-done | bytes 589856 | tf_op jit(solution)/shard_map/ppermute | solution.py:603
  185.7 1.9 shard_map.282
  187.6 1.8 collective-permute-start.21
  189.9 1.5 collective-permute-start.23
  191.4 5.0 %collective-permute-done.21.refs_1_ = bf16[2,96,768]{2,1,0:T(8,128)(2,1)} collective-permute-done((bf16[2,96,768]{2,1,0:T(8,128)(2,1)}, bf16[2,96,768]{2,1,0:T(8,128)(2,1)}, u32[]{:S(2)}, u32[]{:S(2)}) %collective-permute-start.21) | collective-permute-done | bytes 294944 | tf_op jit(solution)/shard_map/ppermute | solution.py:603
  197.7 1.6 shard_map.283
  199.3 1.6 collective-permute-start.26
  200.9 1.5 collective-permute-start.27
  203.6 2.0 copy-done.2
  205.6 9.5 %shard_map.284 = (bf16[1024,768]{1,0:T(8,128)(2,1)}, bf16[32,768]{1,0:T(8,128)(2,1)}, f32[16,768]{1,0:T(8,128)S(1)}) custom-call(bf16[1024,768]{1,0:T(8,128)(2,1)} %bitcast.115, f32[1024,768]{1,0:T(8,128)} %get-tuple-element.405.dx1_ref, bf16[1024,768]{1,0:T(8,128)(2,1)} %get-tuple-element.406.dq3_ref, bf16[1024,768]{1,0:T(8,128)(2,1)} %get-tuple-element.407.dk1_ref, ...), custom_call_target="tpu_custom_call" | custom-call | flops 3623878656 | bytes 11010048 | tf_op jit(solution)/shard_map/pallas_call | solution.py:990
  217.0 3.6 %collective-permute-done.25 = f32[16,768]{1,0:T(8,128)S(1)} collective-permute-done((f32[16,768]{1,0:T(8,128)S(1)}, f32[16,768]{1,0:T(8,128)S(1)}, u32[]{:S(2)}, u32[]{:S(2)}) %collective-permute-start.25) | collective-permute-done | bytes 49184 | tf_op jit(solution)/shard_map/ppermute | solution.py:603
  220.6 6.2 %collective-permute-done.29.got_ref = bf16[288,768]{1,0:T(8,128)(2,1)S(1)} collective-permute-done((bf16[288,768]{1,0:T(8,128)(2,1)S(1)}, bf16[288,768]{1,0:T(8,128)(2,1)S(1)}, u32[]{:S(2)}, u32[]{:S(2)}) %collective-permute-start.29) | collective-permute-done | bytes 442400 | tf_op jit(solution)/shard_map/ppermute | solution.py:603
  226.8 1.5 collective-permute-done.28
  228.3 2.8 %shard_map.285 = (bf16[4,64,768]{2,1,0:T(8,128)(2,1)S(1)}, bf16[4,64,768]{2,1,0:T(8,128)(2,1)S(1)}, bf16[4,64,768]{2,1,0:T(8,128)(2,1)S(1)}, bf16[4,64,768]{2,1,...) custom-call(s32[3]{0:T(128)S(1)} %pad_add_fusion.pick_ref, ...), custom_call_target="tpu_custom_call" | custom-call | bytes 7077888 | tf_op jit(solution)/shard_map/pallas_call | solution.py:748
  233.2 1.5 collective-permute-start.30
  236.0 7.9 %collective-permute-done.30 = f32[16,768]{1,0:T(8,128)S(1)} collective-permute-done((f32[16,768]{1,0:T(8,128)S(1)}, f32[16,768]{1,0:T(8,128)S(1)}, u32[]{:S(2)}, u32[]{:S(2)}) %collective-permute-start.30) | collective-permute-done | bytes 49184 | tf_op jit(solution)/shard_map/ppermute | solution.py:603
  246.4 1.5 collective-permute-start.38
  248.6 3.9 %collective-permute-done.35 = f32[16,768]{1,0:T(8,128)S(1)} collective-permute-done((f32[16,768]{1,0:T(8,128)S(1)}, f32[16,768]{1,0:T(8,128)S(1)}, u32[]{:S(2)}, u32[]{:S(2)}) %collective-permute-start.35) | collective-permute-done | bytes 49184 | tf_op jit(solution)/shard_map/ppermute | solution.py:603
  252.6 2.0 collective-permute-start.40
  255.6 13.8 %collective-permute-done.39 = f32[16,768]{1,0:T(8,128)S(1)} collective-permute-done((f32[16,768]{1,0:T(8,128)S(1)}, f32[16,768]{1,0:T(8,128)S(1)}, u32[]{:S(2)}, u32[]{:S(2)}) %collective-permute-start.39) | collective-permute-done | bytes 49184 | tf_op jit(solution)/shard_map/ppermute | solution.py:603
  (160 shorter events, 34.0 us)
Async XLA Ops:
  12.2 6.8 %collective-permute-start = (bf16[32,768]{1,0:T(8,128)(2,1)S(1)}, bf16[32,768]{1,0:T(8,128)(2,1)S(1)}, u32[]{:S(2)}, u32[]{:S(2)}) collective-permute-start(bf16[32,768]{1,0:T(8,128)(2,1)S(1)} %get-tuple-element.338.a2_ref), channel_id=1, source_target_pairs={{0,16},{2,18},{4,20},{6,22},{8,24},{10,26},{12,28},{14,30},{16,0},... | collective-permute-start | bytes 147464 | tf_op jit(solution)/shard_map/ppermute | solution.py:603
  19.0 20.8 %copy-start.21 = (s32[1,64]{1,0:T(1,128)S(1)}, s32[1,64]{1,0:T(1,128)}, u32[]{:S(2)}) copy-start(s32[1,64]{1,0:T(1,128)} %image_ref.1) | copy-start | bytes 772
  19.7 4.9 %collective-permute-start.1 = (bf16[2,32,768]{2,1,0:T(8,128)(2,1)}, bf16[2,32,768]{2,1,0:T(8,128)(2,1)}, u32[]{:S(2)}, u32[]{:S(2)}) collective-permute-start(bf16[2,32,768]{2,1,0:T(8,128)(2,1)} %get-tuple-element.252), channel_id=1, source_target_pairs={{0,8},{2,10},{4,12},{6,14},{8,0},{10,2},{12,4},{14,6},{16,24},{18,... | collective-permute-start | bytes 294920 | tf_op jit(solution)/shard_map/ppermute | solution.py:603
  21.3 18.5 %copy-start.18 = (f32[32,768]{1,0:T(8,128)S(1)}, f32[32,768]{1,0:T(8,128)}, u32[]{:S(2)}) copy-start(f32[32,768]{1,0:T(8,128)} %copy-done.17) | copy-start | bytes 294916
  25.5 4.7 %collective-permute-start.2 = (bf16[2,2,16,768]{3,2,0,1:T(8,128)(2,1)S(1)}, bf16[2,2,16,768]{3,2,0,1:T(8,128)(2,1)S(1)}, u32[]{:S(2)}, u32[]{:S(2)}) collective-permute-start(bf16[2,2,16,768]{3,2,0,1:T(8,128)(2,1)S(1)} %get-tuple-element.253), channel_id=1, source_target_pairs={{0,4},{2,6},{4,0},{6,2},{8,12},{10,14},{12,8},{14,10},{16,20},{18,... | collective-permute-start | bytes 294920 | tf_op jit(solution)/shard_map/ppermute | solution.py:603
  27.2 5.3 %collective-permute-start.3 = (bf16[2,2,16,768]{3,2,0,1:T(8,128)(2,1)S(1)}, bf16[2,2,16,768]{3,2,0,1:T(8,128)(2,1)S(1)}, u32[]{:S(2)}, u32[]{:S(2)}) collective-permute-start(bf16[2,2,16,768]{3,2,0,1:T(8,128)(2,1)S(1)} %get-tuple-element.254), channel_id=1, source_target_pairs={{0,2},{2,0},{4,6},{6,4},{8,10},{10,8},{12,14},{14,12},{16,18},{18,... | collective-permute-start | bytes 294920 | tf_op jit(solution)/shard_map/ppermute | solution.py:603
  32.5 5.7 %collective-permute-start.4 = (bf16[2,2,2,16,768]{4,3,0,1,2:T(8,128)(2,1)S(1)}, bf16[2,2,2,16,768]{4,3,0,1,2:T(8,128)(2,1)S(1)}, u32[]{:S(2)}, u32[]{:S(2)}) collective-permute-start(bf16[2,2,2,16,768]{4,3,0,1,2:T(8,128)(2,1)S(1)} %pad_maximum_fusion.2), channel_id=1, source_target_pairs={{0,2},{2,0},{4,6},{6,4},{8,10},{10,8},{12,14},{14,12},{16,18},{18,... | collective-permute-start | bytes 589832 | tf_op jit(solution)/shard_map/ppermute | solution.py:603
  34.0 5.7 %collective-permute-start.5 = (bf16[2,2,2,16,768]{4,3,0,1,2:T(8,128)(2,1)S(1)}, bf16[2,2,2,16,768]{4,3,0,1,2:T(8,128)(2,1)S(1)}, u32[]{:S(2)}, u32[]{:S(2)}) collective-permute-start(bf16[2,2,2,16,768]{4,3,0,1,2:T(8,128)(2,1)S(1)} %pad_maximum_fusion.3), channel_id=1, source_target_pairs={{0,4},{2,6},{4,0},{6,2},{8,12},{10,14},{12,8},{14,10},{16,20},{18,... | collective-permute-start | bytes 589832 | tf_op jit(solution)/shard_map/ppermute | solution.py:603
  46.8 45.3 %copy-start.7 = (bf16[512,768]{1,0:T(8,128)(2,1)}, bf16[512,768]{1,0:T(8,128)(2,1)S(1)}, u32[]{:S(2)}) copy-start(bf16[512,768]{1,0:T(8,128)(2,1)S(1)} %get-tuple-element.323.k2_ref) | copy-start | bytes 2359300
  46.8 45.3 %copy-start.9 = (bf16[512,768]{1,0:T(8,128)(2,1)}, bf16[512,768]{1,0:T(8,128)(2,1)S(1)}, u32[]{:S(2)}) copy-start(bf16[512,768]{1,0:T(8,128)(2,1)S(1)} %get-tuple-element.324.v2_ref) | copy-start | bytes 2359300
  46.8 45.3 %copy-start.19 = (bf16[1,32,768]{2,1,0:T(8,128)(2,1)S(1)}, bf16[1,32,768]{2,1,0:T(8,128)(2,1)}, u32[]{:S(2)}) copy-start(bf16[1,32,768]{2,1,0:T(8,128)(2,1)} %param.31) | copy-start | bytes 147460
  95.3 13.0 %collective-permute-start.7 = (bf16[16,96,768]{2,1,0:T(8,128)(2,1)S(1)}, bf16[16,96,768]{2,1,0:T(8,128)(2,1)S(1)}, u32[]{:S(2)}, u32[]{:S(2)}) collective-permute-start(bf16[16,96,768]{2,1,0:T(8,128)(2,1)S(1)} %get-tuple-element.281), channel_id=1, source_target_pairs={{0,1},{1,0},{2,3},{3,2},{4,5},{5,4},{6,7},{7,6},{8,9},{9,8},{10,11... | collective-permute-start | bytes 7077896 | tf_op jit(solution)/shard_map/ppermute | solution.py:603
  95.3 13.0 %collective-permute-start.6 = (bf16[32,896]{1,0:T(8,128)(2,1)S(1)}, bf16[32,896]{1,0:T(8,128)(2,1)S(1)}, u32[]{:S(2)}, u32[]{:S(2)}) collective-permute-start(bf16[32,896]{1,0:T(8,128)(2,1)S(1)} %get-tuple-element.273), channel_id=1, source_target_pairs={{0,16},{2,18},{4,20},{6,22},{8,24},{10,26},{12,28},{14,30},{16,0},... | collective-permute-start | bytes 172040 | tf_op jit(solution)/shard_map/ppermute | solution.py:603
  108.3 18.9 %collective-permute-start.13 = (bf16[16,192,768]{2,1,0:T(8,128)(2,1)}, bf16[16,192,768]{2,1,0:T(8,128)(2,1)}, u32[]{:S(2)}, u32[]{:S(2)}) collective-permute-start(bf16[16,192,768]{2,1,0:T(8,128)(2,1)} %shard_map.276), channel_id=1, source_target_pairs={{0,1},{1,0},{2,3},{3,2},{4,5},{5,4},{6,7},{7,6},{8,9},{9,8},{10,11... | collective-permute-start | bytes 14155784 | tf_op jit(solution)/shard_map/ppermute | solution.py:603
  109.8 7.2 %collective-permute-start.8 = (bf16[2,32,896]{2,1,0:T(8,128)(2,1)}, bf16[2,32,896]{2,1,0:T(8,128)(2,1)}, u32[]{:S(2)}, u32[]{:S(2)}) collective-permute-start(bf16[2,32,896]{2,1,0:T(8,128)(2,1)} %get-tuple-element.282), channel_id=1, source_target_pairs={{0,8},{2,10},{4,12},{6,14},{8,0},{10,2},{12,4},{14,6},{16,24},{18,... | collective-permute-start | bytes 344072 | tf_op jit(solution)/shard_map/ppermute | solution.py:603
  118.5 5.3 %collective-permute-start.9 = (bf16[2,2,16,896]{3,2,0,1:T(8,128)(2,1)}, bf16[2,2,16,896]{3,2,0,1:T(8,128)(2,1)}, u32[]{:S(2)}, u32[]{:S(2)}) collective-permute-start(bf16[2,2,16,896]{3,2,0,1:T(8,128)(2,1)} %get-tuple-element.289), channel_id=1, source_target_pairs={{0,4},{2,6},{4,0},{6,2},{8,12},{10,14},{12,8},{14,10},{16,20},{18,... | collective-permute-start | bytes 344072 | tf_op jit(solution)/shard_map/ppermute | solution.py:603
  119.1 5.7 %collective-permute-start.10 = (bf16[2,2,16,896]{3,2,0,1:T(8,128)(2,1)}, bf16[2,2,16,896]{3,2,0,1:T(8,128)(2,1)S(1)}, u32[]{:S(2)}, u32[]{:S(2)}) collective-permute-start(bf16[2,2,16,896]{3,2,0,1:T(8,128)(2,1)} %get-tuple-element.290), channel_id=1, source_target_pairs={{0,2},{2,0},{4,6},{6,4},{8,10},{10,8},{12,14},{14,12},{16,18},{18,... | collective-permute-start | bytes 344072 | tf_op jit(solution)/shard_map/ppermute | solution.py:603
  124.8 14.0 %collective-permute-start.11 = (bf16[2,2,2,16,896]{4,3,0,1,2:T(8,128)(2,1)S(1)}, bf16[2,2,2,16,896]{4,3,0,1,2:T(8,128)(2,1)S(1)}, u32[]{:S(2)}, u32[]{:S(2)}) collective-permute-start(bf16[2,2,2,16,896]{4,3,0,1,2:T(8,128)(2,1)S(1)} %pad_maximum_fusion), channel_id=1, source_target_pairs={{0,2},{2,0},{4,6},{6,4},{8,10},{10,8},{12,14},{14,12},{16,18},{18,... | collective-permute-start | bytes 688136 | tf_op jit(solution)/shard_map/ppermute | solution.py:603
  126.4 12.5 %collective-permute-start.12 = (bf16[2,2,2,16,896]{4,3,0,1,2:T(8,128)(2,1)S(1)}, bf16[2,2,2,16,896]{4,3,0,1,2:T(8,128)(2,1)S(1)}, u32[]{:S(2)}, u32[]{:S(2)}) collective-permute-start(bf16[2,2,2,16,896]{4,3,0,1,2:T(8,128)(2,1)S(1)} %pad_maximum_fusion.1), channel_id=1, source_target_pairs={{0,4},{2,6},{4,0},{6,2},{8,12},{10,14},{12,8},{14,10},{16,20},{18,... | collective-permute-start | bytes 688136 | tf_op jit(solution)/shard_map/ppermute | solution.py:603
  138.8 26.6 %collective-permute-start.14 = (bf16[8,96,768]{2,1,0:T(8,128)(2,1)}, bf16[8,96,768]{2,1,0:T(8,128)(2,1)S(1)}, u32[]{:S(2)}, u32[]{:S(2)}) collective-permute-start(bf16[8,96,768]{2,1,0:T(8,128)(2,1)} %get-tuple-element.351), channel_id=1, source_target_pairs={{0,2},{2,0},{4,6},{6,4},{8,10},{10,8},{12,14},{14,12},{16,18},{18,... | collective-permute-start | bytes 3538952 | tf_op jit(solution)/shard_map/ppermute | solution.py:603
  140.4 26.0 %collective-permute-start.15 = (bf16[8,96,768]{2,1,0:T(8,128)(2,1)S(1)}, bf16[8,96,768]{2,1,0:T(8,128)(2,1)S(1)}, u32[]{:S(2)}, u32[]{:S(2)}) collective-permute-start(bf16[8,96,768]{2,1,0:T(8,128)(2,1)S(1)} %get-tuple-element.352), channel_id=1, source_target_pairs={{0,4},{2,6},{4,0},{6,2},{8,12},{10,14},{12,8},{14,10},{16,20},{18,... | collective-permute-start | bytes 3538952 | tf_op jit(solution)/shard_map/ppermute | solution.py:603
  141.7 25.9 %collective-permute-start.16 = (bf16[8,96,768]{2,1,0:T(8,128)(2,1)S(1)}, bf16[8,96,768]{2,1,0:T(8,128)(2,1)S(1)}, u32[]{:S(2)}, u32[]{:S(2)}) collective-permute-start(bf16[8,96,768]{2,1,0:T(8,128)(2,1)S(1)} %copy-done.25), channel_id=1, source_target_pairs={{0,8},{2,10},{4,12},{6,14},{8,0},{10,2},{12,4},{14,6},{16,24},{18,... | collective-permute-start | bytes 3538952 | tf_op jit(solution)/shard_map/ppermute | solution.py:603
  142.1 25.6 %copy-start.6 = (bf16[8,96,768]{2,1,0:T(8,128)(2,1)S(1)}, bf16[8,96,768]{2,1,0:T(8,128)(2,1)}, u32[]{:S(2)}) copy-start(bf16[8,96,768]{2,1,0:T(8,128)(2,1)} %copy-done.5) | copy-start | bytes 3538948
  167.6 7.9 %collective-permute-start.20 = (bf16[16,192,768]{2,1,0:T(8,128)(2,1)S(1)}, bf16[16,192,768]{2,1,0:T(8,128)(2,1)S(1)}, u32[]{:S(2)}, u32[]{:S(2)}) collective-permute-start(bf16[16,192,768]{2,1,0:T(8,128)(2,1)S(1)} %get-tuple-element.369), channel_id=1, source_target_pairs={{0,1},{1,0},{2,3},{3,2},{4,5},{5,4},{6,7},{7,6},{8,9},{9,8},{10,11... | collective-permute-start | bytes 14155784 | tf_op jit(solution)/shard_map/ppermute | solution.py:603
  169.6 15.8 %collective-permute-start.17 = (bf16[4,96,768]{2,1,0:T(8,128)(2,1)S(1)}, bf16[4,96,768]{2,1,0:T(8,128)(2,1)S(1)}, u32[]{:S(2)}, u32[]{:S(2)}) collective-permute-start(bf16[4,96,768]{2,1,0:T(8,128)(2,1)S(1)} %get-tuple-element.363), channel_id=1, source_target_pairs={{0,4},{2,6},{4,0},{6,2},{8,12},{10,14},{12,8},{14,10},{16,20},{18,... | collective-permute-start | bytes 1769480 | tf_op jit(solution)/shard_map/ppermute | solution.py:603
  170.2 15.5 %collective-permute-start.18 = (bf16[4,96,768]{2,1,0:T(8,128)(2,1)S(1)}, bf16[4,96,768]{2,1,0:T(8,128)(2,1)S(1)}, u32[]{:S(2)}, u32[]{:S(2)}) collective-permute-start(bf16[4,96,768]{2,1,0:T(8,128)(2,1)S(1)} %get-tuple-element.365), channel_id=1, source_target_pairs={{0,8},{2,10},{4,12},{6,14},{8,0},{10,2},{12,4},{14,6},{16,24},{18,... | collective-permute-start | bytes 1769480 | tf_op jit(solution)/shard_map/ppermute | solution.py:603
  170.5 15.2 %collective-permute-start.19 = (bf16[4,96,768]{2,1,0:T(8,128)(2,1)S(1)}, bf16[4,96,768]{2,1,0:T(8,128)(2,1)S(1)}, u32[]{:S(2)}, u32[]{:S(2)}) collective-permute-start(bf16[4,96,768]{2,1,0:T(8,128)(2,1)S(1)} %get-tuple-element.367), channel_id=1, source_target_pairs={{0,2},{2,0},{4,6},{6,4},{8,10},{10,8},{12,14},{14,12},{16,18},{18,... | collective-permute-start | bytes 1769480 | tf_op jit(solution)/shard_map/ppermute | solution.py:603
  187.6 8.7 %collective-permute-start.21 = (bf16[2,96,768]{2,1,0:T(8,128)(2,1)}, bf16[2,96,768]{2,1,0:T(8,128)(2,1)}, u32[]{:S(2)}, u32[]{:S(2)}) collective-permute-start(bf16[2,96,768]{2,1,0:T(8,128)(2,1)} %get-tuple-element.391), channel_id=1, source_target_pairs={{0,8},{2,10},{4,12},{6,14},{8,0},{10,2},{12,4},{14,6},{16,24},{18,... | collective-permute-start | bytes 884744 | tf_op jit(solution)/shard_map/ppermute | solution.py:603
  189.4 8.0 %collective-permute-start.22 = (bf16[2,96,768]{2,1,0:T(8,128)(2,1)}, bf16[2,96,768]{2,1,0:T(8,128)(2,1)}, u32[]{:S(2)}, u32[]{:S(2)}) collective-permute-start(bf16[2,96,768]{2,1,0:T(8,128)(2,1)} %get-tuple-element.393), channel_id=1, source_target_pairs={{0,2},{2,0},{4,6},{6,4},{8,10},{10,8},{12,14},{14,12},{16,18},{18,... | collective-permute-start | bytes 884744 | tf_op jit(solution)/shard_map/ppermute | solution.py:603
  189.9 7.8 %collective-permute-start.23 = (bf16[2,96,768]{2,1,0:T(8,128)(2,1)}, bf16[2,96,768]{2,1,0:T(8,128)(2,1)}, u32[]{:S(2)}, u32[]{:S(2)}) collective-permute-start(bf16[2,96,768]{2,1,0:T(8,128)(2,1)} %get-tuple-element.395), channel_id=1, source_target_pairs={{0,4},{2,6},{4,0},{6,2},{8,12},{10,14},{12,8},{14,10},{16,20},{18,... | collective-permute-start | bytes 884744 | tf_op jit(solution)/shard_map/ppermute | solution.py:603
  199.3 27.5 %collective-permute-start.26 = (bf16[8,64,768]{2,1,0:T(8,128)(2,1)}, bf16[8,64,768]{2,1,0:T(8,128)(2,1)S(1)}, u32[]{:S(2)}, u32[]{:S(2)}) collective-permute-start(bf16[8,64,768]{2,1,0:T(8,128)(2,1)} %copy-done.30), channel_id=1, source_target_pairs={{0,2},{2,0},{4,6},{6,4},{8,10},{10,8},{12,14},{14,12},{16,18},{18,... | collective-permute-start | bytes 2359304 | tf_op jit(solution)/shard_map/ppermute | solution.py:603
  200.9 25.9 %collective-permute-start.27 = (bf16[8,64,768]{2,1,0:T(8,128)(2,1)S(1)}, bf16[8,64,768]{2,1,0:T(8,128)(2,1)S(1)}, u32[]{:S(2)}, u32[]{:S(2)}) collective-permute-start(bf16[8,64,768]{2,1,0:T(8,128)(2,1)S(1)} %copy-done.29), channel_id=1, source_target_pairs={{0,4},{2,6},{4,0},{6,2},{8,12},{10,14},{12,8},{14,10},{16,20},{18,... | collective-permute-start | bytes 2359304 | tf_op jit(solution)/shard_map/ppermute | solution.py:603
  202.3 26.0 %collective-permute-start.28 = (bf16[8,64,768]{2,1,0:T(8,128)(2,1)S(1)}, bf16[8,64,768]{2,1,0:T(8,128)(2,1)S(1)}, u32[]{:S(2)}, u32[]{:S(2)}) collective-permute-start(bf16[8,64,768]{2,1,0:T(8,128)(2,1)S(1)} %copy-done.27), channel_id=1, source_target_pairs={{0,8},{2,10},{4,12},{6,14},{8,0},{10,2},{12,4},{14,6},{16,24},{18,... | collective-permute-start | bytes 2359304 | tf_op jit(solution)/shard_map/ppermute | solution.py:603
  203.0 23.8 %collective-permute-start.29 = (bf16[288,768]{1,0:T(8,128)(2,1)S(1)}, bf16[288,768]{1,0:T(8,128)(2,1)S(1)}, u32[]{:S(2)}, u32[]{:S(2)}) collective-permute-start(bf16[288,768]{1,0:T(8,128)(2,1)S(1)} %get-tuple-element.429), channel_id=1, source_target_pairs={{0,16},{2,18},{4,20},{6,22},{8,24},{10,26},{12,28},{14,30},{16,0},... | collective-permute-start | bytes 1327112 | tf_op jit(solution)/shard_map/ppermute | solution.py:603
  215.1 1.3 collective-permute-start.24
  216.4 4.2 %collective-permute-start.25 = (f32[16,768]{1,0:T(8,128)S(1)}, f32[16,768]{1,0:T(8,128)S(1)}, u32[]{:S(2)}, u32[]{:S(2)}) collective-permute-start(f32[16,768]{1,0:T(8,128)S(1)} %add.30), channel_id=1, source_target_pairs={{0,2},{2,0},{4,6},{6,4},{8,10},{10,8},{12,14},{14,12},{16,18},{18,... | collective-permute-start | bytes 147464 | tf_op jit(solution)/shard_map/ppermute | solution.py:603
  231.3 3.4 %collective-permute-start.34 = (bf16[288,768]{1,0:T(8,128)(2,1)S(1)}, bf16[288,768]{1,0:T(8,128)(2,1)S(1)}, u32[]{:S(2)}, u32[]{:S(2)}) collective-permute-start(bf16[288,768]{1,0:T(8,128)(2,1)S(1)} %shard_map.286.mine_ref), channel_id=1, source_target_pairs={{0,1},{1,0},{2,3},{3,2},{4,5},{5,4},{6,7},{7,6},{8,9},{9,8},{10,11... | collective-permute-start | bytes 1327112 | tf_op jit(solution)/shard_map/ppermute | solution.py:603
  231.4 12.6 %collective-permute-start.31 = (bf16[4,64,768]{2,1,0:T(8,128)(2,1)S(1)}, bf16[4,64,768]{2,1,0:T(8,128)(2,1)S(1)}, u32[]{:S(2)}, u32[]{:S(2)}) collective-permute-start(bf16[4,64,768]{2,1,0:T(8,128)(2,1)S(1)} %get-tuple-element.438), channel_id=1, source_target_pairs={{0,4},{2,6},{4,0},{6,2},{8,12},{10,14},{12,8},{14,10},{16,20},{18,... | collective-permute-start | bytes 1179656 | tf_op jit(solution)/shard_map/ppermute | solution.py:603
  232.0 12.0 %collective-permute-start.32 = (bf16[4,64,768]{2,1,0:T(8,128)(2,1)S(1)}, bf16[4,64,768]{2,1,0:T(8,128)(2,1)S(1)}, u32[]{:S(2)}, u32[]{:S(2)}) collective-permute-start(bf16[4,64,768]{2,1,0:T(8,128)(2,1)S(1)} %get-tuple-element.439), channel_id=1, source_target_pairs={{0,8},{2,10},{4,12},{6,14},{8,0},{10,2},{12,4},{14,6},{16,24},{18,... | collective-permute-start | bytes 1179656 | tf_op jit(solution)/shard_map/ppermute | solution.py:603
  232.7 11.3 %collective-permute-start.33 = (bf16[4,64,768]{2,1,0:T(8,128)(2,1)S(1)}, bf16[4,64,768]{2,1,0:T(8,128)(2,1)S(1)}, u32[]{:S(2)}, u32[]{:S(2)}) collective-permute-start(bf16[4,64,768]{2,1,0:T(8,128)(2,1)S(1)} %get-tuple-element.440), channel_id=1, source_target_pairs={{0,2},{2,0},{4,6},{6,4},{8,10},{10,8},{12,14},{14,12},{16,18},{18,... | collective-permute-start | bytes 1179656 | tf_op jit(solution)/shard_map/ppermute | solution.py:603
  233.2 10.7 %collective-permute-start.30 = (f32[16,768]{1,0:T(8,128)S(1)}, f32[16,768]{1,0:T(8,128)S(1)}, u32[]{:S(2)}, u32[]{:S(2)}) collective-permute-start(f32[16,768]{1,0:T(8,128)S(1)} %add.31), channel_id=1, source_target_pairs={{0,4},{2,6},{4,0},{6,2},{8,12},{10,14},{12,8},{14,10},{16,20},{18,... | collective-permute-start | bytes 147464 | tf_op jit(solution)/shard_map/ppermute | solution.py:603
  244.8 7.6 %collective-permute-start.36 = (bf16[2,64,768]{2,1,0:T(8,128)(2,1)S(1)}, bf16[2,64,768]{2,1,0:T(8,128)(2,1)S(1)}, u32[]{:S(2)}, u32[]{:S(2)}) collective-permute-start(bf16[2,64,768]{2,1,0:T(8,128)(2,1)S(1)} %get-tuple-element.458), channel_id=1, source_target_pairs={{0,8},{2,10},{4,12},{6,14},{8,0},{10,2},{12,4},{14,6},{16,24},{18,... | collective-permute-start | bytes 589832 | tf_op jit(solution)/shard_map/ppermute | solution.py:603
  245.8 6.6 %collective-permute-start.37 = (bf16[2,64,768]{2,1,0:T(8,128)(2,1)S(1)}, bf16[2,64,768]{2,1,0:T(8,128)(2,1)S(1)}, u32[]{:S(2)}, u32[]{:S(2)}) collective-permute-start(bf16[2,64,768]{2,1,0:T(8,128)(2,1)S(1)} %get-tuple-element.459), channel_id=1, source_target_pairs={{0,2},{2,0},{4,6},{6,4},{8,10},{10,8},{12,14},{14,12},{16,18},{18,... | collective-permute-start | bytes 589832 | tf_op jit(solution)/shard_map/ppermute | solution.py:603
  246.4 6.0 %collective-permute-start.38 = (bf16[2,64,768]{2,1,0:T(8,128)(2,1)S(1)}, bf16[2,64,768]{2,1,0:T(8,128)(2,1)S(1)}, u32[]{:S(2)}, u32[]{:S(2)}) collective-permute-start(bf16[2,64,768]{2,1,0:T(8,128)(2,1)S(1)} %get-tuple-element.460), channel_id=1, source_target_pairs={{0,4},{2,6},{4,0},{6,2},{8,12},{10,14},{12,8},{14,10},{16,20},{18,... | collective-permute-start | bytes 589832 | tf_op jit(solution)/shard_map/ppermute | solution.py:603
  247.9 4.5 %collective-permute-start.35 = (f32[16,768]{1,0:T(8,128)S(1)}, f32[16,768]{1,0:T(8,128)S(1)}, u32[]{:S(2)}, u32[]{:S(2)}) collective-permute-start(f32[16,768]{1,0:T(8,128)S(1)} %add.32), channel_id=1, source_target_pairs={{0,8},{2,10},{4,12},{6,14},{8,0},{10,2},{12,4},{14,6},{16,24},{18,... | collective-permute-start | bytes 147464 | tf_op jit(solution)/shard_map/ppermute | solution.py:603
  252.6 16.9 %collective-permute-start.40 = (bf16[192,768]{1,0:T(8,128)(2,1)S(1)}, bf16[192,768]{1,0:T(8,128)(2,1)S(1)}, u32[]{:S(2)}, u32[]{:S(2)}) collective-permute-start(bf16[192,768]{1,0:T(8,128)(2,1)S(1)} %get-tuple-element.473), channel_id=1, source_target_pairs={{0,16},{2,18},{4,20},{6,22},{8,24},{10,26},{12,28},{14,30},{16,0},... | collective-permute-start | bytes 884744 | tf_op jit(solution)/shard_map/ppermute | solution.py:603
  254.6 14.9 %collective-permute-start.39 = (f32[16,768]{1,0:T(8,128)S(1)}, f32[16,768]{1,0:T(8,128)S(1)}, u32[]{:S(2)}, u32[]{:S(2)}) collective-permute-start(f32[16,768]{1,0:T(8,128)S(1)} %add.33), channel_id=1, source_target_pairs={{0,16},{2,18},{4,20},{6,22},{8,24},{10,26},{12,28},{14,30},{16,0},... | collective-permute-start | bytes 147464 | tf_op jit(solution)/shard_map/ppermute | solution.py:603
  269.5 1.6 collective-permute-start.41
  (30 other events, 272.2 us)
